TPU v7x, 32 devices: a whole 2x2x4 slice. The times are simulated.
32 devices in a mesh: expert: 8 (over z, x), col: 4 (over y, core).
Axes of the slice: x: 2, y: 2, z: 4, core: 2. Of those that a mesh axis runs over, the one named last changes fastest.
Arguments:
- tokens: bfloat16 [1024, 4096], P('expert', 'col'), may hold values from -6 to 6
- routes: int32 [1024, 8], P('expert'), may hold values from 0 to 15, all different within a row; in each aligned block of 128 rows (0 to 127, 128 to 255, ...) at most 96 rows name the same one
- route_weight: float32 [1024, 8], P('expert'), may hold values from 0.02 to 0.25
- language: int32 [1024], P('expert'), may hold values from 0 to 118
- lang_weight: float32 [119], replicated, may hold values from 0.01 to 0.1
- w_gate: bfloat16 [16, 1536, 4096], P('expert', 'col'), may hold values from -0.09375 to 0.09375
- w_up: bfloat16 [16, 1536, 4096], P('expert', 'col'), may hold values from -0.09375 to 0.09375
- w_down: bfloat16 [16, 1536, 4096], P('expert', None, 'col'), may hold values from -0.15625 to 0.15625
Outputs:
- layer_out: bfloat16 [1024, 4096], P('expert', 'col')
- gram: float32 [16, 1536, 1536], P('expert', 'col')
Inputs may be any that keep to these rules, and one draw needn't show every extreme that they name: `routes`: each row names 8 different experts. In each aligned block of 128 rows no expert is named by more than 96 rows, a bound that some block reaches.
All inputs are finite; a program needn't handle non-finite values.
Results may differ from a plain program's by a relative error of at most 0.0063.
Values may be sent and summed in bfloat16 or wider, within the bound.
No kernel may reach another device: no remote copies, remote signals or barrier semaphores. Data moves between devices by JAX's collectives and lax.ppermute only.
A program may use at most 128 MiB of HBM per device.

v0:
```python
import jax
import jax.numpy as jnp
from jax import lax
from jax.sharding import PartitionSpec as P


def on_device(tokens, routes, route_weight, language, lang_weight, w_gate, w_up, w_down):
    tok_rows = routes.shape[0]
    top_count = routes.shape[1]
    local_exp = w_gate.shape[0]
    owners = lax.axis_size("expert")
    experts = local_exp * owners
    capacity = tok_rows * top_count * 3 // (2 * experts)
    expert_ids = jnp.arange(experts, dtype=jnp.int32)
    chosen = routes[:, :, None] == expert_ids[None, None, :]
    hits = jnp.any(chosen, axis=1).astype(jnp.int32)
    coefs = jnp.sum(jnp.where(chosen, route_weight[:, :, None], jnp.zeros((), jnp.float32)), axis=1)
    places = jnp.cumsum(hits, axis=0) - hits
    slot_ids = jnp.arange(capacity, dtype=jnp.int32)
    picks = (hits.T[:, None, :] == 1) & (places.T[:, None, :] == slot_ids[None, :, None])
    row_index = jnp.arange(tok_rows, dtype=jnp.int32)
    slot_token = jnp.sum(jnp.where(picks, row_index[None, None, :], 0), axis=2)
    filled = jnp.any(picks, axis=2)
    lang_table = language[:, None] == jnp.arange(lang_weight.shape[0], dtype=jnp.int32)[None, :]
    calib = jnp.sum(
        jnp.where(lang_table, lang_weight[None, :], jnp.zeros((), jnp.float32)), axis=1
    ).astype(jnp.bfloat16)
    slot_cal = jnp.where(filled, calib[slot_token], jnp.zeros((), jnp.bfloat16)).reshape(
        owners, local_exp, capacity
    )
    slot_coef = jnp.where(
        filled, jnp.take_along_axis(coefs.T, slot_token, axis=1), jnp.zeros((), jnp.float32)
    )
    flat_token = slot_token.reshape(-1)
    flat_filled = filled.reshape(-1)
    whole = lax.all_gather(tokens, "col", axis=1, tiled=True)
    rows = jnp.take(whole, flat_token, axis=0)
    rows = jnp.where(flat_filled[:, None], rows, jnp.zeros((), jnp.bfloat16))
    arrived = lax.all_to_all(
        rows.reshape(owners, local_exp, capacity, whole.shape[1]),
        "expert",
        split_axis=0,
        concat_axis=0,
        tiled=True,
    )
    arrived_cal = lax.all_to_all(slot_cal, "expert", split_axis=0, concat_axis=0, tiled=True)
    gate = jnp.einsum("seck,efk->escf", arrived, w_gate, preferred_element_type=jnp.float32)
    upper = jnp.einsum("seck,efk->escf", arrived, w_up, preferred_element_type=jnp.float32)
    hidden = (jax.nn.silu(gate) * upper).astype(jnp.bfloat16)
    cal_rows = jnp.transpose(arrived_cal, (1, 0, 2))
    scaled = (cal_rows[..., None].astype(jnp.float32) * hidden.astype(jnp.float32)).astype(
        jnp.bfloat16
    )
    d_local = w_down.shape[2]
    piece = lax.all_gather(hidden, "col", axis=3, tiled=True)
    block = jnp.einsum("escu,escv->euv", scaled, piece, preferred_element_type=jnp.float32)
    mixed_now = jnp.einsum("escv,evd->escd", piece, w_down, preferred_element_type=jnp.float32)
    expert_out = mixed_now.astype(jnp.bfloat16)
    returned = lax.all_to_all(expert_out, "expert", split_axis=1, concat_axis=0, tiled=True)
    returned = returned.reshape(experts * capacity, d_local).astype(jnp.float32)
    combined = jnp.zeros((tok_rows, d_local), jnp.float32)
    combined = combined.at[flat_token].add(slot_coef.reshape(-1)[:, None] * returned)
    return (combined.astype(jnp.bfloat16), block)


def solution(mesh):
    in_specs = (
        P("expert", "col"),
        P("expert", None),
        P("expert", None),
        P("expert"),
        P(),
        P("expert", "col", None),
        P("expert", "col", None),
        P("expert", None, "col"),
    )
    out_specs = (P("expert", "col"), P("expert", "col", None))
    return jax.shard_map(
        on_device, mesh=mesh, in_specs=in_specs, out_specs=out_specs, check_vma=False
    )
```

profile of v0, /device:TPU:0, one launch (start us, length us, event | category | flops | bytes accessed | tf_op | source)
XLA Modules:
  0.0 506.7 jit_solution(17625851431964979853)
XLA Ops:
  7.2 0.7 all-gather.3.cloned.1.call-update
  7.9 0.7 fusion.20
  9.1 0.4 select_reduce_fusion
  9.6 0.4 fusion.17
  10.0 19.0 %all-gather.3.cloned.1.call-done = bf16[128,4096]{1,0:T(8,128)(2,1)} async-done(((bf16[128,1024]{1,0:T(8,128)(2,1)}), bf16[128,4096]{1,0:T(8,128)(2,1)}) %all-gather.3.cloned.1.call-update) | async-done | bytes 1048592 | tf_op jit(solution)/shard_map/all_gather | solution.py:36
  29.0 23.4 %gather_fusion = bf16[1536,4096]{1,0:T(8,128)(2,1)} fusion(bf16[128,4096]{1,0:T(8,128)(2,1)} %all-gather.3.cloned.1.call-done, s32[2048]{0:T(1024)S(1)} %pad_clamp_fusion.1), kind=kCustom, calls=%fused_computation | custom fusion | bytes 25171968 | tf_op jit(solution)/shard_map/jit(_take)/gather | solution.py:37
  52.4 6.8 %select_select_fusion = bf16[8,2,96,4096]{3,2,1,0:T(8,128)(2,1)S(1)} fusion(bf16[8,2,96,4096]{3,2,1,0:T(8,128)(2,1)} %bitcast.49, pred[8,2,96]{2,1,0:T(4,128)(4,1)S(1)} %compare_and_fusion, pred[8,2,96]{2,1,0:T(4,128)(4,1)S(1)} %broadcast_in_dim.95), kind=kLoop, calls=%fused_computation.4 | loop fusion | flops 12582912 | bytes 25168896 | tf_op jit(solution)/shard_map/jit(_where)/select_n | solution.py:38
  59.2 278.6 %all_to_all.19 = bf16[8,2,96,4096]{3,2,1,0:T(8,128)(2,1)S(1)} all-to-all(bf16[8,2,96,4096]{3,2,1,0:T(8,128)(2,1)S(1)} %select_select_fusion), channel_id=1, replica_groups=mesh['expert'=8,'col'=4] {'expert'}, dimensions={0} | all-to-all | bytes 25165824 | tf_op jit(solution)/shard_map/all_to_all | solution.py:39
  337.8 9.8 %fusion.2 = f32[2,8,96,384]{3,2,1,0:T(8,128)} fusion(bf16[8,2,96,4096]{3,2,1,0:T(8,128)(2,1)S(1)} %all_to_all.19, bf16[2,384,4096]{2,1,0:T(8,128)(2,1)} %param.13), kind=kOutput, calls=%fused_computation.7 | convolution fusion | flops 4831838208 | bytes 21233664 | tf_op jit(solution)/shard_map/seck,efk->escf/dot_general | solution.py:47
  347.6 10.0 %multiply_convert_fusion.1 = bf16[2,8,96,384]{3,2,1,0:T(8,128)(2,1)} fusion(f32[2,8,96,384]{3,2,1,0:T(8,128)} %fusion.2, bf16[2,384,4096]{2,1,0:T(8,128)(2,1)} %param.14, bf16[8,2,96,4096]{3,2,1,0:T(8,128)(2,1)S(1)} %all_to_all.19), kind=kOutput, calls=%fused_computation.17 | convolution fusion | flops 4835377152 | bytes 22413312 | tf_op jit(solution)/shard_map/seck,efk->escf/dot_general | solution.py:48
  357.9 9.0 %gather_fusion.1 = bf16[1536]{0:T(1024)(128)(2,1)S(1)} fusion(bf16[128]{0:T(256)(128)(2,1)S(1)} %select_reduce_fusion.2, s32[2048]{0:T(1024)S(1)} %pad_clamp_fusion), kind=kCustom, calls=%fused_computation.1 | custom fusion | bytes 12288 | tf_op jit(solution)/shard_map/gather | solution.py:28
  367.0 0.6 broadcast_select_fusion
  367.6 3.6 all-to-all-start.2
  371.2 22.1 %all-gather.5.cloned.1.call-done = bf16[2,8,96,1536]{3,2,1,0:T(8,128)(2,1)} async-done(((bf16[2,8,96,384]{3,2,1,0:T(8,128)(2,1)}), bf16[2,8,96,1536]{3,2,1,0:T(8,128)(2,1)}) %all-gather.5.cloned.1.call-update) | async-done | bytes 4718608 | tf_op jit(solution)/shard_map/all_gather | solution.py:55
  393.3 8.6 %fusion.8 = bf16[2,8,96,1024]{3,2,1,0:T(8,128)(2,1)S(1)} fusion(bf16[2,8,96,1536]{3,2,1,0:T(8,128)(2,1)} %all-gather.5.cloned.1.call-done, bf16[2,1536,1024]{2,1,0:T(8,128)(2,1)} %param.15), kind=kOutput, calls=%fused_computation.18 | convolution fusion | flops 4833411072 | bytes 14155776 | tf_op jit(solution)/shard_map/escv,evd->escd/dot_general | solution.py:57
  401.9 2.0 copy.37
  403.9 5.5 %all-to-all-start.1 = ((bf16[2,8,96,1024]{3,2,0,1:T(8,128)(2,1)}), bf16[2,8,96,1024]{3,2,0,1:T(8,128)(2,1)S(1)}, u32[]{:S(2)}, u32[]{:S(2)}) async-start(bf16[2,8,96,1024]{3,2,0,1:T(8,128)(2,1)} %copy.37), calls=%async_computation.1 | async-start | bytes 6291456 | tf_op jit(solution)/shard_map/all_to_all | solution.py:59
  409.8 10.7 %gather_fusion.2 = f32[1536]{0:T(1024)S(1)} fusion(f32[16,128]{0,1:T(8,128)S(1)} %bitcast.48, s32[1536]{0:T(1024)S(1)} %reshape.137), kind=kCustom, calls=%fused_computation.2 | custom fusion | bytes 24576 | tf_op jit(solution)/shard_map/jit(take_along_axis)/gather | solution.py:32
  420.5 7.0 %convolution_bitcast_fusion = f32[2,384,1536]{2,1,0:T(8,128)} fusion(bf16[2,8,96,1536]{3,2,1,0:T(8,128)(2,1)} %all-gather.5.cloned.1.call-done, bf16[2,8,96,384]{3,2,1,0:T(8,128)(2,1)} %multiply_convert_fusion.1, f32[2,8,96]{2,1,0:T(8,128)S(1)} %copy.38), kind=kOutput, calls=%fused_computation.14 | convolution fusion | flops 1813708800 | bytes 10622976 | tf_op jit(solution)/shard_map/escu,escv->euv/dot_general | solution.py:56
  427.5 53.0 %all-to-all-done.1 = bf16[2,8,96,1024]{3,2,0,1:T(8,128)(2,1)S(1)} async-done(((bf16[2,8,96,1024]{3,2,0,1:T(8,128)(2,1)}), bf16[2,8,96,1024]{3,2,0,1:T(8,128)(2,1)S(1)}, u32[]{:S(2)}, u32[]{:S(2)}) %all-to-all-start.1) | async-done | bytes 3145760 | tf_op jit(solution)/shard_map/all_to_all | solution.py:59
  480.5 0.7 bitcast_convert_fusion
  481.2 3.1 bitcast_multiply_fusion
  484.4 14.8 %scatter_custom_fusion = f32[128,1024]{1,0:T(8,128)S(1)} fusion(s32[1536]{0:T(1024)S(1)} %fusion.21, f32[1536,1024]{1,0:T(8,128)} %bitcast_multiply_fusion, f32[]{:T(128)} %constant.16.clone.1), kind=kCustom, calls=%fused_computation.24 | custom fusion | flops 1572864 | bytes 524800 | tf_op jit(solution)/shard_map/scatter-add | solution.py:62
  499.1 0.7 convert_element_type.50
  (36 shorter events, 1.3 us)
Async XLA Ops:
  7.2 21.9 %all-gather.3.cloned.1.call-start = ((), (), s32[]{:S(2)}) async-start(), calls=%async_computation.3 | async-start | bytes 1310720 | tf_op jit(solution)/shard_map/all_gather | solution.py:36
  7.9 385.4 %all-gather.5.cloned.1.call-start = ((), (), s32[]{:S(2)}) async-start(), calls=%async_computation.4 | async-start | bytes 5898240 | tf_op jit(solution)/shard_map/all_gather | solution.py:55
  347.6 10.2 %copy-start.2 = (f32[119]{0:T(128)S(1)}, f32[119]{0:T(128)}, u32[]{:S(2)}) copy-start(f32[119]{0:T(128)} %param.12) | copy-start | bytes 1432
  347.6 10.2 %copy-start.3 = (s32[128]{0:T(128)S(1)}, s32[128]{0:T(128)}, u32[]{:S(2)}) copy-start(s32[128]{0:T(128)} %param.11) | copy-start | bytes 1540
  367.6 36.3 %all-to-all-start.2 = ((bf16[8,2,96]{2,1,0:T(2,128)(2,1)}), bf16[8,2,96]{2,1,0:T(2,128)(2,1)S(1)}, u32[]{:S(2)}, u32[]{:S(2)}) async-start(bf16[8,2,96]{2,1,0:T(2,128)(2,1)} %broadcast_select_fusion), calls=%async_computation.2 | async-start | bytes 8192 | tf_op jit(solution)/shard_map/all_to_all | solution.py:46
  401.9 7.7 %copy-start = (s32[128,8]{0,1:T(8,128)S(1)}, s32[128,8]{0,1:T(8,128)}, u32[]{:S(2)}) copy-start(s32[128,8]{0,1:T(8,128)} %param.9) | copy-start | bytes 12292
  401.9 7.7 %copy-start.1 = (f32[128,8]{0,1:T(8,128)S(1)}, f32[128,8]{0,1:T(8,128)}, u32[]{:S(2)}) copy-start(f32[128,8]{0,1:T(8,128)} %param.10) | copy-start | bytes 12292
  403.9 76.6 %all-to-all-start.1 = ((bf16[2,8,96,1024]{3,2,0,1:T(8,128)(2,1)}), bf16[2,8,96,1024]{3,2,0,1:T(8,128)(2,1)S(1)}, u32[]{:S(2)}, u32[]{:S(2)}) async-start(bf16[2,8,96,1024]{3,2,0,1:T(8,128)(2,1)} %copy.37), calls=%async_computation.1 | async-start | bytes 6291456 | tf_op jit(solution)/shard_map/all_to_all | solution.py:59
Sparse Core Ops, SparseCore 0:
  9.6 19.4 all-gather.2
  357.8 35.5 all-gather.4
where the time goes:
time: 507 us
  blocking collectives  279 us (55%)
  waiting for transfers between devices  94.9 us (19%)
  local copies, waits for them, and re-layouts  45.9 us (9%)
  matrix products  35.4 us (7%)
  other arithmetic  28.5 us (6%)
  between operations  14.2 us (3%)
  starting transfers between devices  9.22 us (2%)
    all_to_all x1, blocking collectives, on_device(): lax.all_to_all(rows.reshape(owners, local_exp, capacity, whole.shape[1]),...  279 us
    all_to_all x1, waiting for transfers between devices, on_device(): lax.all_to_all(expert_out, 'expert', split_axis=1, concat_axis=0, tiled=T...  53 us
    gather x1, local copies, waits for them, and re-layouts, on_device(): rows = jnp.take(whole, flat_token, axis=0)  23.4 us
    all_gather x1, waiting for transfers between devices, on_device(): piece = lax.all_gather(hidden, 'col', axis=3, tiled=True)  22.1 us
    all_gather x1, waiting for transfers between devices, on_device(): whole = lax.all_gather(tokens, 'col', axis=1, tiled=True)  19 us
    scatter-add x1, other arithmetic, on_device(): combined.at[flat_token].add(slot_coef.reshape(-1)[:, None] * returned)  14.8 us
    gather x2, local copies, waits for them, and re-layouts, on_device(): jnp.take_along_axis(coefs.T, slot_token, axis=1)  10.7 us
  transfers between devices with their start and end apart: 4, of which 3 were waited for; matrix products, arithmetic and copies ran while one was open for 8% of the time, Pallas kernels for 0%

commit v1 on v0

--- a/solution.py
+++ b/solution.py
@@ -1,10 +1,311 @@
 import jax
 import jax.numpy as jnp
 from jax import lax
+from jax.experimental import pallas as pl
+from jax.experimental.pallas import tpu as pltpu
 from jax.sharding import PartitionSpec as P
 
-
-def on_device(tokens, routes, route_weight, language, lang_weight, w_gate, w_up, w_down):
+F32 = jnp.float32
+BF16 = jnp.bfloat16
+ORDER = (0, 1, 3, 2)
+
+
+def whole(shape):
+    return pl.BlockSpec(shape, lambda *_: (0,) * len(shape))
+
+
+ANY = pl.BlockSpec(memory_space=pl.ANY)
+SMEM = pl.BlockSpec(memory_space=pltpu.SMEM)
+
+
+def route_kernel(place, lang_w, *refs):
+    infos, meta = refs[:-1], refs[-1]
+    tok = infos[0].shape[2]
+    lower = (
+        lax.broadcasted_iota(jnp.int32, (tok, tok), 0)
+        < lax.broadcasted_iota(jnp.int32, (tok, tok), 1)
+    ).astype(BF16)
+    language_ids = lax.broadcasted_iota(jnp.int32, (lang_w.shape[0], tok), 0).astype(F32)
+    hits, coefs, cals = [], [], []
+    for info in infos:
+        for b in range(2):
+            routes, weight, lang = info[b, 0:8, :], info[b, 8:16, :], info[b, 16:17, :]
+            for i in range(2):
+                mine = routes == (place[0] * 2 + i).astype(F32)
+                hits.append(jnp.max(jnp.where(mine, 1.0, 0.0), axis=0, keepdims=True))
+                coefs.append(jnp.sum(jnp.where(mine, weight, 0.0), axis=0, keepdims=True))
+            cal = jnp.sum(jnp.where(language_ids == lang, lang_w[...], 0.0), axis=0, keepdims=True)
+            cals.append(cal.astype(BF16).astype(F32))
+    hit = jnp.concatenate(hits, axis=0)
+    before = jnp.dot(hit.astype(BF16), lower, preferred_element_type=F32)
+    slot = jnp.where(hit > 0.5, before, -1.0)
+    meta[...] = jnp.zeros_like(meta)
+    for k in range(len(infos)):
+        for b in range(2):
+            n = 2 * k + b
+            meta[k, b, 0:2, :] = slot[2 * n : 2 * n + 2, :]
+            meta[k, b, 2:3, :] = coefs[2 * n]
+            meta[k, b, 3:4, :] = coefs[2 * n + 1]
+            meta[k, b, 4:5, :] = cals[n]
+
+
+def route_tables(place, lang_col, infos):
+    return pl.pallas_call(
+        route_kernel,
+        out_shape=jax.ShapeDtypeStruct((len(infos), 2, 8, infos[0].shape[2]), F32),
+        in_specs=[SMEM, whole(lang_col.shape)] + [whole(i.shape) for i in infos],
+        out_specs=whole((len(infos), 2, 8, infos[0].shape[2])),
+        grid=(1,),
+    )(place, lang_col, *infos)
+
+
+def picks(slot_row, cap):
+    rows = lax.broadcasted_iota(jnp.int32, (cap, slot_row.shape[1]), 0).astype(F32)
+    return rows == slot_row
+
+
+def hidden_kernel(cap, place, meta, *refs):
+    pieces, (w_gate, w_up, out, x, sems) = refs[:8], refs[8:]
+    tok, feat = pieces[0].shape
+    e, n = pl.program_id(0), pl.program_id(1)
+
+    @pl.when((e == 0) & (n == 0))
+    def _():
+        col = place[1]
+        copies = []
+        for core in range(2):
+            for b in range(2):
+                for y in range(2):
+                    src = pieces[4 * core + 2 * y + b]
+                    at = pl.multiple_of((col ^ (core + 2 * y)) * feat, feat)
+                    i = 4 * core + 2 * y + b
+                    copies.append(
+                        pltpu.make_async_copy(src, x.at[pl.ds(b * tok, tok), pl.ds(at, feat)], sems.at[i])
+                    )
+        for copy in copies:
+            copy.start()
+        for copy in copies:
+            copy.wait()
+
+    dims = (((1,), (1,)), ((), ()))
+    rows = x[...]
+    gate = lax.dot_general(rows, w_gate[0], dims, preferred_element_type=F32)
+    up = lax.dot_general(rows, w_up[0], dims, preferred_element_type=F32)
+    hidden = (gate / (1.0 + jnp.exp(-gate)) * up).astype(BF16)
+    for b in range(2):
+        slot = meta[b, pl.ds(e, 1), :]
+        pick = jnp.where(picks(slot, cap), 1.0, 0.0).astype(BF16)
+        out[0, b * cap : (b + 1) * cap, :] = jnp.dot(
+            pick, hidden[b * tok : (b + 1) * tok], preferred_element_type=F32
+        ).astype(BF16)
+
+
+def hidden_rows(cap, place, meta, pieces, w_gate, w_up, width=384):
+    experts, units, depth = w_gate.shape
+    tok = pieces[0].shape[0]
+    weight = pl.BlockSpec((1, width, depth), lambda e, n: (e, n, 0))
+    flops = 2 * 2 * 2 * tok * experts * units * depth
+    return pl.pallas_call(
+        lambda *a: hidden_kernel(cap, *a),
+        out_shape=jax.ShapeDtypeStruct((experts, 2 * cap, units), BF16),
+        grid=(experts, units // width),
+        in_specs=[SMEM, whole(meta.shape)] + [ANY] * 8 + [weight, weight],
+        out_specs=pl.BlockSpec((1, 2 * cap, width), lambda e, n: (e, 0, n)),
+        scratch_shapes=[pltpu.VMEM((2 * tok, depth), BF16), pltpu.SemaphoreType.DMA((8,))],
+        compiler_params=pltpu.CompilerParams(vmem_limit_bytes=24 * 2**20),
+        cost_estimate=pl.CostEstimate(flops=flops, bytes_accessed=4 * experts * units * depth, transcendentals=0),
+    )(place, meta, *pieces, w_gate, w_up)
+
+
+def down_kernel(cap, place, meta, *refs):
+    pieces, (w_down, own, other, rows, total, sems) = refs[:4], refs[4:]
+    units = pieces[0].shape[2]
+    tok = meta.shape[2]
+    n, e = pl.program_id(0), pl.program_id(1)
+
+    @pl.when((e == 0) & (n == 0))
+    def _():
+        copies = []
+        for i, src in enumerate(pieces):
+            at = pl.multiple_of((place[1] ^ i) * units, units)
+            copies.append(pltpu.make_async_copy(src, rows.at[:, :, pl.ds(at, units)], sems.at[i]))
+        for copy in copies:
+            copy.start()
+        for copy in copies:
+            copy.wait()
+
+    made = jnp.dot(rows[e], w_down[0], preferred_element_type=F32)
+    for b in range(2):
+        pick = picks(meta[b, pl.ds(e, 1), :], cap)
+        coef = jnp.sum(jnp.where(pick, meta[b, pl.ds(2 + e, 1), :], 0.0), axis=1, keepdims=True)
+        part = (made[b * cap : (b + 1) * cap] * coef).astype(BF16)
+        spread = lax.dot_general(
+            jnp.where(pick, 1.0, 0.0).astype(BF16), part, (((0,), (0,)), ((), ())), preferred_element_type=F32
+        )
+        at = pl.ds(b * tok, tok)
+
+        @pl.when(e == 0)
+        def _():
+            total[at, :] = spread
+
+        @pl.when(e == 1)
+        def _():
+            both = total[at, :] + spread
+            if b == 0:
+                own[...] = both
+            else:
+                other[...] = both.astype(BF16)
+
+
+def down_rows(cap, place, meta, pieces, w_down, width=512):
+    experts, depth, cols = w_down.shape
+    tok = meta.shape[2]
+    units = pieces[0].shape[2]
+    flops = 2 * 2 * cap * experts * depth * cols
+    out = pl.BlockSpec((tok, width), lambda n, e: (0, n))
+    return pl.pallas_call(
+        lambda *a: down_kernel(cap, *a),
+        out_shape=(jax.ShapeDtypeStruct((tok, cols), F32), jax.ShapeDtypeStruct((tok, cols), BF16)),
+        grid=(cols // width, experts),
+        in_specs=[SMEM, whole(meta.shape)]
+        + [ANY] * 4
+        + [pl.BlockSpec((1, depth, width), lambda n, e: (e, 0, n))],
+        out_specs=(out, out),
+        scratch_shapes=[
+            pltpu.VMEM((experts, 2 * cap, depth), BF16),
+            pltpu.VMEM((2 * tok, width), F32),
+            pltpu.SemaphoreType.DMA((4,)),
+        ],
+        compiler_params=pltpu.CompilerParams(vmem_limit_bytes=24 * 2**20),
+        cost_estimate=pl.CostEstimate(flops=flops, bytes_accessed=2 * experts * depth * cols, transcendentals=0),
+    )(place, meta, *pieces, w_down)
+
+
+def gram_kernel(cap, place, meta, *refs):
+    planes = meta.shape[0]
+    pieces, (out, rows, scaled, sems) = refs[: 4 * planes], refs[4 * planes :]
+    units = pieces[0].shape[2]
+    e, n = pl.program_id(0), pl.program_id(1)
+
+    @pl.when((e == 0) & (n == 0))
+    def _():
+        copies = []
+        for k in range(planes):
+            for i in range(4):
+                at = pl.multiple_of((place[1] ^ i) * units, units)
+                copies.append(
+                    pltpu.make_async_copy(
+                        pieces[4 * k + i],
+                        rows.at[:, pl.ds(k * 2 * cap, 2 * cap), pl.ds(at, units)],
+                        sems.at[4 * k + i],
+                    )
+                )
+        for copy in copies:
+            copy.start()
+        for copy in copies:
+            copy.wait()
+
+    @pl.when(n == 0)
+    def _():
+        mine = pl.ds(pl.multiple_of(place[1] * units, units), units)
+        for k in range(planes):
+            for b in range(2):
+                pick = picks(meta[k, b, pl.ds(e, 1), :], cap)
+                cal = jnp.sum(jnp.where(pick, meta[k, b, 4:5, :], 0.0), axis=1, keepdims=True)
+                at = pl.ds((2 * k + b) * cap, cap)
+                scaled[at, :] = (rows[e, at, mine].astype(F32) * cal).astype(BF16)
+
+    width = out.shape[2]
+    right = rows[e, :, pl.ds(pl.multiple_of(n * width, width), width)]
+    out[0] = lax.dot_general(scaled[...], right, (((0,), (0,)), ((), ())), preferred_element_type=F32)
+
+
+def gram_blocks(cap, place, meta, pieces, width=512):
+    planes = meta.shape[0]
+    experts, _, units = pieces[0].shape
+    depth = 4 * units
+    total = planes * 2 * cap
+    return pl.pallas_call(
+        lambda *a: gram_kernel(cap, *a),
+        out_shape=jax.ShapeDtypeStruct((experts, units, depth), F32),
+        grid=(experts, depth // width),
+        in_specs=[SMEM, whole(meta.shape)] + [ANY] * (4 * planes),
+        out_specs=pl.BlockSpec((1, units, width), lambda e, n: (e, 0, n)),
+        scratch_shapes=[
+            pltpu.VMEM((experts, total, depth), BF16),
+            pltpu.VMEM((total, units), BF16),
+            pltpu.SemaphoreType.DMA((4 * planes,)),
+        ],
+        compiler_params=pltpu.CompilerParams(vmem_limit_bytes=24 * 2**20),
+        cost_estimate=pl.CostEstimate(
+            flops=2 * experts * total * units * depth,
+            bytes_accessed=4 * experts * units * depth + 2 * experts * total * depth,
+            transcendentals=0,
+        ),
+    )(place, meta, *pieces)
+
+
+CORE = [(c, c ^ 1) for c in range(4)]
+ACROSS_Y = [(c, c ^ 2) for c in range(4)]
+ACROSS_X = [(e, e ^ 1) for e in range(8)]
+
+
+def planes_up(k):
+    return [(2 * ((z + k) % 4) + x, 2 * z + x) for z in range(4) for x in range(2)]
+
+
+def over_core(a):
+    return lax.ppermute(a, "col", CORE)
+
+
+def over_y(a):
+    return lax.ppermute(a, "col", ACROSS_Y)
+
+
+def over_x(a):
+    return lax.ppermute(a, "expert", ACROSS_X)
+
+
+def over_z(a, k):
+    return lax.ppermute(a, "expert", planes_up(k % 4))
+
+
+def by_planes(tokens, routes, route_weight, language, lang_weight, w_gate, w_up, w_down):
+    tok, top = routes.shape
+    experts = w_gate.shape[0] * lax.axis_size("expert")
+    cap = tok * top * 3 // (2 * experts)
+    place = jnp.stack([lax.axis_index("expert"), lax.axis_index("col")]).astype(jnp.int32)
+    info = jnp.concatenate(
+        [routes.T.astype(F32), route_weight.T, language[None, :].astype(F32), jnp.zeros((7, tok), F32)], axis=0
+    )
+    lang_col = jnp.pad(lang_weight, (0, -lang_weight.shape[0] % 128))[:, None]
+    info0 = jnp.stack([info, over_x(info)])
+    infos = [info0] + [over_z(info0, k) for k in (1, 2, 3)]
+    meta = route_tables(place, lang_col, infos)
+
+    out = None
+    hidden = {}
+    later = []
+    blocks = {k: tokens if k == 0 else over_z(tokens, k) for k in ORDER}
+    for turn, k in enumerate(ORDER):
+        own = blocks[k]
+        by_x = over_x(own)
+        by_y = over_y(own)
+        diagonal = over_x(by_y) if turn % 2 == 0 else over_y(by_x)
+        near = [own, by_x, by_y, diagonal]
+        pieces = near + [over_core(p) for p in near]
+        made = hidden_rows(cap, place, meta[k], pieces, w_gate, w_up)
+        made_y = over_y(made)
+        hidden[k] = [made, over_core(made), made_y, over_core(made_y)]
+        mine, other = down_rows(cap, place, meta[k], hidden[k], w_down)
+        part = mine + over_x(other).astype(F32)
+        later.append(part if k == 0 else over_z(part.astype(BF16), -k))
+    gram = gram_blocks(cap, place, meta, [p for k in range(4) for p in hidden[k]])
+    out = sum(p.astype(F32) for p in later)
+    return out.astype(BF16), gram
+
+
+def by_rows(tokens, routes, route_weight, language, lang_weight, w_gate, w_up, w_down):
     tok_rows = routes.shape[0]
     top_count = routes.shape[1]
     local_exp = w_gate.shape[0]
@@ -75,6 +376,5 @@
         P("expert", None, "col"),
     )
     out_specs = (P("expert", "col"), P("expert", "col", None))
-    return jax.shard_map(
-        on_device, mesh=mesh, in_specs=in_specs, out_specs=out_specs, check_vma=False
-    )
+    body = by_planes if dict(mesh.shape) == {"expert": 8, "col": 4} else by_rows
+    return jax.shard_map(body, mesh=mesh, in_specs=in_specs, out_specs=out_specs, check_vma=False)

time: 507 us -> 171 us (0.34)
  blocking collectives: 279 us -> 0 us
  Pallas kernels: 0 us -> 51.7 us
  starting transfers between devices: 9.22 us -> 51.4 us
  waiting for transfers between devices: 94.9 us -> 52.8 us
  local copies, waits for them, and re-layouts: 45.9 us -> 9.38 us
  matrix products: 35.4 us -> 0 us
  other arithmetic: 28.5 us -> 3.77 us
  between operations: 14.2 us -> 0.89 us
    all_to_all x1 -> x0, blocking collectives: 279 us -> none  [on_device(): lax.all_to_all(rows.reshape(owners, local_exp, capacity, whole.shape[1]),...]
    all_to_all x2 -> x0, waiting for transfers between devices: 53 us -> none  [the longest x1 53 us: on_device(): lax.all_to_all(expert_out, 'expert', split_axis=1, concat_axis=0, tiled=T...]
    ppermute x0 -> x54, waiting for transfers between devices: none -> 52.8 us  [the longest x10 24.4 us: over_y(): return lax.ppermute(a, 'col', ACROSS_Y)]
    pallas_call x0 -> x10, Pallas kernels: none -> 51.7 us  [the longest x4 24.5 us: hidden_rows(): pl.pallas_call(lambda *a: hidden_kernel(cap, *a), out_shape=jax.ShapeDtyp...]
    ppermute x0 -> x54, starting transfers between devices: none -> 51.4 us  [the longest x9 24.3 us: over_z(): return lax.ppermute(a, 'expert', planes_up(k % 4))]
    gather x5 -> x0, local copies, waits for them, and re-layouts: 43.2 us -> none  [the longest x1 23.4 us: on_device(): rows = jnp.take(whole, flat_token, axis=0)]
    all_gather x2 -> x0, waiting for transfers between devices: 41.1 us -> none  [the longest x1 22.1 us: on_device(): piece = lax.all_gather(hidden, 'col', axis=3, tiled=True)]
    dot_general x4 -> x0, matrix products: 35.4 us -> none  [the longest x1 10 us: on_device(): jnp.einsum('seck,efk->escf', arrived, w_up, preferred_element_type=jnp.fl...]
  transfers between devices with their start and end apart: 4 -> 54, of which waited for: 3 -> 15; matrix products, arithmetic and copies ran while one was open for 8% -> 3% of each run, Pallas kernels for 0% -> 30%
where the time goes in v1:
time: 171 us; the launch traced here: 170 us
  waiting for transfers between devices  52.8 us (31%)
  Pallas kernels  51.7 us (30%)
  starting transfers between devices  51.4 us (30%)
  local copies, waits for them, and re-layouts  9.38 us (5%)
  other arithmetic  3.77 us (2%)
    pallas_call x4, Pallas kernels, hidden_rows(): pl.pallas_call(lambda *a: hidden_kernel(cap, *a), out_shape=jax.ShapeDtyp...  24.5 us
    ppermute x10, waiting for transfers between devices, over_y(): return lax.ppermute(a, 'col', ACROSS_Y)  24.4 us
    ppermute x9, starting transfers between devices, over_z(): return lax.ppermute(a, 'expert', planes_up(k % 4))  24.3 us
    pallas_call x4, Pallas kernels, down_rows(): pl.pallas_call(lambda *a: down_kernel(cap, *a), out_shape=(jax.ShapeDtype...  19.2 us
    ppermute x9, waiting for transfers between devices, over_z(): return lax.ppermute(a, 'expert', planes_up(k % 4))  15.6 us
    ppermute x11, waiting for transfers between devices, over_x(): return lax.ppermute(a, 'expert', ACROSS_X)  12.8 us
    ppermute x10, starting transfers between devices, over_y(): return lax.ppermute(a, 'col', ACROSS_Y)  12.5 us
    ppermute x11, starting transfers between devices, over_x(): return lax.ppermute(a, 'expert', ACROSS_X)  10.8 us
  transfers between devices with their start and end apart: 54, of which 15 were waited for; matrix products, arithmetic and copies ran while one was open for 3% of the time, Pallas kernels for 30%

profile of v1, /device:TPU:0, one launch (start us, length us, event | category | flops | bytes accessed | tf_op | source)
XLA Modules:
  0.0 170.0 jit_solution(13527639229104377065)
XLA Ops:
  0.6 4.1 %collective-permute-start.41 = (bf16[128,1024]{1,0:T(8,128)(2,1)}, bf16[128,1024]{1,0:T(8,128)(2,1)S(1)}, u32[]{:S(2)}, u32[]{:S(2)}) collective-permute-start(bf16[128,1024]{1,0:T(8,128)(2,1)} %a_2_.1), channel_id=1, source_target_pairs={{16,0},{20,4},{24,8},{28,12},{0,16},{4,20},{8,24},{12,28},{17,1},{... | collective-permute-start | bytes 786440 | tf_op jit(solution)/shard_map/ppermute | solution.py:270
  15.1 4.1 %collective-permute-done.1.refs_1_ = f32[2,24,128]{2,1,0:T(8,128)S(1)} collective-permute-done((f32[2,24,128]{2,1,0:T(8,128)S(1)}, f32[2,24,128]{2,1,0:T(8,128)S(1)}, u32[]{:S(2)}, u32[]{:S(2)}) %collective-permute-start.1) | collective-permute-done | bytes 24608 | tf_op jit(solution)/shard_map/ppermute | solution.py:270
  21.6 3.0 %collective-permute-done.2.refs_2_ = f32[2,24,128]{2,1,0:T(8,128)S(1)} collective-permute-done((f32[2,24,128]{2,1,0:T(8,128)S(1)}, f32[2,24,128]{2,1,0:T(8,128)S(1)}, u32[]{:S(2)}, u32[]{:S(2)}) %collective-permute-start.2) | collective-permute-done | bytes 24608 | tf_op jit(solution)/shard_map/ppermute | solution.py:270
  40.7 4.0 %collective-permute-done.29.a_3_ = bf16[128,1024]{1,0:T(8,128)(2,1)S(1)} collective-permute-done((bf16[128,1024]{1,0:T(8,128)(2,1)S(1)}, bf16[128,1024]{1,0:T(8,128)(2,1)S(1)}, u32[]{:S(2)}, u32[]{:S(2)}) %collective-permute-start.29) | collective-permute-done | bytes 262176 | tf_op jit(solution)/shard_map/ppermute | solution.py:266
  46.4 2.9 %collective-permute-done.6.a_5_ = bf16[128,1024]{1,0:T(8,128)(2,1)} collective-permute-done((bf16[128,1024]{1,0:T(8,128)(2,1)S(1)}, bf16[128,1024]{1,0:T(8,128)(2,1)}, u32[]{:S(2)}, u32[]{:S(2)}) %collective-permute-start.6) | collective-permute-done | bytes 262176 | tf_op jit(solution)/shard_map/ppermute | solution.py:266
  55.6 2.8 %copy-done = bf16[2,384,4096]{2,1,0:T(8,128)(2,1)S(1)} copy-done((bf16[2,384,4096]{2,1,0:T(8,128)(2,1)S(1)}, bf16[2,384,4096]{2,1,0:T(8,128)(2,1)}, u32[]{:S(2)}) %copy-start) | copy-done | bytes 6291480
  58.4 2.8 %copy-done.2 = bf16[2,384,4096]{2,1,0:T(8,128)(2,1)S(1)} copy-done((bf16[2,384,4096]{2,1,0:T(8,128)(2,1)S(1)}, bf16[2,384,4096]{2,1,0:T(8,128)(2,1)}, u32[]{:S(2)}) %copy-start.2) | copy-done | bytes 6291480
  62.8 7.1 %shard_map.96.a_2_ = bf16[2,192,384]{2,1,0:T(8,128)(2,1)S(1)} custom-call(s32[2]{0:T(128)S(1)} %copy-done.5, f32[2,8,128]{2,1,0:T(8,128)S(1)} %get-tuple-element.18.a_1_, bf16[128,1024]{1,0:T(8,128)(2,1)S(1)} %copy-done.4, bf16[128,1024]{1,0:T(8,128)(2,1)S(1)} %collective-permute-done.4.a_3_, bf16[128,1024]{1,0:T(8,128)(2,1)S(1)} %collective-permute-done.5.a_4_, ...), custom_call_target="tpu_custom_call" | custom-call | flops 3221225472 | bytes 12582912 | tf_op jit(solution)/shard_map/pallas_call | solution.py:108
  72.5 5.8 %shard_map.102.a_2_.a_10_ = bf16[2,192,384]{2,1,0:T(8,128)(2,1)S(1)} custom-call(s32[2]{0:T(128)S(1)} %copy-done.5, f32[2,8,128]{2,1,0:T(8,128)S(1)} %get-tuple-element.19.a_1_, bf16[128,1024]{1,0:T(8,128)(2,1)S(1)} %collective-permute-done.41.a_2_, bf16[128,1024]{1,0:T(8,128)(2,1)S(1)} %collective-permute-done.42.a_3_, ...), custom_call_target="tpu_custom_call" | custom-call | flops 3221225472 | bytes 12582912 | tf_op jit(solution)/shard_map/pallas_call | solution.py:108
  79.7 4.6 %collective-permute-done.18.a_5_ = bf16[128,1024]{1,0:T(8,128)(2,1)S(1)} collective-permute-done((bf16[128,1024]{1,0:T(8,128)(2,1)S(1)}, bf16[128,1024]{1,0:T(8,128)(2,1)S(1)}, u32[]{:S(2)}, u32[]{:S(2)}) %collective-permute-start.18) | collective-permute-done | bytes 262176 | tf_op jit(solution)/shard_map/ppermute | solution.py:262
  84.8 5.8 %shard_map.100.a_2_.a_14_ = bf16[2,192,384]{2,1,0:T(8,128)(2,1)S(1)} custom-call(s32[2]{0:T(128)S(1)} %copy-done.5, f32[2,8,128]{2,1,0:T(8,128)S(1)} %get-tuple-element.20.a_1_, bf16[128,1024]{1,0:T(8,128)(2,1)S(1)} %collective-permute-done.28.a_2_, bf16[128,1024]{1,0:T(8,128)(2,1)S(1)} %collective-permute-done.29.a_3_, ...), custom_call_target="tpu_custom_call" | custom-call | flops 3221225472 | bytes 12582912 | tf_op jit(solution)/shard_map/pallas_call | solution.py:108
  94.1 5.8 %shard_map.98.a_2_.a_6_ = bf16[2,192,384]{2,1,0:T(8,128)(2,1)S(1)} custom-call(s32[2]{0:T(128)S(1)} %copy-done.6, f32[2,8,128]{2,1,0:T(8,128)S(1)} %get-tuple-element.21.a_1_, bf16[128,1024]{1,0:T(8,128)(2,1)S(1)} %collective-permute-done.15.a_2_, bf16[128,1024]{1,0:T(8,128)(2,1)S(1)} %collective-permute-done.16.a_3_, ...), custom_call_target="tpu_custom_call" | custom-call | flops 3221225472 | bytes 12582912 | tf_op jit(solution)/shard_map/pallas_call | solution.py:108
  100.7 6.2 %collective-permute-done.50.a_4_.a_12_ = bf16[2,192,384]{2,1,0:T(8,128)(2,1)S(1)} collective-permute-done((bf16[2,192,384]{2,1,0:T(8,128)(2,1)S(1)}, bf16[2,192,384]{2,1,0:T(8,128)(2,1)S(1)}, u32[]{:S(2)}, u32[]{:S(2)}) %collective-permute-start.50) | collective-permute-done | bytes 294944 | tf_op jit(solution)/shard_map/ppermute | solution.py:262
  107.5 5.7 %collective-permute-done.37.a_4_.a_16_ = bf16[2,192,384]{2,1,0:T(8,128)(2,1)S(1)} collective-permute-done((bf16[2,192,384]{2,1,0:T(8,128)(2,1)S(1)}, bf16[2,192,384]{2,1,0:T(8,128)(2,1)S(1)}, u32[]{:S(2)}, u32[]{:S(2)}) %collective-permute-start.37) | collective-permute-done | bytes 294944 | tf_op jit(solution)/shard_map/ppermute | solution.py:262
  113.2 5.4 %collective-permute-done.24.a_4_.a_8_ = bf16[2,192,384]{2,1,0:T(8,128)(2,1)S(1)} collective-permute-done((bf16[2,192,384]{2,1,0:T(8,128)(2,1)S(1)}, bf16[2,192,384]{2,1,0:T(8,128)(2,1)S(1)}, u32[]{:S(2)}, u32[]{:S(2)}) %collective-permute-start.24) | collective-permute-done | bytes 294944 | tf_op jit(solution)/shard_map/ppermute | solution.py:262
  119.2 4.8 %shard_map.103 = (f32[128,1024]{1,0:T(8,128)S(1)}, bf16[128,1024]{1,0:T(8,128)(2,1)S(1)}) custom-call(s32[2]{0:T(128)S(1)} %copy-done.6, f32[2,8,128]{2,1,0:T(8,128)S(1)} %get-tuple-element.19.a_1_, bf16[2,192,384]{2,1,0:T(8,128)(2,1)S(1)} %shard_map.102.a_2_.a_10_, bf16[2,192,384]{2,1,0:T(8,128)(2,1)S(1)} %collective-permute-done.49.a_3_.a_11_, ...), custom_call_target="tpu_custom_call" | custom-call | flops 1207959552 | bytes 6291456 | tf_op jit(solution)/shard_map/pallas_call | solution.py:166
  125.3 4.8 %shard_map.97 = (f32[128,1024]{1,0:T(8,128)S(1)}, bf16[128,1024]{1,0:T(8,128)(2,1)S(1)}) custom-call(s32[2]{0:T(128)S(1)} %copy-done.6, f32[2,8,128]{2,1,0:T(8,128)S(1)} %get-tuple-element.18.a_1_, bf16[2,192,384]{2,1,0:T(8,128)(2,1)S(1)} %shard_map.96.a_2_, bf16[2,192,384]{2,1,0:T(8,128)(2,1)S(1)} %collective-permute-done.11.a_3_, ...), custom_call_target="tpu_custom_call" | custom-call | flops 1207959552 | bytes 6291456 | tf_op jit(solution)/shard_map/pallas_call | solution.py:166
  131.0 4.8 %shard_map.101 = (f32[128,1024]{1,0:T(8,128)S(1)}, bf16[128,1024]{1,0:T(8,128)(2,1)S(1)}) custom-call(s32[2]{0:T(128)S(1)} %copy-done.6, f32[2,8,128]{2,1,0:T(8,128)S(1)} %get-tuple-element.20.a_1_, bf16[2,192,384]{2,1,0:T(8,128)(2,1)S(1)} %shard_map.100.a_2_.a_14_, bf16[2,192,384]{2,1,0:T(8,128)(2,1)S(1)} %collective-permute-done.36.a_3_.a_15_, ...), custom_call_target="tpu_custom_call" | custom-call | flops 1207959552 | bytes 6291456 | tf_op jit(solution)/shard_map/pallas_call | solution.py:166
  137.1 4.8 %shard_map.99 = (f32[128,1024]{1,0:T(8,128)S(1)}, bf16[128,1024]{1,0:T(8,128)(2,1)S(1)}) custom-call(s32[2]{0:T(128)S(1)} %copy-done.6, f32[2,8,128]{2,1,0:T(8,128)S(1)} %get-tuple-element.21.a_1_, bf16[2,192,384]{2,1,0:T(8,128)(2,1)S(1)} %shard_map.98.a_2_.a_6_, bf16[2,192,384]{2,1,0:T(8,128)(2,1)S(1)} %collective-permute-done.23.a_3_.a_7_, ...), custom_call_target="tpu_custom_call" | custom-call | flops 1207959552 | bytes 6291456 | tf_op jit(solution)/shard_map/pallas_call | solution.py:166
  142.9 6.1 %collective-permute-start.53 = (bf16[128,1024]{1,0:T(8,128)(2,1)S(1)}, bf16[128,1024]{1,0:T(8,128)(2,1)S(1)}, u32[]{:S(2)}, u32[]{:S(2)}) collective-permute-start(bf16[128,1024]{1,0:T(8,128)(2,1)S(1)} %add_convert_fusion.1), channel_id=1, source_target_pairs={{16,0},{20,4},{24,8},{28,12},{0,16},{4,20},{8,24},{12,28},{17,1},{... | collective-permute-start | bytes 786440 | tf_op jit(solution)/shard_map/ppermute | solution.py:270
  149.1 4.4 %collective-permute-start.40 = (bf16[128,1024]{1,0:T(8,128)(2,1)S(1)}, bf16[128,1024]{1,0:T(8,128)(2,1)S(1)}, u32[]{:S(2)}, u32[]{:S(2)}) collective-permute-start(bf16[128,1024]{1,0:T(8,128)(2,1)S(1)} %add_convert_fusion.2), channel_id=1, source_target_pairs={{8,0},{12,4},{16,8},{20,12},{24,16},{28,20},{0,24},{4,28},{9,1},{1... | collective-permute-start | bytes 786440 | tf_op jit(solution)/shard_map/ppermute | solution.py:270
  153.6 2.8 %collective-permute-start.27 = (bf16[128,1024]{1,0:T(8,128)(2,1)S(1)}, bf16[128,1024]{1,0:T(8,128)(2,1)S(1)}, u32[]{:S(2)}, u32[]{:S(2)}) collective-permute-start(bf16[128,1024]{1,0:T(8,128)(2,1)S(1)} %add_convert_fusion.3), channel_id=1, source_target_pairs={{24,0},{28,4},{0,8},{4,12},{8,16},{12,20},{16,24},{20,28},{25,1},{... | collective-permute-start | bytes 786440 | tf_op jit(solution)/shard_map/ppermute | solution.py:270
  156.3 6.3 %shard_map.104 = f32[2,384,1536]{2,1,0:T(8,128)} custom-call(s32[2]{0:T(128)S(1)} %copy-done.6, f32[4,2,8,128]{3,2,1,0:T(8,128)S(1)} %copy-done.3, bf16[2,192,384]{2,1,0:T(8,128)(2,1)S(1)} %shard_map.96.a_2_, bf16[2,192,384]{2,1,0:T(8,128)(2,1)S(1)} %collective-permute-done.11.a_3_, bf16[2,192,384]{2,1,0:T(8,128)(2,1)S(1)} %collective-permute-done.12.a_4_, ...), custom_call_target="tpu_custom_call" | custom-call | flops 1811939328 | bytes 9437184 | tf_op jit(solution)/shard_map/pallas_call | solution.py:228
  162.6 6.4 %collective-permute-done.27 = bf16[128,1024]{1,0:T(8,128)(2,1)S(1)} collective-permute-done((bf16[128,1024]{1,0:T(8,128)(2,1)S(1)}, bf16[128,1024]{1,0:T(8,128)(2,1)S(1)}, u32[]{:S(2)}, u32[]{:S(2)}) %collective-permute-start.27) | collective-permute-done | bytes 262176 | tf_op jit(solution)/shard_map/ppermute | solution.py:270
  (135 shorter events, 53.7 us)
Async XLA Ops:
  0.6 27.1 %collective-permute-start.41 = (bf16[128,1024]{1,0:T(8,128)(2,1)}, bf16[128,1024]{1,0:T(8,128)(2,1)S(1)}, u32[]{:S(2)}, u32[]{:S(2)}) collective-permute-start(bf16[128,1024]{1,0:T(8,128)(2,1)} %a_2_.1), channel_id=1, source_target_pairs={{16,0},{20,4},{24,8},{28,12},{0,16},{4,20},{8,24},{12,28},{17,1},{... | collective-permute-start | bytes 786440 | tf_op jit(solution)/shard_map/ppermute | solution.py:270
  4.7 23.0 %collective-permute-start.28 = (bf16[128,1024]{1,0:T(8,128)(2,1)}, bf16[128,1024]{1,0:T(8,128)(2,1)S(1)}, u32[]{:S(2)}, u32[]{:S(2)}) collective-permute-start(bf16[128,1024]{1,0:T(8,128)(2,1)} %a_2_.1), channel_id=1, source_target_pairs={{24,0},{28,4},{0,8},{4,12},{8,16},{12,20},{16,24},{20,28},{25,1},{... | collective-permute-start | bytes 786440 | tf_op jit(solution)/shard_map/ppermute | solution.py:270
  40.2 14.3 %collective-permute-start.9 = (bf16[128,1024]{1,0:T(8,128)(2,1)S(1)}, bf16[128,1024]{1,0:T(8,128)(2,1)}, u32[]{:S(2)}, u32[]{:S(2)}) collective-permute-start(bf16[128,1024]{1,0:T(8,128)(2,1)S(1)} %collective-permute-done.5.a_4_), channel_id=1, source_target_pairs={{0,1},{1,0},{2,3},{3,2},{4,5},{5,4},{6,7},{7,6},{8,9},{9,8},{10,11... | collective-permute-start | bytes 786440 | tf_op jit(solution)/shard_map/ppermute | solution.py:258
  53.0 16.9 %collective-permute-start.16 = (bf16[128,1024]{1,0:T(8,128)(2,1)S(1)}, bf16[128,1024]{1,0:T(8,128)(2,1)S(1)}, u32[]{:S(2)}, u32[]{:S(2)}) collective-permute-start(bf16[128,1024]{1,0:T(8,128)(2,1)S(1)} %collective-permute-done.15.a_2_), channel_id=1, source_target_pairs={{0,4},{4,0},{8,12},{12,8},{16,20},{20,16},{24,28},{28,24},{1,5},{5... | collective-permute-start | bytes 786440 | tf_op jit(solution)/shard_map/ppermute | solution.py:266
  54.3 16.9 %collective-permute-start.46 = (bf16[128,1024]{1,0:T(8,128)(2,1)S(1)}, bf16[128,1024]{1,0:T(8,128)(2,1)S(1)}, u32[]{:S(2)}, u32[]{:S(2)}) collective-permute-start(bf16[128,1024]{1,0:T(8,128)(2,1)S(1)} %collective-permute-done.42.a_3_), channel_id=1, source_target_pairs={{0,1},{1,0},{2,3},{3,2},{4,5},{5,4},{6,7},{7,6},{8,9},{9,8},{10,11... | collective-permute-start | bytes 786440 | tf_op jit(solution)/shard_map/ppermute | solution.py:258
  54.5 16.9 %collective-permute-start.47 = (bf16[128,1024]{1,0:T(8,128)(2,1)S(1)}, bf16[128,1024]{1,0:T(8,128)(2,1)S(1)}, u32[]{:S(2)}, u32[]{:S(2)}) collective-permute-start(bf16[128,1024]{1,0:T(8,128)(2,1)S(1)} %collective-permute-done.43.a_4_), channel_id=1, source_target_pairs={{0,1},{1,0},{2,3},{3,2},{4,5},{5,4},{6,7},{7,6},{8,9},{9,8},{10,11... | collective-permute-start | bytes 786440 | tf_op jit(solution)/shard_map/ppermute | solution.py:258
  54.8 16.9 %collective-permute-start.31 = (bf16[128,1024]{1,0:T(8,128)(2,1)S(1)}, bf16[128,1024]{1,0:T(8,128)(2,1)S(1)}, u32[]{:S(2)}, u32[]{:S(2)}) collective-permute-start(bf16[128,1024]{1,0:T(8,128)(2,1)S(1)} %collective-permute-done.30.a_4_), channel_id=1, source_target_pairs={{0,4},{4,0},{8,12},{12,8},{16,20},{20,16},{24,28},{28,24},{1,5},{5... | collective-permute-start | bytes 786440 | tf_op jit(solution)/shard_map/ppermute | solution.py:266
  55.6 16.9 %collective-permute-start.48 = (bf16[128,1024]{1,0:T(8,128)(2,1)S(1)}, bf16[128,1024]{1,0:T(8,128)(2,1)S(1)}, u32[]{:S(2)}, u32[]{:S(2)}) collective-permute-start(bf16[128,1024]{1,0:T(8,128)(2,1)S(1)} %collective-permute-done.44.a_5_), channel_id=1, source_target_pairs={{0,1},{1,0},{2,3},{3,2},{4,5},{5,4},{6,7},{7,6},{8,9},{9,8},{10,11... | collective-permute-start | bytes 786440 | tf_op jit(solution)/shard_map/ppermute | solution.py:258
  84.3 15.5 %collective-permute-start.11 = (bf16[2,192,384]{2,1,0:T(8,128)(2,1)S(1)}, bf16[2,192,384]{2,1,0:T(8,128)(2,1)S(1)}, u32[]{:S(2)}, u32[]{:S(2)}) collective-permute-start(bf16[2,192,384]{2,1,0:T(8,128)(2,1)S(1)} %shard_map.96.a_2_), channel_id=1, source_target_pairs={{0,1},{1,0},{2,3},{3,2},{4,5},{5,4},{6,7},{7,6},{8,9},{9,8},{10,11... | collective-permute-start | bytes 884744 | tf_op jit(solution)/shard_map/ppermute | solution.py:258
  90.7 16.3 %collective-permute-start.12 = (bf16[2,192,384]{2,1,0:T(8,128)(2,1)S(1)}, bf16[2,192,384]{2,1,0:T(8,128)(2,1)S(1)}, u32[]{:S(2)}, u32[]{:S(2)}) collective-permute-start(bf16[2,192,384]{2,1,0:T(8,128)(2,1)S(1)} %shard_map.96.a_2_), channel_id=1, source_target_pairs={{0,2},{1,3},{2,0},{3,1},{4,6},{5,7},{6,4},{7,5},{8,10},{9,11},{10,... | collective-permute-start | bytes 884744 | tf_op jit(solution)/shard_map/ppermute | solution.py:262
  92.0 15.5 %collective-permute-start.49 = (bf16[2,192,384]{2,1,0:T(8,128)(2,1)S(1)}, bf16[2,192,384]{2,1,0:T(8,128)(2,1)S(1)}, u32[]{:S(2)}, u32[]{:S(2)}) collective-permute-start(bf16[2,192,384]{2,1,0:T(8,128)(2,1)S(1)} %shard_map.102.a_2_.a_10_), channel_id=1, source_target_pairs={{0,1},{1,0},{2,3},{3,2},{4,5},{5,4},{6,7},{7,6},{8,9},{9,8},{10,11... | collective-permute-start | bytes 884744 | tf_op jit(solution)/shard_map/ppermute | solution.py:258
  92.0 14.9 %collective-permute-start.50 = (bf16[2,192,384]{2,1,0:T(8,128)(2,1)S(1)}, bf16[2,192,384]{2,1,0:T(8,128)(2,1)S(1)}, u32[]{:S(2)}, u32[]{:S(2)}) collective-permute-start(bf16[2,192,384]{2,1,0:T(8,128)(2,1)S(1)} %shard_map.102.a_2_.a_10_), channel_id=1, source_target_pairs={{0,2},{1,3},{2,0},{3,1},{4,6},{5,7},{6,4},{7,5},{8,10},{9,11},{10,... | collective-permute-start | bytes 884744 | tf_op jit(solution)/shard_map/ppermute | solution.py:262
  92.8 20.4 %collective-permute-start.37 = (bf16[2,192,384]{2,1,0:T(8,128)(2,1)S(1)}, bf16[2,192,384]{2,1,0:T(8,128)(2,1)S(1)}, u32[]{:S(2)}, u32[]{:S(2)}) collective-permute-start(bf16[2,192,384]{2,1,0:T(8,128)(2,1)S(1)} %shard_map.100.a_2_.a_14_), channel_id=1, source_target_pairs={{0,2},{1,3},{2,0},{3,1},{4,6},{5,7},{6,4},{7,5},{8,10},{9,11},{10,... | collective-permute-start | bytes 884744 | tf_op jit(solution)/shard_map/ppermute | solution.py:262
  99.9 18.8 %collective-permute-start.24 = (bf16[2,192,384]{2,1,0:T(8,128)(2,1)S(1)}, bf16[2,192,384]{2,1,0:T(8,128)(2,1)S(1)}, u32[]{:S(2)}, u32[]{:S(2)}) collective-permute-start(bf16[2,192,384]{2,1,0:T(8,128)(2,1)S(1)} %shard_map.98.a_2_.a_6_), channel_id=1, source_target_pairs={{0,2},{1,3},{2,0},{3,1},{4,6},{5,7},{6,4},{7,5},{8,10},{9,11},{10,... | collective-permute-start | bytes 884744 | tf_op jit(solution)/shard_map/ppermute | solution.py:262
  106.9 17.1 %collective-permute-start.13 = (bf16[2,192,384]{2,1,0:T(8,128)(2,1)S(1)}, bf16[2,192,384]{2,1,0:T(8,128)(2,1)S(1)}, u32[]{:S(2)}, u32[]{:S(2)}) collective-permute-start(bf16[2,192,384]{2,1,0:T(8,128)(2,1)S(1)} %collective-permute-done.12.a_4_), channel_id=1, source_target_pairs={{0,1},{1,0},{2,3},{3,2},{4,5},{5,4},{6,7},{7,6},{8,9},{9,8},{10,11... | collective-permute-start | bytes 884744 | tf_op jit(solution)/shard_map/ppermute | solution.py:258
  107.4 22.7 %collective-permute-start.36 = (bf16[2,192,384]{2,1,0:T(8,128)(2,1)S(1)}, bf16[2,192,384]{2,1,0:T(8,128)(2,1)S(1)}, u32[]{:S(2)}, u32[]{:S(2)}) collective-permute-start(bf16[2,192,384]{2,1,0:T(8,128)(2,1)S(1)} %shard_map.100.a_2_.a_14_), channel_id=1, source_target_pairs={{0,1},{1,0},{2,3},{3,2},{4,5},{5,4},{6,7},{7,6},{8,9},{9,8},{10,11... | collective-permute-start | bytes 884744 | tf_op jit(solution)/shard_map/ppermute | solution.py:258
  113.2 17.7 %collective-permute-start.38 = (bf16[2,192,384]{2,1,0:T(8,128)(2,1)S(1)}, bf16[2,192,384]{2,1,0:T(8,128)(2,1)S(1)}, u32[]{:S(2)}, u32[]{:S(2)}) collective-permute-start(bf16[2,192,384]{2,1,0:T(8,128)(2,1)S(1)} %collective-permute-done.37.a_4_.a_16_), channel_id=1, source_target_pairs={{0,1},{1,0},{2,3},{3,2},{4,5},{5,4},{6,7},{7,6},{8,9},{9,8},{10,11... | collective-permute-start | bytes 884744 | tf_op jit(solution)/shard_map/ppermute | solution.py:258
  118.6 18.4 %collective-permute-start.23 = (bf16[2,192,384]{2,1,0:T(8,128)(2,1)S(1)}, bf16[2,192,384]{2,1,0:T(8,128)(2,1)S(1)}, u32[]{:S(2)}, u32[]{:S(2)}) collective-permute-start(bf16[2,192,384]{2,1,0:T(8,128)(2,1)S(1)} %shard_map.98.a_2_.a_6_), channel_id=1, source_target_pairs={{0,1},{1,0},{2,3},{3,2},{4,5},{5,4},{6,7},{7,6},{8,9},{9,8},{10,11... | collective-permute-start | bytes 884744 | tf_op jit(solution)/shard_map/ppermute | solution.py:258
  118.6 18.4 %collective-permute-start.25 = (bf16[2,192,384]{2,1,0:T(8,128)(2,1)S(1)}, bf16[2,192,384]{2,1,0:T(8,128)(2,1)S(1)}, u32[]{:S(2)}, u32[]{:S(2)}) collective-permute-start(bf16[2,192,384]{2,1,0:T(8,128)(2,1)S(1)} %collective-permute-done.24.a_4_.a_8_), channel_id=1, source_target_pairs={{0,1},{1,0},{2,3},{3,2},{4,5},{5,4},{6,7},{7,6},{8,9},{9,8},{10,11... | collective-permute-start | bytes 884744 | tf_op jit(solution)/shard_map/ppermute | solution.py:258
  124.0 18.8 %collective-permute-start.52 = (bf16[128,1024]{1,0:T(8,128)(2,1)S(1)}, bf16[128,1024]{1,0:T(8,128)(2,1)S(1)}, u32[]{:S(2)}, u32[]{:S(2)}) collective-permute-start(bf16[128,1024]{1,0:T(8,128)(2,1)S(1)} %get-tuple-element.17), channel_id=1, source_target_pairs={{0,4},{4,0},{8,12},{12,8},{16,20},{20,16},{24,28},{28,24},{1,5},{5... | collective-permute-start | bytes 786440 | tf_op jit(solution)/shard_map/ppermute | solution.py:266
  130.1 32.5 %collective-permute-start.14 = (bf16[128,1024]{1,0:T(8,128)(2,1)S(1)}, bf16[128,1024]{1,0:T(8,128)(2,1)S(1)}, u32[]{:S(2)}, u32[]{:S(2)}) collective-permute-start(bf16[128,1024]{1,0:T(8,128)(2,1)S(1)} %get-tuple-element.11), channel_id=1, source_target_pairs={{0,4},{4,0},{8,12},{12,8},{16,20},{20,16},{24,28},{28,24},{1,5},{5... | collective-permute-start | bytes 786440 | tf_op jit(solution)/shard_map/ppermute | solution.py:266
  142.9 19.8 %collective-permute-start.53 = (bf16[128,1024]{1,0:T(8,128)(2,1)S(1)}, bf16[128,1024]{1,0:T(8,128)(2,1)S(1)}, u32[]{:S(2)}, u32[]{:S(2)}) collective-permute-start(bf16[128,1024]{1,0:T(8,128)(2,1)S(1)} %add_convert_fusion.1), channel_id=1, source_target_pairs={{16,0},{20,4},{24,8},{28,12},{0,16},{4,20},{8,24},{12,28},{17,1},{... | collective-permute-start | bytes 786440 | tf_op jit(solution)/shard_map/ppermute | solution.py:270
  149.1 13.6 %collective-permute-start.40 = (bf16[128,1024]{1,0:T(8,128)(2,1)S(1)}, bf16[128,1024]{1,0:T(8,128)(2,1)S(1)}, u32[]{:S(2)}, u32[]{:S(2)}) collective-permute-start(bf16[128,1024]{1,0:T(8,128)(2,1)S(1)} %add_convert_fusion.2), channel_id=1, source_target_pairs={{8,0},{12,4},{16,8},{20,12},{24,16},{28,20},{0,24},{4,28},{9,1},{1... | collective-permute-start | bytes 786440 | tf_op jit(solution)/shard_map/ppermute | solution.py:270
  153.6 15.5 %collective-permute-start.27 = (bf16[128,1024]{1,0:T(8,128)(2,1)S(1)}, bf16[128,1024]{1,0:T(8,128)(2,1)S(1)}, u32[]{:S(2)}, u32[]{:S(2)}) collective-permute-start(bf16[128,1024]{1,0:T(8,128)(2,1)S(1)} %add_convert_fusion.3), channel_id=1, source_target_pairs={{24,0},{28,4},{0,8},{4,12},{8,16},{12,20},{16,24},{20,28},{25,1},{... | collective-permute-start | bytes 786440 | tf_op jit(solution)/shard_map/ppermute | solution.py:270
  (43 other events, 526.5 us)

commit v2 on v0

--- a/solution.py
+++ b/solution.py
@@ -1,10 +1,339 @@
 import jax
 import jax.numpy as jnp
 from jax import lax
+from jax.experimental import pallas as pl
+from jax.experimental.pallas import tpu as pltpu
 from jax.sharding import PartitionSpec as P
 
-
-def on_device(tokens, routes, route_weight, language, lang_weight, w_gate, w_up, w_down):
+F32 = jnp.float32
+BF16 = jnp.bfloat16
+ORDER = (0, 1, 2, 3)
+
+
+def whole(shape):
+    return pl.BlockSpec(shape, lambda *_: (0,) * len(shape))
+
+
+ANY = pl.BlockSpec(memory_space=pl.ANY)
+SMEM = pl.BlockSpec(memory_space=pltpu.SMEM)
+VMEM = pl.BlockSpec(memory_space=pltpu.VMEM)
+HBM = pl.BlockSpec(memory_space=pltpu.HBM)
+
+
+def fill_routes(place, lang_w, info, meta):
+    tok = info.shape[2]
+    lower = (
+        lax.broadcasted_iota(jnp.int32, (tok, tok), 0)
+        < lax.broadcasted_iota(jnp.int32, (tok, tok), 1)
+    ).astype(BF16)
+    language_ids = lax.broadcasted_iota(jnp.int32, (lang_w.shape[1], tok), 0).astype(F32)
+    lang_column = jnp.broadcast_to(lang_w[...], (tok, lang_w.shape[1])).T
+    meta[...] = jnp.zeros_like(meta)
+    for b in range(2):
+        routes, weight, lang = info[b, 0:8, :], info[b, 8:16, :], info[b, 16:17, :]
+        hits = []
+        for i in range(2):
+            mine = routes == (place[0] * 2 + i).astype(F32)
+            hits.append(jnp.max(jnp.where(mine, 1.0, 0.0), axis=0, keepdims=True))
+            meta[b, 2 + i : 3 + i, :] = jnp.sum(jnp.where(mine, weight, 0.0), axis=0, keepdims=True)
+        hit = jnp.concatenate(hits + [jnp.zeros((6, tok), F32)], axis=0)
+        before = jnp.dot(hit.astype(BF16), lower, preferred_element_type=F32)
+        meta[b, 0:2, :] = jnp.where(hit > 0.5, before, -1.0)[0:2]
+        cal = jnp.sum(jnp.where(language_ids == lang, lang_column, 0.0), axis=0, keepdims=True)
+        meta[b, 4:5, :] = cal.astype(BF16).astype(F32)
+
+
+def picks(slot_row, cap):
+    rows = lax.broadcasted_iota(jnp.int32, (cap, slot_row.shape[1]), 0).astype(F32)
+    return rows == slot_row
+
+
+def in_hbm(a):
+    return pltpu.with_memory_space_constraint(a, pltpu.HBM)
+
+
+def held(a):
+    return pltpu.with_memory_space_constraint(a, pltpu.VMEM)
+
+
+def hidden_kernel(cap, first, place, lang_w, info, *refs):
+    if first:
+        pieces, (w_gate, w_up, out, meta, gate_held, up_held, x, sems, weight_sems) = refs[:-9], refs[-9:]
+    else:
+        pieces, (gate_held, up_held, out, meta, x, sems) = refs[:-6], refs[-6:]
+    tok = meta.shape[2]
+    feat = x.shape[1] // 4
+    half = len(pieces) // 2
+    experts = gate_held.shape[0]
+    copies = []
+    for core in range(2):
+        row = 0
+        for i in range(half):
+            src = pieces[core * half + i]
+            b, y = ((0, 0), (1, 0), (0, 1))[i] if i < 3 else (1, 1)
+            at = pl.multiple_of((place[1] ^ (core + 2 * y)) * feat, feat)
+            dst = x.at[pl.ds(b * tok + row, src.shape[0]), pl.ds(at, feat)]
+            if i >= 3:
+                row += src.shape[0]
+            copies.append(pltpu.make_async_copy(src, dst, sems.at[core * half + i]))
+    if first:
+        for i, (src, dst) in enumerate(((w_gate, gate_held), (w_up, up_held))):
+            copies += [
+                pltpu.make_async_copy(src.at[e], dst.at[e], weight_sems.at[2 * e + i]) for e in range(experts)
+            ]
+    for copy in copies:
+        copy.start()
+    fill_routes(place, lang_w, info, meta)
+    for copy in copies:
+        copy.wait()
+    dims = (((1,), (1,)), ((), ()))
+    for e in range(experts):
+        gate = lax.dot_general(gate_held[e], x[...], dims, preferred_element_type=F32)
+        up = lax.dot_general(up_held[e], x[...], dims, preferred_element_type=F32)
+        hidden = (gate / (1.0 + jnp.exp(-gate)) * up).astype(BF16)
+        for b in range(2):
+            pick = jnp.where(picks(meta[b, e : e + 1, :], cap), 1.0, 0.0).astype(BF16)
+            out[e, b * cap : (b + 1) * cap, :] = lax.dot_general(
+                pick, hidden[:, b * tok : (b + 1) * tok], dims, preferred_element_type=F32
+            ).astype(BF16)
+
+
+def hidden_rows(cap, first, place, lang_row, info, pieces, w_gate, w_up):
+    experts, units, depth = w_gate.shape
+    tok = info.shape[2]
+    outs = (pltpu.VMEM((experts, 2 * cap, units), BF16), jax.ShapeDtypeStruct((2, 8, tok), F32))
+    scratch = [pltpu.VMEM((2 * tok, depth), BF16), pltpu.SemaphoreType.DMA((len(pieces),))]
+    if first:
+        outs += (pltpu.VMEM(w_gate.shape, BF16), pltpu.VMEM(w_up.shape, BF16))
+        scratch.append(pltpu.SemaphoreType.DMA((2 * experts,)))
+    where = in_hbm if first else held
+    return pl.pallas_call(
+        lambda *a: hidden_kernel(cap, first, *a),
+        out_shape=outs,
+        in_specs=[SMEM, VMEM, VMEM] + [ANY] * len(pieces) + [HBM if first else VMEM] * 2,
+        out_specs=(VMEM,) * len(outs),
+        scratch_shapes=scratch,
+        compiler_params=pltpu.CompilerParams(vmem_limit_bytes=8 * 2**20),
+        cost_estimate=pl.CostEstimate(
+            flops=8 * tok * experts * units * depth, bytes_accessed=0, transcendentals=0
+        ),
+    )(place, lang_row, info, *map(in_hbm, pieces), where(w_gate), where(w_up))
+
+
+def down_kernel(cap, place, meta, made, made_c, made_y, made_d, w_down, rows, own, other, total, sems):
+    units = made.shape[2]
+    tok = meta.shape[2]
+    copies = []
+    for i, src in enumerate((made, made_c, made_y, made_d)):
+        at = pl.multiple_of((place[1] ^ i) * units, units)
+        copies.append(pltpu.make_async_copy(src, rows.at[:, :, pl.ds(at, units)], sems.at[i]))
+    for copy in copies:
+        copy.start()
+    for copy in copies:
+        copy.wait()
+    for e in range(w_down.shape[0]):
+        eo = jnp.dot(rows[e], w_down[e], preferred_element_type=F32)
+        for b in range(2):
+            pick = picks(meta[b, e : e + 1, :], cap)
+            coef = jnp.sum(jnp.where(pick, meta[b, 2 + e : 3 + e, :], 0.0), axis=1, keepdims=True)
+            part = (eo[b * cap : (b + 1) * cap] * coef).astype(BF16)
+            spread = lax.dot_general(
+                jnp.where(pick, 1.0, 0.0).astype(BF16), part, (((0,), (0,)), ((), ())), preferred_element_type=F32
+            )
+            at = pl.ds(b * tok, tok)
+            if e == 0:
+                total[at, :] = spread
+            elif b == 0:
+                own[...] = total[at, :] + spread
+            else:
+                other[...] = (total[at, :] + spread).astype(BF16)
+
+
+def down_rows(cap, place, meta, pieces, w_down):
+    experts, depth, cols = w_down.shape
+    tok = meta.shape[2]
+    return pl.pallas_call(
+        lambda *a: down_kernel(cap, *a),
+        out_shape=(
+            pltpu.VMEM((experts, 2 * cap, depth), BF16),
+            pltpu.VMEM((tok, cols), F32),
+            pltpu.VMEM((tok, cols), BF16),
+        ),
+        in_specs=[SMEM, VMEM] + [ANY] * 4 + [VMEM],
+        out_specs=(VMEM, VMEM, VMEM),
+        scratch_shapes=[pltpu.VMEM((2 * tok, cols), F32), pltpu.SemaphoreType.DMA((4,))],
+        compiler_params=pltpu.CompilerParams(vmem_limit_bytes=8 * 2**20),
+        cost_estimate=pl.CostEstimate(
+            flops=4 * cap * experts * depth * cols, bytes_accessed=0, transcendentals=0
+        ),
+    )(place, meta, *pieces, held(w_down))
+
+
+def gram_kernel(cap, place, *refs):
+    planes = len(refs) // 2 - 2
+    metas, parts, (out, rows, scaled, sems) = refs[:planes], refs[planes : 2 * planes], refs[2 * planes :]
+    units = scaled.shape[1]
+    e, n = pl.program_id(0), pl.program_id(1)
+
+    @pl.when((e == 0) & (n == 0))
+    def _():
+        copies = [
+            pltpu.make_async_copy(parts[k], rows.at[:, pl.ds(k * 2 * cap, 2 * cap), :], sems.at[k])
+            for k in range(planes)
+        ]
+        for copy in copies:
+            copy.start()
+        for copy in copies:
+            copy.wait()
+
+    @pl.when(n == 0)
+    def _():
+        mine = pl.ds(pl.multiple_of(place[1] * units, units), units)
+        for k in range(planes):
+            for b in range(2):
+                pick = picks(metas[k][b, pl.ds(e, 1), :], cap)
+                cal = jnp.sum(jnp.where(pick, metas[k][b, 4:5, :], 0.0), axis=1, keepdims=True)
+                at = pl.ds((2 * k + b) * cap, cap)
+                scaled[at, :] = (rows[e, at, mine].astype(F32) * cal).astype(BF16)
+
+    width = out.shape[2]
+    right = rows[e, :, pl.ds(pl.multiple_of(n * width, width), width)]
+    out[0] = lax.dot_general(scaled[...], right, (((0,), (0,)), ((), ())), preferred_element_type=F32)
+
+
+def gram_blocks(cap, place, metas, parts, width=768):
+    planes = len(parts)
+    experts, _, depth = parts[0].shape
+    units = depth // 4
+    total = planes * 2 * cap
+    return pl.pallas_call(
+        lambda *a: gram_kernel(cap, *a),
+        out_shape=jax.ShapeDtypeStruct((experts, units, depth), F32),
+        grid=(experts, depth // width),
+        in_specs=[SMEM] + [whole(m.shape) for m in metas] + [ANY] * planes,
+        out_specs=pl.BlockSpec((1, units, width), lambda e, n: (e, 0, n)),
+        scratch_shapes=[
+            pltpu.VMEM((experts, total, depth), BF16),
+            pltpu.VMEM((total, units), BF16),
+            pltpu.SemaphoreType.DMA((planes,)),
+        ],
+        compiler_params=pltpu.CompilerParams(vmem_limit_bytes=11 * 2**20),
+        cost_estimate=pl.CostEstimate(
+            flops=2 * experts * total * units * depth, bytes_accessed=4 * experts * units * depth, transcendentals=0
+        ),
+    )(place, *metas, *parts)
+
+
+CORE = [(c, c ^ 1) for c in range(4)]
+ACROSS_Y = [(c, c ^ 2) for c in range(4)]
+ACROSS_X = [(e, e ^ 1) for e in range(8)]
+
+
+def planes_up(k):
+    return [(2 * ((z + k) % 4) + x, 2 * z + x) for z in range(4) for x in range(2)]
+
+
+def over_core(a, what):
+    with jax.named_scope(what):
+        return lax.ppermute(a, "col", CORE)
+
+
+def over_y(a, what):
+    with jax.named_scope(what):
+        return lax.ppermute(a, "col", ACROSS_Y)
+
+
+def over_x(a, what):
+    with jax.named_scope(what):
+        return lax.ppermute(a, "expert", ACROSS_X)
+
+
+def over_z(a, k, what):
+    with jax.named_scope(what):
+        return lax.ppermute(a, "expert", planes_up(k % 4))
+
+
+def by_planes(tokens, routes, route_weight, language, lang_weight, w_gate, w_up, w_down):
+    tok, top = routes.shape
+    experts = w_gate.shape[0] * lax.axis_size("expert")
+    cap = tok * top * 3 // (2 * experts)
+    place = jnp.stack([lax.axis_index("expert"), lax.axis_index("col")]).astype(jnp.int32)
+    lang_row = jnp.pad(lang_weight, (0, -lang_weight.shape[0] % 128))[None, :]
+    n = len(ORDER)
+    half = tok // 2
+    live, metas, parts, back = {}, {}, {}, {}
+    weights = kept = None
+
+    def at(turn):
+        return ORDER[turn] if 0 <= turn < n else None
+
+    for step in range(n + 5):
+        new = {}
+        if step == 0:
+            new["t0"] = tokens
+            info = jnp.concatenate(
+                [routes.T.astype(F32), route_weight.T, language[None, :].astype(F32), jnp.zeros((7, tok), F32)], axis=0
+            )
+            new["info"], new["info_x"] = info, over_x(info, "info_x")
+            new["c0"] = over_core(tokens, "tok_c00")
+        if step == 1:
+            new["info0"] = jnp.stack([live.pop("info"), live.pop("info_x")])
+        if 2 <= step < n + 1:
+            k = ORDER[step - 1]
+            new[f"info{k}"] = over_z(live["info0"], k, f"info_z{k}")
+        if step < n - 1:
+            k = ORDER[step + 1]
+            new[f"t{k}"] = over_z(live["t0"] if step else tokens, k, f"tok_z{k}")
+        k = at(step)
+        if k is not None:
+            source = live[f"t{k}"] if step else tokens
+            new[f"x{k}"], new[f"y{k}"] = over_x(source, f"tok_x{k}"), over_y(source, f"tok_y{k}")
+        k = at(step - 1)
+        if k is not None:
+            three = [live.pop(f"t{k}") if k else tokens, live.pop(f"x{k}"), live.pop(f"y{k}")]
+            if step < n - 1:
+                across = [over_x(three[2][:half], f"tok_dx{k}"), over_y(three[1][half:], f"tok_dy{k}")]
+            else:
+                across = [over_x(three[2], f"tok_dx{k}")]
+            new[f"near{k}"] = three + across
+        k = at(step - 2)
+        if k is not None:
+            near = live.pop(f"near{k}")
+            info = live.pop(f"info{k}") if k else live["info0"]
+            far = [live.pop("c0") if i == 0 and k == 0 else over_core(p, f"tok_c{i}{k}") for i, p in enumerate(near)]
+            new[f"h{k}"], metas[k], *weights = hidden_rows(
+                cap, k == 0, place, lang_row, info, near + far, *(weights or (w_gate, w_up))
+            )
+            weights = weights or kept
+            kept = weights
+        k = at(step - 3)
+        if k is not None:
+            made = live[f"h{k}"]
+            new[f"hy{k}"], new[f"hc{k}"] = over_y(made, f"hid_y{k}"), over_core(made, f"hid_c{k}")
+        k = at(step - 4)
+        if k is not None:
+            pieces = [live.pop(f"{name}{k}") for name in ("h", "hc", "hy")]
+            pieces.append(over_core(pieces[2], f"hid_d{k}"))
+            parts[k], new[f"own{k}"], new[f"other{k}"] = down_rows(cap, place, metas[k], pieces, w_down)
+        k = at(step - 5)
+        if k is not None:
+            new[f"mine{k}"], new[f"met{k}"] = live.pop(f"own{k}"), over_x(live.pop(f"other{k}"), f"sum_x{k}")
+        k = at(step - 6)
+        if k is not None:
+            part = live.pop(f"mine{k}") + live.pop(f"met{k}").astype(F32)
+            back[k] = part if k == 0 else over_z(part.astype(BF16), -k, f"sum_z{k}")
+        if step == n:
+            live.pop("t0"), live.pop("info0")
+        live = lax.optimization_barrier({**live, **new})
+    gram = gram_blocks(cap, place, [metas[k] for k in ORDER], [parts[k] for k in ORDER])
+    k = ORDER[-1]
+    part = (live[f"mine{k}"] + live[f"met{k}"].astype(F32)).astype(BF16)
+    out = sum(back[k].astype(F32) for k in ORDER[:-1])
+    out = out + over_z(part, -k, f"sum_z{k}").astype(F32)
+    return out.astype(BF16), gram
+
+
+def by_rows(tokens, routes, route_weight, language, lang_weight, w_gate, w_up, w_down):
     tok_rows = routes.shape[0]
     top_count = routes.shape[1]
     local_exp = w_gate.shape[0]
@@ -75,6 +404,5 @@
         P("expert", None, "col"),
     )
     out_specs = (P("expert", "col"), P("expert", "col", None))
-    return jax.shard_map(
-        on_device, mesh=mesh, in_specs=in_specs, out_specs=out_specs, check_vma=False
-    )
+    body = by_planes if dict(mesh.shape) == {"expert": 8, "col": 4} else by_rows
+    return jax.shard_map(body, mesh=mesh, in_specs=in_specs, out_specs=out_specs, check_vma=False)

time: 507 us -> 142 us (0.28)
  blocking collectives: 279 us -> 0 us
  waiting for transfers between devices: 94.9 us -> 41.9 us
  Pallas kernels: 0 us -> 44.1 us
  local copies, waits for them, and re-layouts: 45.9 us -> 3.42 us
  starting transfers between devices: 9.22 us -> 44.7 us
  matrix products: 35.4 us -> 0 us
  other arithmetic: 28.5 us -> 3.27 us
  between operations: 14.2 us -> 1.35 us
    all_to_all x1 -> x0, blocking collectives: 279 us -> none  [on_device(): lax.all_to_all(rows.reshape(owners, local_exp, capacity, whole.shape[1]),...]
    all_to_all x2 -> x0, waiting for transfers between devices: 53 us -> none  [the longest x1 53 us: on_device(): lax.all_to_all(expert_out, 'expert', split_axis=1, concat_axis=0, tiled=T...]
    ppermute x0 -> x58, starting transfers between devices: none -> 44.7 us  [the longest x9 16.9 us: over_z(): return lax.ppermute(a, 'expert', planes_up(k % 4))]
    pallas_call x0 -> x9, Pallas kernels: none -> 44.1 us  [the longest x4 27.9 us: hidden_rows(): pl.pallas_call(lambda *a: hidden_kernel(cap, first, *a), out_shape=outs,...]
    gather x5 -> x0, local copies, waits for them, and re-layouts: 43.2 us -> none  [the longest x1 23.4 us: on_device(): rows = jnp.take(whole, flat_token, axis=0)]
    ppermute x0 -> x58, waiting for transfers between devices: none -> 41.9 us  [the longest x13 26.9 us: over_x(): return lax.ppermute(a, 'expert', ACROSS_X)]
    all_gather x2 -> x0, waiting for transfers between devices: 41.1 us -> none  [the longest x1 22.1 us: on_device(): piece = lax.all_gather(hidden, 'col', axis=3, tiled=True)]
    dot_general x4 -> x0, matrix products: 35.4 us -> none  [the longest x1 10 us: on_device(): jnp.einsum('seck,efk->escf', arrived, w_up, preferred_element_type=jnp.fl...]
  transfers between devices with their start and end apart: 4 -> 58, of which waited for: 3 -> 14; matrix products, arithmetic and copies ran while one was open for 8% -> 2% of each run, Pallas kernels for 0% -> 32%
where the time goes in v2:
time: 142 us; the launch traced here: 139 us
  starting transfers between devices  44.7 us (31%)
  Pallas kernels  44.1 us (31%)
  waiting for transfers between devices  41.9 us (30%)
  local copies, waits for them, and re-layouts  3.42 us (2%)
  other arithmetic  3.27 us (2%)
    pallas_call x4, Pallas kernels, hidden_rows(): pl.pallas_call(lambda *a: hidden_kernel(cap, first, *a), out_shape=outs,...  27.9 us
    ppermute x13, waiting for transfers between devices, over_x(): return lax.ppermute(a, 'expert', ACROSS_X)  26.9 us
    ppermute x9, starting transfers between devices, over_z(): return lax.ppermute(a, 'expert', planes_up(k % 4))  16.9 us
    ppermute x9, waiting for transfers between devices, over_z(): return lax.ppermute(a, 'expert', planes_up(k % 4))  13.1 us
    ppermute x13, starting transfers between devices, over_x(): return lax.ppermute(a, 'expert', ACROSS_X)  12 us
    ppermute x10, starting transfers between devices, over_y(): return lax.ppermute(a, 'col', ACROSS_Y)  11.2 us
    pallas_call x4, Pallas kernels, down_rows(): pl.pallas_call(lambda *a: down_kernel(cap, *a), out_shape=(pltpu.VMEM((ex...  10.6 us
    pallas_call x1, Pallas kernels, gram_blocks(): pl.pallas_call(lambda *a: gram_kernel(cap, *a), out_shape=jax.ShapeDtypeS...  5.68 us
  transfers between devices with their start and end apart: 58, of which 14 were waited for; matrix products, arithmetic and copies ran while one was open for 2% of the time, Pallas kernels for 32%

profile of v2, /device:TPU:0, one launch (start us, length us, event | category | flops | bytes accessed | tf_op | source)
XLA Modules:
  0.0 138.7 jit_solution(152726262776865439)
XLA Ops:
  0.6 3.0 %collective-permute-start.4 = (bf16[128,1024]{1,0:T(8,128)(2,1)}, bf16[128,1024]{1,0:T(8,128)(2,1)S(1)}, u32[]{:S(2)}, u32[]{:S(2)}) collective-permute-start(bf16[128,1024]{1,0:T(8,128)(2,1)} %a_3_), channel_id=1, source_target_pairs={{0,2},{1,3},{2,0},{3,1},{4,6},{5,7},{6,4},{7,5},{8,10},{9,11},{10,... | collective-permute-start | bytes 786440 | tf_op jit(solution)/shard_map/tok_y0/ppermute | solution.py:243
  5.2 3.6 %collective-permute-start.2 = (bf16[128,1024]{1,0:T(8,128)(2,1)}, bf16[128,1024]{1,0:T(8,128)(2,1)S(1)}, u32[]{:S(2)}, u32[]{:S(2)}) collective-permute-start(bf16[128,1024]{1,0:T(8,128)(2,1)} %a_3_), channel_id=1, source_target_pairs={{8,0},{12,4},{16,8},{20,12},{24,16},{28,20},{0,24},{4,28},{9,1},{1... | collective-permute-start | bytes 786440 | tf_op jit(solution)/shard_map/tok_z1/ppermute | solution.py:253
  11.5 3.2 %collective-permute-done.1 = f32[24,128]{1,0:T(8,128)S(1)} collective-permute-done((f32[24,128]{1,0:T(8,128)S(1)}, f32[24,128]{1,0:T(8,128)S(1)}, u32[]{:S(2)}, u32[]{:S(2)}) %collective-permute-start.1) | collective-permute-done | bytes 12320 | tf_op jit(solution)/shard_map/info_x/ppermute | solution.py:248
  19.7 5.8 %collective-permute-done.5.a_6_ = bf16[64,1024]{1,0:T(8,128)(2,1)S(1)} collective-permute-done((bf16[64,1024]{1,0:T(8,128)(2,1)S(1)}, bf16[64,1024]{1,0:T(8,128)(2,1)S(1)}, u32[]{:S(2)}, u32[]{:S(2)}) %collective-permute-start.5) | collective-permute-done | bytes 131104 | tf_op jit(solution)/shard_map/tok_dx0/ppermute | solution.py:248
  25.5 3.5 %collective-permute-done.7.a_3_ = bf16[128,1024]{1,0:T(8,128)(2,1)S(1)} collective-permute-done((bf16[128,1024]{1,0:T(8,128)(2,1)}, bf16[128,1024]{1,0:T(8,128)(2,1)S(1)}, u32[]{:S(2)}, u32[]{:S(2)}) %collective-permute-start.7) | collective-permute-done | bytes 262176 | tf_op jit(solution)/shard_map/tok_z2/ppermute | solution.py:253
  32.1 2.4 %collective-permute-done.14.a_2_ = f32[2,24,128]{2,1,0:T(8,128)S(1)} collective-permute-done((f32[2,24,128]{2,1,0:T(8,128)S(1)}, f32[2,24,128]{2,1,0:T(8,128)S(1)}, u32[]{:S(2)}, u32[]{:S(2)}) %collective-permute-start.14) | collective-permute-done | bytes 24608 | tf_op jit(solution)/shard_map/info_z1/ppermute | solution.py:253
  39.3 9.8 %shard_map.95 = (bf16[2,192,384]{2,1,0:T(8,128)(2,1)S(1)}, f32[2,8,128]{2,1,0:T(8,128)S(1)}, bf16[2,384,4096]{2,1,0:T(8,128)(2,1)S(1)}, bf16[2,384,4096]{2,1,0:T(8,128)(2,1)S(1)}) custom-call(s32[2]{0:T(128)S(1)} %pad_add_fusion.a_0_, f32[1,128]{1,0:T(1,128)S(1)} %pad_bitcast_fusion.a_1_, f32[2,24,128]{2,1,0:T(8,128)S(1)} %pad_maximum_fusion.a_2_, ...), custom_call_target="tpu_custom_call" | custom-call | flops 3221225472 | tf_op jit(solution)/shard_map/pallas_call | solution.py:110
  50.0 3.0 %collective-permute-start.27 = (f32[2,24,128]{2,1,0:T(8,128)S(1)}, f32[2,24,128]{2,1,0:T(8,128)S(1)}, u32[]{:S(2)}, u32[]{:S(2)}) collective-permute-start(f32[2,24,128]{2,1,0:T(8,128)S(1)} %pad_maximum_fusion.a_2_), channel_id=1, source_target_pairs={{16,0},{20,4},{24,8},{28,12},{0,16},{4,20},{8,24},{12,28},{17,1},{... | collective-permute-start | bytes 73736 | tf_op jit(solution)/shard_map/info_z2/ppermute | solution.py:253
  53.1 2.2 %collective-permute-done.27.a_2_ = f32[2,24,128]{2,1,0:T(8,128)S(1)} collective-permute-done((f32[2,24,128]{2,1,0:T(8,128)S(1)}, f32[2,24,128]{2,1,0:T(8,128)S(1)}, u32[]{:S(2)}, u32[]{:S(2)}) %collective-permute-start.27) | collective-permute-done | bytes 24608 | tf_op jit(solution)/shard_map/info_z2/ppermute | solution.py:253
  59.6 6.0 %shard_map.96 = (bf16[2,192,384]{2,1,0:T(8,128)(2,1)S(1)}, f32[2,8,128]{2,1,0:T(8,128)S(1)}) custom-call(s32[2]{0:T(128)S(1)} %pad_add_fusion.a_0_, f32[1,128]{1,0:T(1,128)S(1)} %pad_bitcast_fusion.a_1_, f32[2,24,128]{2,1,0:T(8,128)S(1)} %collective-permute-done.14.a_2_, bf16[128,1024]{1,0:T(8,128)(2,1)} %copy-done.6, bf16[128,1024]{1,0:T(8,128)(2,1)} %copy-done.1, ...), custom_call_target="tpu_custom_call" | custom-call | flops 3221225472 | tf_op jit(solution)/shard_map/pallas_call | solution.py:110
  65.6 5.0 %collective-permute-done.28.a_6_ = bf16[128,1024]{1,0:T(8,128)(2,1)S(1)} collective-permute-done((bf16[128,1024]{1,0:T(8,128)(2,1)S(1)}, bf16[128,1024]{1,0:T(8,128)(2,1)S(1)}, u32[]{:S(2)}, u32[]{:S(2)}) %collective-permute-start.28) | collective-permute-done | bytes 262176 | tf_op jit(solution)/shard_map/tok_dx2/ppermute | solution.py:248
  74.4 6.0 %shard_map.97 = (bf16[2,192,384]{2,1,0:T(8,128)(2,1)S(1)}, f32[2,8,128]{2,1,0:T(8,128)S(1)}) custom-call(s32[2]{0:T(128)S(1)} %pad_add_fusion.a_0_, f32[1,128]{1,0:T(1,128)S(1)} %pad_bitcast_fusion.a_1_, f32[2,24,128]{2,1,0:T(8,128)S(1)} %collective-permute-done.27.a_2_, bf16[128,1024]{1,0:T(8,128)(2,1)} %copy-done.4, bf16[128,1024]{1,0:T(8,128)(2,1)} %copy-done.8, ...), custom_call_target="tpu_custom_call" | custom-call | flops 3221225472 | tf_op jit(solution)/shard_map/pallas_call | solution.py:110
  80.4 2.6 %shard_map.98 = (bf16[2,192,1536]{2,1,0:T(8,128)(2,1)S(1)}, f32[128,1024]{1,0:T(8,128)S(1)}, bf16[128,1024]{1,0:T(8,128)(2,1)S(1)}) custom-call(s32[2]{0:T(128)S(1)} %pad_add_fusion.a_0_, f32[2,8,128]{2,1,0:T(8,128)S(1)} %get-tuple-element.146.a_1_, bf16[2,192,384]{2,1,0:T(8,128)(2,1)S(1)} %get-tuple-element.147.a_2_, ...), custom_call_target="tpu_custom_call" | custom-call | flops 1207959552 | tf_op jit(solution)/shard_map/pallas_call | solution.py:155
  88.5 6.0 %shard_map.99 = (bf16[2,192,384]{2,1,0:T(8,128)(2,1)S(1)}, f32[2,8,128]{2,1,0:T(8,128)S(1)}) custom-call(s32[2]{0:T(128)S(1)} %pad_add_fusion.a_0_, f32[1,128]{1,0:T(1,128)S(1)} %pad_bitcast_fusion.a_1_, f32[2,24,128]{2,1,0:T(8,128)S(1)} %collective-permute-done.37.a_2_, bf16[128,1024]{1,0:T(8,128)(2,1)} %copy-done.5, bf16[128,1024]{1,0:T(8,128)(2,1)} %copy-done.10, ...), custom_call_target="tpu_custom_call" | custom-call | flops 3221225472 | tf_op jit(solution)/shard_map/pallas_call | solution.py:110
  94.5 2.6 %shard_map.100 = (bf16[2,192,1536]{2,1,0:T(8,128)(2,1)S(1)}, f32[128,1024]{1,0:T(8,128)S(1)}, bf16[128,1024]{1,0:T(8,128)(2,1)S(1)}) custom-call(s32[2]{0:T(128)S(1)} %pad_add_fusion.a_0_, f32[2,8,128]{2,1,0:T(8,128)S(1)} %get-tuple-element.161.a_1_.a_2_, bf16[2,192,384]{2,1,0:T(8,128)(2,1)S(1)} %get-tuple-element.162.a_2_, ...), custom_call_target="tpu_custom_call" | custom-call | flops 1207959552 | tf_op jit(solution)/shard_map/pallas_call | solution.py:155
  98.9 2.7 %shard_map.101 = (bf16[2,192,1536]{2,1,0:T(8,128)(2,1)S(1)}, f32[128,1024]{1,0:T(8,128)S(1)}, bf16[128,1024]{1,0:T(8,128)(2,1)S(1)}) custom-call(s32[2]{0:T(128)S(1)} %pad_add_fusion.a_0_, f32[2,8,128]{2,1,0:T(8,128)S(1)} %get-tuple-element.172.a_1_.a_3_, bf16[2,192,384]{2,1,0:T(8,128)(2,1)S(1)} %get-tuple-element.173.a_2_, ...), custom_call_target="tpu_custom_call" | custom-call | flops 1207959552 | tf_op jit(solution)/shard_map/pallas_call | solution.py:155
  101.5 5.4 %collective-permute-done.50 = bf16[128,1024]{1,0:T(8,128)(2,1)S(1)} collective-permute-done((bf16[128,1024]{1,0:T(8,128)(2,1)S(1)}, bf16[128,1024]{1,0:T(8,128)(2,1)S(1)}, u32[]{:S(2)}, u32[]{:S(2)}) %collective-permute-start.50) | collective-permute-done | bytes 262176 | tf_op jit(solution)/shard_map/sum_x1/ppermute | solution.py:248
  108.5 2.6 %shard_map.102 = (bf16[2,192,1536]{2,1,0:T(8,128)(2,1)S(1)}, f32[128,1024]{1,0:T(8,128)S(1)}, bf16[128,1024]{1,0:T(8,128)(2,1)S(1)}) custom-call(s32[2]{0:T(128)S(1)} %pad_add_fusion.a_0_, f32[2,8,128]{2,1,0:T(8,128)S(1)} %get-tuple-element.182.a_1_.a_4_, bf16[2,192,384]{2,1,0:T(8,128)(2,1)S(1)} %get-tuple-element.183.a_2_, ...), custom_call_target="tpu_custom_call" | custom-call | flops 1207959552 | tf_op jit(solution)/shard_map/pallas_call | solution.py:155
  111.1 4.5 %collective-permute-done.53 = bf16[128,1024]{1,0:T(8,128)(2,1)S(1)} collective-permute-done((bf16[128,1024]{1,0:T(8,128)(2,1)S(1)}, bf16[128,1024]{1,0:T(8,128)(2,1)S(1)}, u32[]{:S(2)}, u32[]{:S(2)}) %collective-permute-start.53) | collective-permute-done | bytes 262176 | tf_op jit(solution)/shard_map/sum_x2/ppermute | solution.py:248
  116.3 2.7 %collective-permute-start.52 = (bf16[128,1024]{1,0:T(8,128)(2,1)S(1)}, bf16[128,1024]{1,0:T(8,128)(2,1)S(1)}, u32[]{:S(2)}, u32[]{:S(2)}) collective-permute-start(bf16[128,1024]{1,0:T(8,128)(2,1)S(1)} %add_convert_fusion.3), channel_id=1, source_target_pairs={{24,0},{28,4},{0,8},{4,12},{8,16},{12,20},{16,24},{20,28},{25,1},{... | collective-permute-start | bytes 786440 | tf_op jit(solution)/shard_map/sum_z1/ppermute | solution.py:253
  120.5 3.0 %collective-permute-done.56 = bf16[128,1024]{1,0:T(8,128)(2,1)S(1)} collective-permute-done((bf16[128,1024]{1,0:T(8,128)(2,1)S(1)}, bf16[128,1024]{1,0:T(8,128)(2,1)S(1)}, u32[]{:S(2)}, u32[]{:S(2)}) %collective-permute-start.56) | collective-permute-done | bytes 262176 | tf_op jit(solution)/shard_map/sum_x3/ppermute | solution.py:248
  123.6 3.6 %collective-permute-start.57 = (bf16[128,1024]{1,0:T(8,128)(2,1)S(1)}, bf16[128,1024]{1,0:T(8,128)(2,1)S(1)}, u32[]{:S(2)}, u32[]{:S(2)}) collective-permute-start(bf16[128,1024]{1,0:T(8,128)(2,1)S(1)} %add_convert_fusion.1), channel_id=1, source_target_pairs={{8,0},{12,4},{16,8},{20,12},{24,16},{28,20},{0,24},{4,28},{9,1},{1... | collective-permute-start | bytes 786440 | tf_op jit(solution)/shard_map/sum_z3/ppermute | solution.py:253
  127.1 5.7 %shard_map.103 = f32[2,384,1536]{2,1,0:T(8,128)} custom-call(s32[2]{0:T(128)S(1)} %pad_add_fusion.a_0_, f32[2,8,128]{2,1,0:T(8,128)S(1)} %get-tuple-element.146.a_1_, f32[2,8,128]{2,1,0:T(8,128)S(1)} %get-tuple-element.161.a_1_.a_2_, f32[2,8,128]{2,1,0:T(8,128)S(1)} %get-tuple-element.172.a_1_.a_3_, f32[2,8,128]{2,1,0:T(8,128)S(1)} %get-tuple-element.182.a_1_.a_4_, ...), custom_call_target="tpu_custom_call" | custom-call | flops 1811939328 | bytes 4718592 | tf_op jit(solution)/shard_map/pallas_call | solution.py:209
  132.8 4.2 %collective-permute-done.55 = bf16[128,1024]{1,0:T(8,128)(2,1)S(1)} collective-permute-done((bf16[128,1024]{1,0:T(8,128)(2,1)S(1)}, bf16[128,1024]{1,0:T(8,128)(2,1)S(1)}, u32[]{:S(2)}, u32[]{:S(2)}) %collective-permute-start.55) | collective-permute-done | bytes 262176 | tf_op jit(solution)/shard_map/sum_z2/ppermute | solution.py:253
  (192 shorter events, 38.2 us)
Async XLA Ops:
  0.6 14.0 %collective-permute-start.4 = (bf16[128,1024]{1,0:T(8,128)(2,1)}, bf16[128,1024]{1,0:T(8,128)(2,1)S(1)}, u32[]{:S(2)}, u32[]{:S(2)}) collective-permute-start(bf16[128,1024]{1,0:T(8,128)(2,1)} %a_3_), channel_id=1, source_target_pairs={{0,2},{1,3},{2,0},{3,1},{4,6},{5,7},{6,4},{7,5},{8,10},{9,11},{10,... | collective-permute-start | bytes 786440 | tf_op jit(solution)/shard_map/tok_y0/ppermute | solution.py:243
  3.7 11.0 %collective-permute-start.3 = (bf16[128,1024]{1,0:T(8,128)(2,1)}, bf16[128,1024]{1,0:T(8,128)(2,1)S(1)}, u32[]{:S(2)}, u32[]{:S(2)}) collective-permute-start(bf16[128,1024]{1,0:T(8,128)(2,1)} %a_3_), channel_id=1, source_target_pairs={{0,4},{4,0},{8,12},{12,8},{16,20},{20,16},{24,28},{28,24},{1,5},{5... | collective-permute-start | bytes 786440 | tf_op jit(solution)/shard_map/tok_x0/ppermute | solution.py:248
  14.7 14.3 %collective-permute-start.7 = (bf16[128,1024]{1,0:T(8,128)(2,1)}, bf16[128,1024]{1,0:T(8,128)(2,1)S(1)}, u32[]{:S(2)}, u32[]{:S(2)}) collective-permute-start(bf16[128,1024]{1,0:T(8,128)(2,1)} %a_3_), channel_id=1, source_target_pairs={{16,0},{20,4},{24,8},{28,12},{0,16},{4,20},{8,24},{12,28},{17,1},{... | collective-permute-start | bytes 786440 | tf_op jit(solution)/shard_map/tok_z2/ppermute | solution.py:253
  15.5 13.5 %collective-permute-start.9 = (bf16[128,1024]{1,0:T(8,128)(2,1)S(1)}, bf16[128,1024]{1,0:T(8,128)(2,1)S(1)}, u32[]{:S(2)}, u32[]{:S(2)}) collective-permute-start(bf16[128,1024]{1,0:T(8,128)(2,1)S(1)} %collective-permute-done.2.a_3_), channel_id=1, source_target_pairs={{0,2},{1,3},{2,0},{3,1},{4,6},{5,7},{6,4},{7,5},{8,10},{9,11},{10,... | collective-permute-start | bytes 786440 | tf_op jit(solution)/shard_map/tok_y1/ppermute | solution.py:243
  16.0 13.0 %collective-permute-start.8 = (bf16[128,1024]{1,0:T(8,128)(2,1)S(1)}, bf16[128,1024]{1,0:T(8,128)(2,1)S(1)}, u32[]{:S(2)}, u32[]{:S(2)}) collective-permute-start(bf16[128,1024]{1,0:T(8,128)(2,1)S(1)} %collective-permute-done.2.a_3_), channel_id=1, source_target_pairs={{0,4},{4,0},{8,12},{12,8},{16,20},{20,16},{24,28},{28,24},{1,5},{5... | collective-permute-start | bytes 786440 | tf_op jit(solution)/shard_map/tok_x1/ppermute | solution.py:248
  34.6 14.7 %collective-permute-start.19 = (bf16[128,1024]{1,0:T(8,128)(2,1)S(1)}, bf16[128,1024]{1,0:T(8,128)(2,1)S(1)}, u32[]{:S(2)}, u32[]{:S(2)}) collective-permute-start(bf16[128,1024]{1,0:T(8,128)(2,1)S(1)} %collective-permute-done.7.a_3_), channel_id=1, source_target_pairs={{0,2},{1,3},{2,0},{3,1},{4,6},{5,7},{6,4},{7,5},{8,10},{9,11},{10,... | collective-permute-start | bytes 786440 | tf_op jit(solution)/shard_map/tok_y2/ppermute | solution.py:243
  35.1 14.2 %collective-permute-start.18 = (bf16[128,1024]{1,0:T(8,128)(2,1)S(1)}, bf16[128,1024]{1,0:T(8,128)(2,1)S(1)}, u32[]{:S(2)}, u32[]{:S(2)}) collective-permute-start(bf16[128,1024]{1,0:T(8,128)(2,1)S(1)} %collective-permute-done.7.a_3_), channel_id=1, source_target_pairs={{0,4},{4,0},{8,12},{12,8},{16,20},{20,16},{24,28},{28,24},{1,5},{5... | collective-permute-start | bytes 786440 | tf_op jit(solution)/shard_map/tok_x2/ppermute | solution.py:248
  35.6 13.6 %collective-permute-start.15 = (bf16[64,1024]{1,0:T(8,128)(2,1)S(1)}, bf16[64,1024]{1,0:T(8,128)(2,1)S(1)}, u32[]{:S(2)}, u32[]{:S(2)}) collective-permute-start(bf16[64,1024]{1,0:T(8,128)(2,1)S(1)} %slice.14), channel_id=1, source_target_pairs={{0,4},{4,0},{8,12},{12,8},{16,20},{20,16},{24,28},{28,24},{1,5},{5... | collective-permute-start | bytes 393224 | tf_op jit(solution)/shard_map/tok_dx1/ppermute | solution.py:248
  37.1 12.1 %collective-permute-start.16 = (bf16[64,1024]{1,0:T(8,128)(2,1)S(1)}, bf16[64,1024]{1,0:T(8,128)(2,1)S(1)}, u32[]{:S(2)}, u32[]{:S(2)}) collective-permute-start(bf16[64,1024]{1,0:T(8,128)(2,1)S(1)} %slice.15), channel_id=1, source_target_pairs={{0,2},{1,3},{2,0},{3,1},{4,6},{5,7},{6,4},{7,5},{8,10},{9,11},{10,... | collective-permute-start | bytes 393224 | tf_op jit(solution)/shard_map/tok_dy1/ppermute | solution.py:243
  38.6 10.6 %collective-permute-start.17 = (bf16[128,1024]{1,0:T(8,128)(2,1)}, bf16[128,1024]{1,0:T(8,128)(2,1)S(1)}, u32[]{:S(2)}, u32[]{:S(2)}) collective-permute-start(bf16[128,1024]{1,0:T(8,128)(2,1)} %a_3_), channel_id=1, source_target_pairs={{24,0},{28,4},{0,8},{4,12},{8,16},{12,20},{16,24},{20,28},{25,1},{... | collective-permute-start | bytes 786440 | tf_op jit(solution)/shard_map/tok_z3/ppermute | solution.py:253
  55.3 15.3 %collective-permute-start.30 = (bf16[128,1024]{1,0:T(8,128)(2,1)S(1)}, bf16[128,1024]{1,0:T(8,128)(2,1)S(1)}, u32[]{:S(2)}, u32[]{:S(2)}) collective-permute-start(bf16[128,1024]{1,0:T(8,128)(2,1)S(1)} %collective-permute-done.17.a_3_), channel_id=1, source_target_pairs={{0,2},{1,3},{2,0},{3,1},{4,6},{5,7},{6,4},{7,5},{8,10},{9,11},{10,... | collective-permute-start | bytes 786440 | tf_op jit(solution)/shard_map/tok_y3/ppermute | solution.py:243
  56.6 14.0 %collective-permute-start.29 = (bf16[128,1024]{1,0:T(8,128)(2,1)S(1)}, bf16[128,1024]{1,0:T(8,128)(2,1)S(1)}, u32[]{:S(2)}, u32[]{:S(2)}) collective-permute-start(bf16[128,1024]{1,0:T(8,128)(2,1)S(1)} %collective-permute-done.17.a_3_), channel_id=1, source_target_pairs={{0,4},{4,0},{8,12},{12,8},{16,20},{20,16},{24,28},{28,24},{1,5},{5... | collective-permute-start | bytes 786440 | tf_op jit(solution)/shard_map/tok_x3/ppermute | solution.py:248
  57.2 13.5 %collective-permute-start.26 = (bf16[2,192,384]{2,1,0:T(8,128)(2,1)S(1)}, bf16[2,192,384]{2,1,0:T(8,128)(2,1)S(1)}, u32[]{:S(2)}, u32[]{:S(2)}) collective-permute-start(bf16[2,192,384]{2,1,0:T(8,128)(2,1)S(1)} %get-tuple-element.147.a_2_), channel_id=1, source_target_pairs={{0,2},{1,3},{2,0},{3,1},{4,6},{5,7},{6,4},{7,5},{8,10},{9,11},{10,... | collective-permute-start | bytes 884744 | tf_op jit(solution)/shard_map/hid_y0/ppermute | solution.py:243
  58.0 12.7 %collective-permute-start.25 = (bf16[2,192,384]{2,1,0:T(8,128)(2,1)S(1)}, bf16[2,192,384]{2,1,0:T(8,128)(2,1)S(1)}, u32[]{:S(2)}, u32[]{:S(2)}) collective-permute-start(bf16[2,192,384]{2,1,0:T(8,128)(2,1)S(1)} %get-tuple-element.147.a_2_), channel_id=1, source_target_pairs={{0,1},{1,0},{2,3},{3,2},{4,5},{5,4},{6,7},{7,6},{8,9},{9,8},{10,11... | collective-permute-start | bytes 884744 | tf_op jit(solution)/shard_map/hid_c0/ppermute | solution.py:238
  58.0 12.6 %collective-permute-start.28 = (bf16[128,1024]{1,0:T(8,128)(2,1)S(1)}, bf16[128,1024]{1,0:T(8,128)(2,1)S(1)}, u32[]{:S(2)}, u32[]{:S(2)}) collective-permute-start(bf16[128,1024]{1,0:T(8,128)(2,1)S(1)} %collective-permute-done.19.a_5_), channel_id=1, source_target_pairs={{0,4},{4,0},{8,12},{12,8},{16,20},{20,16},{24,28},{28,24},{1,5},{5... | collective-permute-start | bytes 786440 | tf_op jit(solution)/shard_map/tok_dx2/ppermute | solution.py:248
  71.8 11.3 %collective-permute-start.36 = (bf16[2,192,384]{2,1,0:T(8,128)(2,1)S(1)}, bf16[2,192,384]{2,1,0:T(8,128)(2,1)S(1)}, u32[]{:S(2)}, u32[]{:S(2)}) collective-permute-start(bf16[2,192,384]{2,1,0:T(8,128)(2,1)S(1)} %get-tuple-element.162.a_2_), channel_id=1, source_target_pairs={{0,2},{1,3},{2,0},{3,1},{4,6},{5,7},{6,4},{7,5},{8,10},{9,11},{10,... | collective-permute-start | bytes 884744 | tf_op jit(solution)/shard_map/hid_y1/ppermute | solution.py:243
  72.6 10.6 %collective-permute-start.35 = (bf16[2,192,384]{2,1,0:T(8,128)(2,1)S(1)}, bf16[2,192,384]{2,1,0:T(8,128)(2,1)S(1)}, u32[]{:S(2)}, u32[]{:S(2)}) collective-permute-start(bf16[2,192,384]{2,1,0:T(8,128)(2,1)S(1)} %get-tuple-element.162.a_2_), channel_id=1, source_target_pairs={{0,1},{1,0},{2,3},{3,2},{4,5},{5,4},{6,7},{7,6},{8,9},{9,8},{10,11... | collective-permute-start | bytes 884744 | tf_op jit(solution)/shard_map/hid_c1/ppermute | solution.py:238
  72.7 10.4 %collective-permute-start.37 = (f32[2,24,128]{2,1,0:T(8,128)S(1)}, f32[2,24,128]{2,1,0:T(8,128)S(1)}, u32[]{:S(2)}, u32[]{:S(2)}) collective-permute-start(f32[2,24,128]{2,1,0:T(8,128)S(1)} %pad_maximum_fusion.a_2_), channel_id=1, source_target_pairs={{24,0},{28,4},{0,8},{4,12},{8,16},{12,20},{16,24},{20,28},{25,1},{... | collective-permute-start | bytes 73736 | tf_op jit(solution)/shard_map/info_z3/ppermute | solution.py:253
  84.2 12.9 %collective-permute-start.45 = (bf16[2,192,384]{2,1,0:T(8,128)(2,1)S(1)}, bf16[2,192,384]{2,1,0:T(8,128)(2,1)S(1)}, u32[]{:S(2)}, u32[]{:S(2)}) collective-permute-start(bf16[2,192,384]{2,1,0:T(8,128)(2,1)S(1)} %get-tuple-element.173.a_2_), channel_id=1, source_target_pairs={{0,2},{1,3},{2,0},{3,1},{4,6},{5,7},{6,4},{7,5},{8,10},{9,11},{10,... | collective-permute-start | bytes 884744 | tf_op jit(solution)/shard_map/hid_y2/ppermute | solution.py:243
  85.5 11.7 %collective-permute-start.44 = (bf16[2,192,384]{2,1,0:T(8,128)(2,1)S(1)}, bf16[2,192,384]{2,1,0:T(8,128)(2,1)S(1)}, u32[]{:S(2)}, u32[]{:S(2)}) collective-permute-start(bf16[2,192,384]{2,1,0:T(8,128)(2,1)S(1)} %get-tuple-element.173.a_2_), channel_id=1, source_target_pairs={{0,1},{1,0},{2,3},{3,2},{4,5},{5,4},{6,7},{7,6},{8,9},{9,8},{10,11... | collective-permute-start | bytes 884744 | tf_op jit(solution)/shard_map/hid_c2/ppermute | solution.py:238
  85.5 11.6 %collective-permute-start.46 = (bf16[128,1024]{1,0:T(8,128)(2,1)S(1)}, bf16[128,1024]{1,0:T(8,128)(2,1)S(1)}, u32[]{:S(2)}, u32[]{:S(2)}) collective-permute-start(bf16[128,1024]{1,0:T(8,128)(2,1)S(1)} %get-tuple-element.159), channel_id=1, source_target_pairs={{0,4},{4,0},{8,12},{12,8},{16,20},{20,16},{24,28},{28,24},{1,5},{5... | collective-permute-start | bytes 786440 | tf_op jit(solution)/shard_map/sum_x0/ppermute | solution.py:248
  116.3 16.6 %collective-permute-start.52 = (bf16[128,1024]{1,0:T(8,128)(2,1)S(1)}, bf16[128,1024]{1,0:T(8,128)(2,1)S(1)}, u32[]{:S(2)}, u32[]{:S(2)}) collective-permute-start(bf16[128,1024]{1,0:T(8,128)(2,1)S(1)} %add_convert_fusion.3), channel_id=1, source_target_pairs={{24,0},{28,4},{0,8},{4,12},{8,16},{12,20},{16,24},{20,28},{25,1},{... | collective-permute-start | bytes 786440 | tf_op jit(solution)/shard_map/sum_z1/ppermute | solution.py:253
  119.0 18.1 %collective-permute-start.55 = (bf16[128,1024]{1,0:T(8,128)(2,1)S(1)}, bf16[128,1024]{1,0:T(8,128)(2,1)S(1)}, u32[]{:S(2)}, u32[]{:S(2)}) collective-permute-start(bf16[128,1024]{1,0:T(8,128)(2,1)S(1)} %add_convert_fusion.2), channel_id=1, source_target_pairs={{16,0},{20,4},{24,8},{28,12},{0,16},{4,20},{8,24},{12,28},{17,1},{... | collective-permute-start | bytes 786440 | tf_op jit(solution)/shard_map/sum_z2/ppermute | solution.py:253
  123.6 14.2 %collective-permute-start.57 = (bf16[128,1024]{1,0:T(8,128)(2,1)S(1)}, bf16[128,1024]{1,0:T(8,128)(2,1)S(1)}, u32[]{:S(2)}, u32[]{:S(2)}) collective-permute-start(bf16[128,1024]{1,0:T(8,128)(2,1)S(1)} %add_convert_fusion.1), channel_id=1, source_target_pairs={{8,0},{12,4},{16,8},{20,12},{24,16},{28,20},{0,24},{4,28},{9,1},{1... | collective-permute-start | bytes 786440 | tf_op jit(solution)/shard_map/sum_z3/ppermute | solution.py:253
  (71 other events, 588.7 us)

commit v3 on v2

--- a/solution.py
+++ b/solution.py
@@ -7,7 +7,7 @@
 
 F32 = jnp.float32
 BF16 = jnp.bfloat16
-ORDER = (0, 1, 2, 3)
+ORDER = (0, 3, 2, 1)
 
 
 def whole(shape):
@@ -20,8 +20,35 @@
 HBM = pl.BlockSpec(memory_space=pltpu.HBM)
 
 
+def pack_kernel(tokens, routes, weight, language, out, sem):
+    top, tok = routes.shape
+    copy = pltpu.make_async_copy(tokens, out.at[pl.ds(0, tok)], sem)
+    copy.start()
+    out[tok:, :] = jnp.zeros((out.shape[0] - tok, out.shape[1]), BF16)
+    out[tok : tok + top, 0:tok] = routes[...].astype(F32).astype(BF16)
+    left = weight[...]
+    for i in range(1, 4):
+        part = left.astype(BF16)
+        out[tok : tok + top, i * tok : (i + 1) * tok] = part
+        left = left - part.astype(F32)
+    out[tok : tok + 1, 4 * tok : 5 * tok] = language[...].astype(F32).astype(BF16)
+    copy.wait()
+
+
+def pack_tokens(tokens, routes, route_weight, language):
+    tok, feat = tokens.shape
+    return pl.pallas_call(
+        pack_kernel,
+        out_shape=pltpu.VMEM((tok + 16, feat), BF16),
+        in_specs=[HBM, VMEM, VMEM, VMEM],
+        out_specs=VMEM,
+        scratch_shapes=[pltpu.SemaphoreType.DMA],
+    )(in_hbm(tokens), routes.T, route_weight.T, language[None, :])
+
+
 def fill_routes(place, lang_w, info, meta):
-    tok = info.shape[2]
+    tok = meta.shape[2]
+    top = 8
     lower = (
         lax.broadcasted_iota(jnp.int32, (tok, tok), 0)
         < lax.broadcasted_iota(jnp.int32, (tok, tok), 1)
@@ -30,7 +57,9 @@
     lang_column = jnp.broadcast_to(lang_w[...], (tok, lang_w.shape[1])).T
     meta[...] = jnp.zeros_like(meta)
     for b in range(2):
-        routes, weight, lang = info[b, 0:8, :], info[b, 8:16, :], info[b, 16:17, :]
+        block = info[b].astype(F32)
+        routes, lang = block[0:top, 0:tok], block[0:1, 4 * tok : 5 * tok]
+        weight = sum(block[0:top, i * tok : (i + 1) * tok] for i in (1, 2, 3))
         hits = []
         for i in range(2):
             mine = routes == (place[0] * 2 + i).astype(F32)
@@ -56,11 +85,11 @@
     return pltpu.with_memory_space_constraint(a, pltpu.VMEM)
 
 
-def hidden_kernel(cap, first, place, lang_w, info, *refs):
+def hidden_kernel(cap, first, place, lang_w, *refs):
     if first:
-        pieces, (w_gate, w_up, out, meta, gate_held, up_held, x, sems, weight_sems) = refs[:-9], refs[-9:]
+        pieces, (w_gate, w_up, out, meta, gate_held, up_held, x, info, sems, weight_sems) = refs[:-10], refs[-10:]
     else:
-        pieces, (gate_held, up_held, out, meta, x, sems) = refs[:-6], refs[-6:]
+        pieces, (gate_held, up_held, out, meta, x, info, sems) = refs[:-7], refs[-7:]
     tok = meta.shape[2]
     feat = x.shape[1] // 4
     half = len(pieces) // 2
@@ -70,6 +99,8 @@
         row = 0
         for i in range(half):
             src = pieces[core * half + i]
+            if src.shape[0] > tok:
+                src = src.at[pl.ds(0, tok)]
             b, y = ((0, 0), (1, 0), (0, 1))[i] if i < 3 else (1, 1)
             at = pl.multiple_of((place[1] ^ (core + 2 * y)) * feat, feat)
             dst = x.at[pl.ds(b * tok + row, src.shape[0]), pl.ds(at, feat)]
@@ -81,14 +112,18 @@
             copies += [
                 pltpu.make_async_copy(src.at[e], dst.at[e], weight_sems.at[2 * e + i]) for e in range(experts)
             ]
-    for copy in copies:
+    routes = [
+        pltpu.make_async_copy(pieces[b].at[pl.ds(tok, 16)], info.at[b], sems.at[len(pieces) + b]) for b in range(2)
+    ]
+    for copy in routes + copies:
         copy.start()
-    fill_routes(place, lang_w, info, meta)
-    for copy in copies:
+    for copy in routes + copies:
         copy.wait()
     dims = (((1,), (1,)), ((), ()))
     for e in range(experts):
         gate = lax.dot_general(gate_held[e], x[...], dims, preferred_element_type=F32)
+        if e == 0:
+            fill_routes(place, lang_w, info, meta)
         up = lax.dot_general(up_held[e], x[...], dims, preferred_element_type=F32)
         hidden = (gate / (1.0 + jnp.exp(-gate)) * up).astype(BF16)
         for b in range(2):
@@ -98,11 +133,14 @@
             ).astype(BF16)
 
 
-def hidden_rows(cap, first, place, lang_row, info, pieces, w_gate, w_up):
+def hidden_rows(cap, first, place, lang_row, tok, pieces, w_gate, w_up):
     experts, units, depth = w_gate.shape
-    tok = info.shape[2]
     outs = (pltpu.VMEM((experts, 2 * cap, units), BF16), jax.ShapeDtypeStruct((2, 8, tok), F32))
-    scratch = [pltpu.VMEM((2 * tok, depth), BF16), pltpu.SemaphoreType.DMA((len(pieces),))]
+    scratch = [
+        pltpu.VMEM((2 * tok, depth), BF16),
+        pltpu.VMEM((2, 16, depth // 4), BF16),
+        pltpu.SemaphoreType.DMA((len(pieces) + 2,)),
+    ]
     if first:
         outs += (pltpu.VMEM(w_gate.shape, BF16), pltpu.VMEM(w_up.shape, BF16))
         scratch.append(pltpu.SemaphoreType.DMA((2 * experts,)))
@@ -110,14 +148,11 @@
     return pl.pallas_call(
         lambda *a: hidden_kernel(cap, first, *a),
         out_shape=outs,
-        in_specs=[SMEM, VMEM, VMEM] + [ANY] * len(pieces) + [HBM if first else VMEM] * 2,
+        in_specs=[SMEM, VMEM] + [ANY] * len(pieces) + [HBM if first else VMEM] * 2,
         out_specs=(VMEM,) * len(outs),
         scratch_shapes=scratch,
         compiler_params=pltpu.CompilerParams(vmem_limit_bytes=8 * 2**20),
-        cost_estimate=pl.CostEstimate(
-            flops=8 * tok * experts * units * depth, bytes_accessed=0, transcendentals=0
-        ),
-    )(place, lang_row, info, *map(in_hbm, pieces), where(w_gate), where(w_up))
+    )(place, lang_row, *map(in_hbm, pieces), where(w_gate), where(w_up))
 
 
 def down_kernel(cap, place, meta, made, made_c, made_y, made_d, w_down, rows, own, other, total, sems):
@@ -163,9 +198,6 @@
         out_specs=(VMEM, VMEM, VMEM),
         scratch_shapes=[pltpu.VMEM((2 * tok, cols), F32), pltpu.SemaphoreType.DMA((4,))],
         compiler_params=pltpu.CompilerParams(vmem_limit_bytes=8 * 2**20),
-        cost_estimate=pl.CostEstimate(
-            flops=4 * cap * experts * depth * cols, bytes_accessed=0, transcendentals=0
-        ),
     )(place, meta, *pieces, held(w_down))
 
 
@@ -218,9 +250,6 @@
             pltpu.SemaphoreType.DMA((planes,)),
         ],
         compiler_params=pltpu.CompilerParams(vmem_limit_bytes=11 * 2**20),
-        cost_estimate=pl.CostEstimate(
-            flops=2 * experts * total * units * depth, bytes_accessed=4 * experts * units * depth, transcendentals=0
-        ),
     )(place, *metas, *parts)
 
 
@@ -251,6 +280,10 @@
 def over_z(a, k, what):
     with jax.named_scope(what):
         return lax.ppermute(a, "expert", planes_up(k % 4))
+
+
+def after(a, *others):
+    return lax.optimization_barrier((a, *others))[0]
 
 
 def by_planes(tokens, routes, route_weight, language, lang_weight, w_gate, w_up, w_down):
@@ -261,75 +294,72 @@
     lang_row = jnp.pad(lang_weight, (0, -lang_weight.shape[0] % 128))[None, :]
     n = len(ORDER)
     half = tok // 2
-    live, metas, parts, back = {}, {}, {}, {}
-    weights = kept = None
+    packed = pack_tokens(tokens, routes, route_weight, language)
+    live, metas, parts, sums, kept = {"t0": packed, "lang": lang_row}, {}, {}, {}, None
 
     def at(turn):
         return ORDER[turn] if 0 <= turn < n else None
 
-    for step in range(n + 5):
+    def weigh(k):
+        both = [live.pop(f"h{k}"), live.pop(f"hy{k}")]
+        far = [over_core(both[0], f"hid_c{k}"), over_core(both[1], f"hid_d{k}")]
+        parts[k], *sums[k] = down_rows(cap, place, metas[k], [both[0], far[0], both[1], far[1]], w_down)
+
+    for step in range(n + 2):
         new = {}
         if step == 0:
-            new["t0"] = tokens
-            info = jnp.concatenate(
-                [routes.T.astype(F32), route_weight.T, language[None, :].astype(F32), jnp.zeros((7, tok), F32)], axis=0
-            )
-            new["info"], new["info_x"] = info, over_x(info, "info_x")
-            new["c0"] = over_core(tokens, "tok_c00")
+            new["c0"] = over_core(packed, "tok_c00")
+            new["t3"] = over_z(packed, 3, "tok_z3")
+            early = over_z(packed, 1, "tok_z1")
         if step == 1:
-            new["info0"] = jnp.stack([live.pop("info"), live.pop("info_x")])
-        if 2 <= step < n + 1:
-            k = ORDER[step - 1]
-            new[f"info{k}"] = over_z(live["info0"], k, f"info_z{k}")
-        if step < n - 1:
-            k = ORDER[step + 1]
-            new[f"t{k}"] = over_z(live["t0"] if step else tokens, k, f"tok_z{k}")
+            new["t2"] = over_z(live["t3"], 3, "tok_z2")
+        if step == 2:
+            new["t1"] = live.pop("early")
         k = at(step)
         if k is not None:
-            source = live[f"t{k}"] if step else tokens
-            new[f"x{k}"], new[f"y{k}"] = over_x(source, f"tok_x{k}"), over_y(source, f"tok_y{k}")
+            new[f"x{k}"], new[f"y{k}"] = over_x(live[f"t{k}"], f"tok_x{k}"), over_y(live[f"t{k}"], f"tok_y{k}")
         k = at(step - 1)
         if k is not None:
-            three = [live.pop(f"t{k}") if k else tokens, live.pop(f"x{k}"), live.pop(f"y{k}")]
-            if step < n - 1:
-                across = [over_x(three[2][:half], f"tok_dx{k}"), over_y(three[1][half:], f"tok_dy{k}")]
+            three = [live[f"t{k}"] if k == 0 else live.pop(f"t{k}"), live.pop(f"x{k}"), live.pop(f"y{k}")]
+            if step in (1, 2, 3):
+                low, high = three[2][:half], three[1][half:tok]
+                if step == 1:
+                    low, high, new["early"] = lax.optimization_barrier((low, high, early))
+                across = [over_x(low, f"tok_dx{k}"), over_y(high, f"tok_dy{k}")]
             else:
                 across = [over_x(three[2], f"tok_dx{k}")]
             new[f"near{k}"] = three + across
         k = at(step - 2)
         if k is not None:
             near = live.pop(f"near{k}")
-            info = live.pop(f"info{k}") if k else live["info0"]
             far = [live.pop("c0") if i == 0 and k == 0 else over_core(p, f"tok_c{i}{k}") for i, p in enumerate(near)]
-            new[f"h{k}"], metas[k], *weights = hidden_rows(
-                cap, k == 0, place, lang_row, info, near + far, *(weights or (w_gate, w_up))
-            )
-            weights = weights or kept
-            kept = weights
+            made = hidden_rows(cap, not kept, place, live["lang"], tok, near + far, *(kept or (w_gate, w_up)))
+            new[f"h{k}"], metas[k] = made[:2]
+            kept = kept or made[2:]
         k = at(step - 3)
-        if k is not None:
-            made = live[f"h{k}"]
-            new[f"hy{k}"], new[f"hc{k}"] = over_y(made, f"hid_y{k}"), over_core(made, f"hid_c{k}")
-        k = at(step - 4)
-        if k is not None:
-            pieces = [live.pop(f"{name}{k}") for name in ("h", "hc", "hy")]
-            pieces.append(over_core(pieces[2], f"hid_d{k}"))
-            parts[k], new[f"own{k}"], new[f"other{k}"] = down_rows(cap, place, metas[k], pieces, w_down)
-        k = at(step - 5)
-        if k is not None:
-            new[f"mine{k}"], new[f"met{k}"] = live.pop(f"own{k}"), over_x(live.pop(f"other{k}"), f"sum_x{k}")
-        k = at(step - 6)
-        if k is not None:
-            part = live.pop(f"mine{k}") + live.pop(f"met{k}").astype(F32)
-            back[k] = part if k == 0 else over_z(part.astype(BF16), -k, f"sum_z{k}")
+        if k:
+            new[f"hy{k}"] = over_y(live[f"h{k}"], f"hid_y{k}")
         if step == n:
-            live.pop("t0"), live.pop("info0")
+            live.pop("t0")
         live = lax.optimization_barrier({**live, **new})
-    gram = gram_blocks(cap, place, [metas[k] for k in ORDER], [parts[k] for k in ORDER])
-    k = ORDER[-1]
-    part = (live[f"mine{k}"] + live[f"met{k}"].astype(F32)).astype(BF16)
-    out = sum(back[k].astype(F32) for k in ORDER[:-1])
-    out = out + over_z(part, -k, f"sum_z{k}").astype(F32)
+
+    live["hy1"] = over_y(live["h1"], "hid_y1")
+    weigh(2)
+    met2 = over_x(sums[2][1], "sum_x2")
+    weigh(3)
+    met3 = over_x(sums[3][1], "sum_x3")
+    weigh(1)
+    met1 = over_x(sums[1][1], "sum_x1")
+    back3 = over_z((sums[3][0] + met3.astype(F32)).astype(BF16), 1, "sum_z3")
+    way2 = over_z((sums[2][0] + met2.astype(F32)).astype(BF16), 3, "sum_z2")
+    live["hy0"] = over_y(after(live["h0"], sums[2][1]), "hid_y0")
+    weigh(0)
+    met0 = over_x(sums[0][1], "sum_x0")
+    part = sums[1][0] + met1.astype(F32) + way2.astype(F32)
+    last, own_part = lax.optimization_barrier((part.astype(BF16), parts[0]))
+    back1 = over_z(last, 3, "sum_z1")
+    out = sums[0][0] + met0.astype(F32) + back3.astype(F32) + back1.astype(F32)
+    gram = gram_blocks(cap, place, [metas[k] for k in ORDER], [own_part if k == 0 else parts[k] for k in ORDER])
     return out.astype(BF16), gram
 
 

time: 142 us -> 124 us (0.87); the launches traced: 139 us -> 124 us
  waiting for transfers between devices: 41.9 us -> 21.2 us
  starting transfers between devices: 44.7 us -> 48.3 us
  local copies, waits for them, and re-layouts: 3.42 us -> 5.95 us
  other arithmetic: 3.27 us -> 1.13 us
  Pallas kernels: 44.1 us -> 46.1 us
    ppermute x13 -> x12, waiting for transfers between devices: 26.9 us -> 6.67 us  [over_x(): return lax.ppermute(a, 'expert', ACROSS_X)]
    ppermute x9 -> x6, waiting for transfers between devices: 13.1 us -> 6.23 us  [over_z(): return lax.ppermute(a, 'expert', planes_up(k % 4))]
    ppermute x10 -> x11, waiting for transfers between devices: 0.03 us -> 5.75 us  [over_y(): return lax.ppermute(a, 'col', ACROSS_Y)]
    pallas_call x0 -> x1, Pallas kernels: none -> 1.66 us  [pack_tokens(): pl.pallas_call(pack_kernel, out_shape=pltpu.VMEM((tok + 16, feat), BF16),...]
    ppermute x26 -> x27, starting transfers between devices: 4.59 us -> 6.17 us  [over_core(): return lax.ppermute(a, 'col', CORE)]
    ppermute x10 -> x11, starting transfers between devices: 11.2 us -> 12.4 us  [over_y(): return lax.ppermute(a, 'col', ACROSS_Y)]
    ppermute x13 -> x12, starting transfers between devices: 12 us -> 12.8 us  [over_x(): return lax.ppermute(a, 'expert', ACROSS_X)]
    ppermute x9 -> x6, starting transfers between devices: 16.9 us -> 16.9 us  [over_z(): return lax.ppermute(a, 'expert', planes_up(k % 4))]
  transfers between devices with their start and end apart: 58 -> 56, of which waited for: 14 -> 17; matrix products, arithmetic and copies ran while one was open for 2% -> 2% of each run, Pallas kernels for 32% -> 36%
where the time goes in v3:
time: 124 us
  starting transfers between devices  48.3 us (39%)
  Pallas kernels  46.1 us (37%)
  waiting for transfers between devices  21.2 us (17%)
  local copies, waits for them, and re-layouts  5.95 us (5%)
    pallas_call x4, Pallas kernels, hidden_rows(): pl.pallas_call(lambda *a: hidden_kernel(cap, first, *a), out_shape=outs,...  28.2 us
    ppermute x6, starting transfers between devices, over_z(): return lax.ppermute(a, 'expert', planes_up(k % 4))  16.9 us
    ppermute x12, starting transfers between devices, over_x(): return lax.ppermute(a, 'expert', ACROSS_X)  12.8 us
    ppermute x11, starting transfers between devices, over_y(): return lax.ppermute(a, 'col', ACROSS_Y)  12.4 us
    pallas_call x4, Pallas kernels, down_rows(): pl.pallas_call(lambda *a: down_kernel(cap, *a), out_shape=(pltpu.VMEM((ex...  10.5 us
    ppermute x12, waiting for transfers between devices, over_x(): return lax.ppermute(a, 'expert', ACROSS_X)  6.67 us
    ppermute x6, waiting for transfers between devices, over_z(): return lax.ppermute(a, 'expert', planes_up(k % 4))  6.23 us
    ppermute x27, starting transfers between devices, over_core(): return lax.ppermute(a, 'col', CORE)  6.17 us
  transfers between devices with their start and end apart: 56, of which 17 were waited for; matrix products, arithmetic and copies ran while one was open for 2% of the time, Pallas kernels for 36%

profile of v3, /device:TPU:0, one launch (start us, length us, event | category | flops | bytes accessed | tf_op | source)
XLA Modules:
  0.0 123.8 jit_solution(10828271572160060397)
XLA Ops:
  0.6 1.7 %shard_map.95.a_2_ = bf16[144,1024]{1,0:T(8,128)(2,1)S(1)} custom-call(bf16[128,1024]{1,0:T(8,128)(2,1)} %tokens.1, s32[8,128]{1,0:T(8,128)} %bitcast.9, f32[8,128]{1,0:T(8,128)} %bitcast.10, s32[1,128]{1,0:T(1,128)} %bitcast.11), custom_call_target="tpu_custom_call" | custom-call | tf_op jit(solution)/shard_map/pallas_call | solution.py:40
  2.8 2.6 %collective-permute-start.1 = (bf16[144,1024]{1,0:T(8,128)(2,1)S(1)}, bf16[144,1024]{1,0:T(8,128)(2,1)S(1)}, u32[]{:S(2)}, u32[]{:S(2)}) collective-permute-start(bf16[144,1024]{1,0:T(8,128)(2,1)S(1)} %shard_map.95.a_2_), channel_id=1, source_target_pairs={{24,0},{28,4},{0,8},{4,12},{8,16},{12,20},{16,24},{20,28},{25,1},{... | collective-permute-start | bytes 884744 | tf_op jit(solution)/shard_map/tok_z3/ppermute | solution.py:282
  7.0 1.5 %collective-permute-start.3 = (bf16[144,1024]{1,0:T(8,128)(2,1)S(1)}, bf16[144,1024]{1,0:T(8,128)(2,1)S(1)}, u32[]{:S(2)}, u32[]{:S(2)}) collective-permute-start(bf16[144,1024]{1,0:T(8,128)(2,1)S(1)} %shard_map.95.a_2_), channel_id=1, source_target_pairs={{0,2},{1,3},{2,0},{3,1},{4,6},{5,7},{6,4},{7,5},{8,10},{9,11},{10,... | collective-permute-start | bytes 884744 | tf_op jit(solution)/shard_map/tok_y0/ppermute | solution.py:272
  8.5 2.2 %collective-permute-start.4 = (bf16[144,1024]{1,0:T(8,128)(2,1)S(1)}, bf16[144,1024]{1,0:T(8,128)(2,1)S(1)}, u32[]{:S(2)}, u32[]{:S(2)}) collective-permute-start(bf16[144,1024]{1,0:T(8,128)(2,1)S(1)} %shard_map.95.a_2_), channel_id=1, source_target_pairs={{8,0},{12,4},{16,8},{20,12},{24,16},{28,20},{0,24},{4,28},{9,1},{1... | collective-permute-start | bytes 884744 | tf_op jit(solution)/shard_map/tok_z1/ppermute | solution.py:282
  11.4 4.0 %collective-permute-done.1.a_2_ = bf16[144,1024]{1,0:T(8,128)(2,1)S(1)} collective-permute-done((bf16[144,1024]{1,0:T(8,128)(2,1)S(1)}, bf16[144,1024]{1,0:T(8,128)(2,1)S(1)}, u32[]{:S(2)}, u32[]{:S(2)}) %collective-permute-start.1) | collective-permute-done | bytes 294944 | tf_op jit(solution)/shard_map/tok_z3/ppermute | solution.py:282
  15.8 1.6 %collective-permute-start.7 = (bf16[144,1024]{1,0:T(8,128)(2,1)S(1)}, bf16[144,1024]{1,0:T(8,128)(2,1)S(1)}, u32[]{:S(2)}, u32[]{:S(2)}) collective-permute-start(bf16[144,1024]{1,0:T(8,128)(2,1)S(1)} %collective-permute-done.1.a_2_), channel_id=1, source_target_pairs={{24,0},{28,4},{0,8},{4,12},{8,16},{12,20},{16,24},{20,28},{25,1},{... | collective-permute-start | bytes 884744 | tf_op jit(solution)/shard_map/tok_z2/ppermute | solution.py:282
  17.9 1.5 %collective-permute-start.9 = (bf16[144,1024]{1,0:T(8,128)(2,1)S(1)}, bf16[144,1024]{1,0:T(8,128)(2,1)S(1)}, u32[]{:S(2)}, u32[]{:S(2)}) collective-permute-start(bf16[144,1024]{1,0:T(8,128)(2,1)S(1)} %collective-permute-done.1.a_2_), channel_id=1, source_target_pairs={{0,2},{1,3},{2,0},{3,1},{4,6},{5,7},{6,4},{7,5},{8,10},{9,11},{10,... | collective-permute-start | bytes 884744 | tf_op jit(solution)/shard_map/tok_y3/ppermute | solution.py:272
  19.4 2.2 %collective-permute-done.4.a_2_ = bf16[144,1024]{1,0:T(8,128)(2,1)S(1)} collective-permute-done((bf16[144,1024]{1,0:T(8,128)(2,1)S(1)}, bf16[144,1024]{1,0:T(8,128)(2,1)S(1)}, u32[]{:S(2)}, u32[]{:S(2)}) %collective-permute-start.4) | collective-permute-done | bytes 294944 | tf_op jit(solution)/shard_map/tok_z1/ppermute | solution.py:282
  21.6 1.6 %collective-permute-start.5 = (bf16[64,1024]{1,0:T(8,128)(2,1)S(1)}, bf16[64,1024]{1,0:T(8,128)(2,1)S(1)}, u32[]{:S(2)}, u32[]{:S(2)}) collective-permute-start(bf16[64,1024]{1,0:T(8,128)(2,1)S(1)} %slice.18), channel_id=1, source_target_pairs={{0,4},{4,0},{8,12},{12,8},{16,20},{20,16},{24,28},{28,24},{1,5},{5... | collective-permute-start | bytes 393224 | tf_op jit(solution)/shard_map/tok_dx0/ppermute | solution.py:277
  24.6 3.2 %collective-permute-done.5.a_5_ = bf16[64,1024]{1,0:T(8,128)(2,1)S(1)} collective-permute-done((bf16[64,1024]{1,0:T(8,128)(2,1)S(1)}, bf16[64,1024]{1,0:T(8,128)(2,1)S(1)}, u32[]{:S(2)}, u32[]{:S(2)}) %collective-permute-start.5) | collective-permute-done | bytes 131104 | tf_op jit(solution)/shard_map/tok_dx0/ppermute | solution.py:277
  35.3 9.9 %shard_map.96 = (bf16[2,192,384]{2,1,0:T(8,128)(2,1)S(1)}, f32[2,8,128]{2,1,0:T(8,128)S(1)}, bf16[2,384,4096]{2,1,0:T(8,128)(2,1)S(1)}, bf16[2,384,4096]{2,1,0:T(8,128)(2,1)S(1)}) custom-call(s32[2]{0:T(128)S(1)} %pad_add_fusion.a_0_, f32[1,128]{1,0:T(1,128)S(1)} %pad_bitcast_fusion.a_1_, bf16[144,1024]{1,0:T(8,128)(2,1)} %copy-done, ...), custom_call_target="tpu_custom_call" | custom-call | tf_op jit(solution)/shard_map/pallas_call | solution.py:148
  52.1 6.1 %shard_map.97 = (bf16[2,192,384]{2,1,0:T(8,128)(2,1)S(1)}, f32[2,8,128]{2,1,0:T(8,128)S(1)}) custom-call(s32[2]{0:T(128)S(1)} %pad_add_fusion.a_0_, f32[1,128]{1,0:T(1,128)S(1)} %pad_bitcast_fusion.a_1_, bf16[144,1024]{1,0:T(8,128)(2,1)} %copy-done.9, bf16[144,1024]{1,0:T(8,128)(2,1)} %copy-done.3, bf16[144,1024]{1,0:T(8,128)(2,1)} %copy-done.4, ...), custom_call_target="tpu_custom_call" | custom-call | tf_op jit(solution)/shard_map/pallas_call | solution.py:148
  65.6 6.1 %shard_map.98 = (bf16[2,192,384]{2,1,0:T(8,128)(2,1)S(1)}, f32[2,8,128]{2,1,0:T(8,128)S(1)}) custom-call(s32[2]{0:T(128)S(1)} %pad_add_fusion.a_0_, f32[1,128]{1,0:T(1,128)S(1)} %pad_bitcast_fusion.a_1_, bf16[144,1024]{1,0:T(8,128)(2,1)} %copy-done.8, bf16[144,1024]{1,0:T(8,128)(2,1)} %copy-done.1, bf16[144,1024]{1,0:T(8,128)(2,1)} %copy-done.2, ...), custom_call_target="tpu_custom_call" | custom-call | tf_op jit(solution)/shard_map/pallas_call | solution.py:148
  75.8 6.2 %shard_map.99 = (bf16[2,192,384]{2,1,0:T(8,128)(2,1)S(1)}, f32[2,8,128]{2,1,0:T(8,128)S(1)}) custom-call(s32[2]{0:T(128)S(1)} %pad_add_fusion.a_0_, f32[1,128]{1,0:T(1,128)S(1)} %pad_bitcast_fusion.a_1_, bf16[144,1024]{1,0:T(8,128)(2,1)} %copy-done.7, bf16[144,1024]{1,0:T(8,128)(2,1)} %copy-done.10, bf16[144,1024]{1,0:T(8,128)(2,1)} %copy-done.11, ...), custom_call_target="tpu_custom_call" | custom-call | tf_op jit(solution)/shard_map/pallas_call | solution.py:148
  84.1 2.6 %shard_map.100 = (bf16[2,192,1536]{2,1,0:T(8,128)(2,1)S(1)}, f32[128,1024]{1,0:T(8,128)S(1)}, bf16[128,1024]{1,0:T(8,128)(2,1)S(1)}) custom-call(s32[2]{0:T(128)S(1)} %pad_add_fusion.a_0_, f32[2,8,128]{2,1,0:T(8,128)S(1)} %get-tuple-element.145.a_1_.a_3_, bf16[2,192,384]{2,1,0:T(8,128)(2,1)S(1)} %get-tuple-element.146.a_2_, ...), custom_call_target="tpu_custom_call" | custom-call | tf_op jit(solution)/shard_map/pallas_call | solution.py:190
  87.9 3.8 %collective-permute-done.50.a_4_ = bf16[2,192,384]{2,1,0:T(8,128)(2,1)S(1)} collective-permute-done((bf16[2,192,384]{2,1,0:T(8,128)(2,1)S(1)}, bf16[2,192,384]{2,1,0:T(8,128)(2,1)S(1)}, u32[]{:S(2)}, u32[]{:S(2)}) %collective-permute-start.50) | collective-permute-done | bytes 294944 | tf_op jit(solution)/shard_map/hid_y1/ppermute | solution.py:272
  92.5 2.6 %shard_map.102 = (bf16[2,192,1536]{2,1,0:T(8,128)(2,1)S(1)}, f32[128,1024]{1,0:T(8,128)S(1)}, bf16[128,1024]{1,0:T(8,128)(2,1)S(1)}) custom-call(s32[2]{0:T(128)S(1)} %pad_add_fusion.a_0_, f32[2,8,128]{2,1,0:T(8,128)S(1)} %get-tuple-element.152.a_1_.a_2_, bf16[2,192,384]{2,1,0:T(8,128)(2,1)S(1)} %get-tuple-element.153.a_2_, ...), custom_call_target="tpu_custom_call" | custom-call | tf_op jit(solution)/shard_map/pallas_call | solution.py:190
  96.3 3.5 %collective-permute-start.54 = (bf16[128,1024]{1,0:T(8,128)(2,1)S(1)}, bf16[128,1024]{1,0:T(8,128)(2,1)S(1)}, u32[]{:S(2)}, u32[]{:S(2)}) collective-permute-start(bf16[128,1024]{1,0:T(8,128)(2,1)S(1)} %add_convert_fusion.2), channel_id=1, source_target_pairs={{24,0},{28,4},{0,8},{4,12},{8,16},{12,20},{16,24},{20,28},{25,1},{... | collective-permute-start | bytes 786440 | tf_op jit(solution)/shard_map/sum_z2/ppermute | solution.py:282
  99.8 2.6 %shard_map.103 = (bf16[2,192,1536]{2,1,0:T(8,128)(2,1)S(1)}, f32[128,1024]{1,0:T(8,128)S(1)}, bf16[128,1024]{1,0:T(8,128)(2,1)S(1)}) custom-call(s32[2]{0:T(128)S(1)} %pad_add_fusion.a_0_, f32[2,8,128]{2,1,0:T(8,128)S(1)} %get-tuple-element.157.a_1_.a_4_, bf16[2,192,384]{2,1,0:T(8,128)(2,1)S(1)} %get-tuple-element.158.a_2_, ...), custom_call_target="tpu_custom_call" | custom-call | tf_op jit(solution)/shard_map/pallas_call | solution.py:190
  104.1 4.5 %collective-permute-start.48 = (bf16[128,1024]{1,0:T(8,128)(2,1)S(1)}, bf16[128,1024]{1,0:T(8,128)(2,1)S(1)}, u32[]{:S(2)}, u32[]{:S(2)}) collective-permute-start(bf16[128,1024]{1,0:T(8,128)(2,1)S(1)} %add_convert_fusion.3), channel_id=1, source_target_pairs={{8,0},{12,4},{16,8},{20,12},{24,16},{28,20},{0,24},{4,28},{9,1},{1... | collective-permute-start | bytes 786440 | tf_op jit(solution)/shard_map/sum_z3/ppermute | solution.py:282
  108.6 1.8 %collective-permute-done.52 = bf16[128,1024]{1,0:T(8,128)(2,1)S(1)} collective-permute-done((bf16[128,1024]{1,0:T(8,128)(2,1)S(1)}, bf16[128,1024]{1,0:T(8,128)(2,1)S(1)}, u32[]{:S(2)}, u32[]{:S(2)}) %collective-permute-start.52) | collective-permute-done | bytes 262176 | tf_op jit(solution)/shard_map/sum_x1/ppermute | solution.py:277
  110.5 2.6 %shard_map.101 = (bf16[2,192,1536]{2,1,0:T(8,128)(2,1)S(1)}, f32[128,1024]{1,0:T(8,128)S(1)}, bf16[128,1024]{1,0:T(8,128)(2,1)S(1)}) custom-call(s32[2]{0:T(128)S(1)} %pad_add_fusion.a_0_, f32[2,8,128]{2,1,0:T(8,128)S(1)} %get-tuple-element.101.a_1_, bf16[2,192,384]{2,1,0:T(8,128)(2,1)S(1)} %get-tuple-element.149.a_2_, ...), custom_call_target="tpu_custom_call" | custom-call | tf_op jit(solution)/shard_map/pallas_call | solution.py:190
  113.1 2.4 %collective-permute-start.55 = (bf16[128,1024]{1,0:T(8,128)(2,1)S(1)}, bf16[128,1024]{1,0:T(8,128)(2,1)S(1)}, u32[]{:S(2)}, u32[]{:S(2)}) collective-permute-start(bf16[128,1024]{1,0:T(8,128)(2,1)S(1)} %add_convert_fusion.1), channel_id=1, source_target_pairs={{24,0},{28,4},{0,8},{4,12},{8,16},{12,20},{16,24},{20,28},{25,1},{... | collective-permute-start | bytes 786440 | tf_op jit(solution)/shard_map/sum_z1/ppermute | solution.py:282
  116.6 5.7 %shard_map.104 = f32[2,384,1536]{2,1,0:T(8,128)} custom-call(s32[2]{0:T(128)S(1)} %pad_add_fusion.a_0_, f32[2,8,128]{2,1,0:T(8,128)S(1)} %get-tuple-element.101.a_1_, f32[2,8,128]{2,1,0:T(8,128)S(1)} %get-tuple-element.152.a_1_.a_2_, f32[2,8,128]{2,1,0:T(8,128)S(1)} %get-tuple-element.145.a_1_.a_3_, f32[2,8,128]{2,1,0:T(8,128)S(1)} %get-tuple-element.157.a_1_.a_4_, ...), custom_call_target="tpu_custom_call" | custom-call | tf_op jit(solution)/shard_map/pallas_call | solution.py:241
  (185 shorter events, 40.0 us)
Async XLA Ops:
  2.3 9.1 %collective-permute-start = (bf16[144,1024]{1,0:T(8,128)(2,1)S(1)}, bf16[144,1024]{1,0:T(8,128)(2,1)S(1)}, u32[]{:S(2)}, u32[]{:S(2)}) collective-permute-start(bf16[144,1024]{1,0:T(8,128)(2,1)S(1)} %shard_map.95.a_2_), channel_id=1, source_target_pairs={{0,1},{1,0},{2,3},{3,2},{4,5},{5,4},{6,7},{7,6},{8,9},{9,8},{10,11... | collective-permute-start | bytes 884744 | tf_op jit(solution)/shard_map/tok_c00/ppermute | solution.py:267
  2.8 12.6 %collective-permute-start.1 = (bf16[144,1024]{1,0:T(8,128)(2,1)S(1)}, bf16[144,1024]{1,0:T(8,128)(2,1)S(1)}, u32[]{:S(2)}, u32[]{:S(2)}) collective-permute-start(bf16[144,1024]{1,0:T(8,128)(2,1)S(1)} %shard_map.95.a_2_), channel_id=1, source_target_pairs={{24,0},{28,4},{0,8},{4,12},{8,16},{12,20},{16,24},{20,28},{25,1},{... | collective-permute-start | bytes 884744 | tf_op jit(solution)/shard_map/tok_z3/ppermute | solution.py:282
  5.5 9.9 %collective-permute-start.2 = (bf16[144,1024]{1,0:T(8,128)(2,1)S(1)}, bf16[144,1024]{1,0:T(8,128)(2,1)S(1)}, u32[]{:S(2)}, u32[]{:S(2)}) collective-permute-start(bf16[144,1024]{1,0:T(8,128)(2,1)S(1)} %shard_map.95.a_2_), channel_id=1, source_target_pairs={{0,4},{4,0},{8,12},{12,8},{16,20},{20,16},{24,28},{28,24},{1,5},{5... | collective-permute-start | bytes 884744 | tf_op jit(solution)/shard_map/tok_x0/ppermute | solution.py:277
  8.5 13.2 %collective-permute-start.4 = (bf16[144,1024]{1,0:T(8,128)(2,1)S(1)}, bf16[144,1024]{1,0:T(8,128)(2,1)S(1)}, u32[]{:S(2)}, u32[]{:S(2)}) collective-permute-start(bf16[144,1024]{1,0:T(8,128)(2,1)S(1)} %shard_map.95.a_2_), channel_id=1, source_target_pairs={{8,0},{12,4},{16,8},{20,12},{24,16},{28,20},{0,24},{4,28},{9,1},{1... | collective-permute-start | bytes 884744 | tf_op jit(solution)/shard_map/tok_z1/ppermute | solution.py:282
  15.8 12.5 %collective-permute-start.7 = (bf16[144,1024]{1,0:T(8,128)(2,1)S(1)}, bf16[144,1024]{1,0:T(8,128)(2,1)S(1)}, u32[]{:S(2)}, u32[]{:S(2)}) collective-permute-start(bf16[144,1024]{1,0:T(8,128)(2,1)S(1)} %collective-permute-done.1.a_2_), channel_id=1, source_target_pairs={{24,0},{28,4},{0,8},{4,12},{8,16},{12,20},{16,24},{20,28},{25,1},{... | collective-permute-start | bytes 884744 | tf_op jit(solution)/shard_map/tok_z2/ppermute | solution.py:282
  17.3 11.0 %collective-permute-start.8 = (bf16[144,1024]{1,0:T(8,128)(2,1)S(1)}, bf16[144,1024]{1,0:T(8,128)(2,1)S(1)}, u32[]{:S(2)}, u32[]{:S(2)}) collective-permute-start(bf16[144,1024]{1,0:T(8,128)(2,1)S(1)} %collective-permute-done.1.a_2_), channel_id=1, source_target_pairs={{0,4},{4,0},{8,12},{12,8},{16,20},{20,16},{24,28},{28,24},{1,5},{5... | collective-permute-start | bytes 884744 | tf_op jit(solution)/shard_map/tok_x3/ppermute | solution.py:277
  17.9 10.5 %collective-permute-start.9 = (bf16[144,1024]{1,0:T(8,128)(2,1)S(1)}, bf16[144,1024]{1,0:T(8,128)(2,1)S(1)}, u32[]{:S(2)}, u32[]{:S(2)}) collective-permute-start(bf16[144,1024]{1,0:T(8,128)(2,1)S(1)} %collective-permute-done.1.a_2_), channel_id=1, source_target_pairs={{0,2},{1,3},{2,0},{3,1},{4,6},{5,7},{6,4},{7,5},{8,10},{9,11},{10,... | collective-permute-start | bytes 884744 | tf_op jit(solution)/shard_map/tok_y3/ppermute | solution.py:272
  29.0 16.1 %collective-permute-start.16 = (bf16[144,1024]{1,0:T(8,128)(2,1)S(1)}, bf16[144,1024]{1,0:T(8,128)(2,1)S(1)}, u32[]{:S(2)}, u32[]{:S(2)}) collective-permute-start(bf16[144,1024]{1,0:T(8,128)(2,1)S(1)} %collective-permute-done.7.a_2_), channel_id=1, source_target_pairs={{0,4},{4,0},{8,12},{12,8},{16,20},{20,16},{24,28},{28,24},{1,5},{5... | collective-permute-start | bytes 884744 | tf_op jit(solution)/shard_map/tok_x2/ppermute | solution.py:277
  30.2 14.9 %collective-permute-start.17 = (bf16[144,1024]{1,0:T(8,128)(2,1)S(1)}, bf16[144,1024]{1,0:T(8,128)(2,1)S(1)}, u32[]{:S(2)}, u32[]{:S(2)}) collective-permute-start(bf16[144,1024]{1,0:T(8,128)(2,1)S(1)} %collective-permute-done.7.a_2_), channel_id=1, source_target_pairs={{0,2},{1,3},{2,0},{3,1},{4,6},{5,7},{6,4},{7,5},{8,10},{9,11},{10,... | collective-permute-start | bytes 884744 | tf_op jit(solution)/shard_map/tok_y2/ppermute | solution.py:272
  33.8 11.4 %collective-permute-start.14 = (bf16[64,1024]{1,0:T(8,128)(2,1)}, bf16[64,1024]{1,0:T(8,128)(2,1)}, u32[]{:S(2)}, u32[]{:S(2)}) collective-permute-start(bf16[64,1024]{1,0:T(8,128)(2,1)} %slice.20), channel_id=1, source_target_pairs={{0,4},{4,0},{8,12},{12,8},{16,20},{20,16},{24,28},{28,24},{1,5},{5... | collective-permute-start | bytes 393224 | tf_op jit(solution)/shard_map/tok_dx3/ppermute | solution.py:277
  34.4 10.7 %collective-permute-start.15 = (bf16[64,1024]{1,0:T(8,128)(2,1)}, bf16[64,1024]{1,0:T(8,128)(2,1)}, u32[]{:S(2)}, u32[]{:S(2)}) collective-permute-start(bf16[64,1024]{1,0:T(8,128)(2,1)} %slice.21), channel_id=1, source_target_pairs={{0,2},{1,3},{2,0},{3,1},{4,6},{5,7},{6,4},{7,5},{8,10},{9,11},{10,... | collective-permute-start | bytes 393224 | tf_op jit(solution)/shard_map/tok_dy3/ppermute | solution.py:272
  47.2 12.9 %collective-permute-start.25 = (bf16[144,1024]{1,0:T(8,128)(2,1)S(1)}, bf16[144,1024]{1,0:T(8,128)(2,1)S(1)}, u32[]{:S(2)}, u32[]{:S(2)}) collective-permute-start(bf16[144,1024]{1,0:T(8,128)(2,1)S(1)} %collective-permute-done.4.a_2_), channel_id=1, source_target_pairs={{0,4},{4,0},{8,12},{12,8},{16,20},{20,16},{24,28},{28,24},{1,5},{5... | collective-permute-start | bytes 884744 | tf_op jit(solution)/shard_map/tok_x1/ppermute | solution.py:277
  48.5 11.7 %collective-permute-start.26 = (bf16[144,1024]{1,0:T(8,128)(2,1)S(1)}, bf16[144,1024]{1,0:T(8,128)(2,1)S(1)}, u32[]{:S(2)}, u32[]{:S(2)}) collective-permute-start(bf16[144,1024]{1,0:T(8,128)(2,1)S(1)} %collective-permute-done.4.a_2_), channel_id=1, source_target_pairs={{0,2},{1,3},{2,0},{3,1},{4,6},{5,7},{6,4},{7,5},{8,10},{9,11},{10,... | collective-permute-start | bytes 884744 | tf_op jit(solution)/shard_map/tok_y1/ppermute | solution.py:272
  50.1 9.0 %collective-permute-start.23 = (bf16[64,1024]{1,0:T(8,128)(2,1)S(1)}, bf16[64,1024]{1,0:T(8,128)(2,1)S(1)}, u32[]{:S(2)}, u32[]{:S(2)}) collective-permute-start(bf16[64,1024]{1,0:T(8,128)(2,1)S(1)} %slice.22), channel_id=1, source_target_pairs={{0,4},{4,0},{8,12},{12,8},{16,20},{20,16},{24,28},{28,24},{1,5},{5... | collective-permute-start | bytes 393224 | tf_op jit(solution)/shard_map/tok_dx2/ppermute | solution.py:277
  50.8 9.4 %collective-permute-start.24 = (bf16[64,1024]{1,0:T(8,128)(2,1)S(1)}, bf16[64,1024]{1,0:T(8,128)(2,1)S(1)}, u32[]{:S(2)}, u32[]{:S(2)}) collective-permute-start(bf16[64,1024]{1,0:T(8,128)(2,1)S(1)} %slice.23), channel_id=1, source_target_pairs={{0,2},{1,3},{2,0},{3,1},{4,6},{5,7},{6,4},{7,5},{8,10},{9,11},{10,... | collective-permute-start | bytes 393224 | tf_op jit(solution)/shard_map/tok_dy2/ppermute | solution.py:272
  61.6 10.1 %collective-permute-start.32 = (bf16[2,192,384]{2,1,0:T(8,128)(2,1)S(1)}, bf16[2,192,384]{2,1,0:T(8,128)(2,1)S(1)}, u32[]{:S(2)}, u32[]{:S(2)}) collective-permute-start(bf16[2,192,384]{2,1,0:T(8,128)(2,1)S(1)} %get-tuple-element.153.a_2_), channel_id=1, source_target_pairs={{0,2},{1,3},{2,0},{3,1},{4,6},{5,7},{6,4},{7,5},{8,10},{9,11},{10,... | collective-permute-start | bytes 884744 | tf_op jit(solution)/shard_map/hid_y3/ppermute | solution.py:272
  73.0 9.1 %collective-permute-start.38 = (bf16[2,192,384]{2,1,0:T(8,128)(2,1)S(1)}, bf16[2,192,384]{2,1,0:T(8,128)(2,1)S(1)}, u32[]{:S(2)}, u32[]{:S(2)}) collective-permute-start(bf16[2,192,384]{2,1,0:T(8,128)(2,1)S(1)} %get-tuple-element.146.a_2_), channel_id=1, source_target_pairs={{0,2},{1,3},{2,0},{3,1},{4,6},{5,7},{6,4},{7,5},{8,10},{9,11},{10,... | collective-permute-start | bytes 884744 | tf_op jit(solution)/shard_map/hid_y2/ppermute | solution.py:272
  82.6 9.1 %collective-permute-start.50 = (bf16[2,192,384]{2,1,0:T(8,128)(2,1)S(1)}, bf16[2,192,384]{2,1,0:T(8,128)(2,1)S(1)}, u32[]{:S(2)}, u32[]{:S(2)}) collective-permute-start(bf16[2,192,384]{2,1,0:T(8,128)(2,1)S(1)} %get-tuple-element.158.a_2_), channel_id=1, source_target_pairs={{0,2},{1,3},{2,0},{3,1},{4,6},{5,7},{6,4},{7,5},{8,10},{9,11},{10,... | collective-permute-start | bytes 884744 | tf_op jit(solution)/shard_map/hid_y1/ppermute | solution.py:272
  86.8 9.4 %collective-permute-start.53 = (bf16[128,1024]{1,0:T(8,128)(2,1)S(1)}, bf16[128,1024]{1,0:T(8,128)(2,1)S(1)}, u32[]{:S(2)}, u32[]{:S(2)}) collective-permute-start(bf16[128,1024]{1,0:T(8,128)(2,1)S(1)} %get-tuple-element.148), channel_id=1, source_target_pairs={{0,4},{4,0},{8,12},{12,8},{16,20},{20,16},{24,28},{28,24},{1,5},{5... | collective-permute-start | bytes 786440 | tf_op jit(solution)/shard_map/sum_x2/ppermute | solution.py:277
  87.9 11.9 %collective-permute-start.49 = (bf16[2,192,384]{2,1,0:T(8,128)(2,1)S(1)}, bf16[2,192,384]{2,1,0:T(8,128)(2,1)S(1)}, u32[]{:S(2)}, u32[]{:S(2)}) collective-permute-start(bf16[2,192,384]{2,1,0:T(8,128)(2,1)S(1)} %get-tuple-element.158.a_2_), channel_id=1, source_target_pairs={{0,1},{1,0},{2,3},{3,2},{4,5},{5,4},{6,7},{7,6},{8,9},{9,8},{10,11... | collective-permute-start | bytes 884744 | tf_op jit(solution)/shard_map/hid_c1/ppermute | solution.py:267
  91.7 11.8 %collective-permute-start.42 = (bf16[2,192,384]{2,1,0:T(8,128)(2,1)S(1)}, bf16[2,192,384]{2,1,0:T(8,128)(2,1)S(1)}, u32[]{:S(2)}, u32[]{:S(2)}) collective-permute-start(bf16[2,192,384]{2,1,0:T(8,128)(2,1)S(1)} %get-tuple-element.149.a_2_), channel_id=1, source_target_pairs={{0,2},{1,3},{2,0},{3,1},{4,6},{5,7},{6,4},{7,5},{8,10},{9,11},{10,... | collective-permute-start | bytes 884744 | tf_op jit(solution)/shard_map/hid_y0/ppermute | solution.py:272
  96.3 12.3 %collective-permute-start.54 = (bf16[128,1024]{1,0:T(8,128)(2,1)S(1)}, bf16[128,1024]{1,0:T(8,128)(2,1)S(1)}, u32[]{:S(2)}, u32[]{:S(2)}) collective-permute-start(bf16[128,1024]{1,0:T(8,128)(2,1)S(1)} %add_convert_fusion.2), channel_id=1, source_target_pairs={{24,0},{28,4},{0,8},{4,12},{8,16},{12,20},{16,24},{20,28},{25,1},{... | collective-permute-start | bytes 786440 | tf_op jit(solution)/shard_map/sum_z2/ppermute | solution.py:282
  104.1 18.1 %collective-permute-start.48 = (bf16[128,1024]{1,0:T(8,128)(2,1)S(1)}, bf16[128,1024]{1,0:T(8,128)(2,1)S(1)}, u32[]{:S(2)}, u32[]{:S(2)}) collective-permute-start(bf16[128,1024]{1,0:T(8,128)(2,1)S(1)} %add_convert_fusion.3), channel_id=1, source_target_pairs={{8,0},{12,4},{16,8},{20,12},{24,16},{28,20},{0,24},{4,28},{9,1},{1... | collective-permute-start | bytes 786440 | tf_op jit(solution)/shard_map/sum_z3/ppermute | solution.py:282
  113.1 9.1 %collective-permute-start.55 = (bf16[128,1024]{1,0:T(8,128)(2,1)S(1)}, bf16[128,1024]{1,0:T(8,128)(2,1)S(1)}, u32[]{:S(2)}, u32[]{:S(2)}) collective-permute-start(bf16[128,1024]{1,0:T(8,128)(2,1)S(1)} %add_convert_fusion.1), channel_id=1, source_target_pairs={{24,0},{28,4},{0,8},{4,12},{8,16},{12,20},{16,24},{20,28},{25,1},{... | collective-permute-start | bytes 786440 | tf_op jit(solution)/shard_map/sum_z1/ppermute | solution.py:282
  (69 other events, 526.1 us)

commit v4 on v3

--- a/solution.py
+++ b/solution.py
@@ -107,20 +107,25 @@
             if i >= 3:
                 row += src.shape[0]
             copies.append(pltpu.make_async_copy(src, dst, sems.at[core * half + i]))
+    loads = [[] for _ in range(experts)]
     if first:
-        for i, (src, dst) in enumerate(((w_gate, gate_held), (w_up, up_held))):
-            copies += [
-                pltpu.make_async_copy(src.at[e], dst.at[e], weight_sems.at[2 * e + i]) for e in range(experts)
-            ]
+        for e in range(experts):
+            for i, (src, dst) in enumerate(((w_gate, gate_held), (w_up, up_held))):
+                loads[e].append(pltpu.make_async_copy(src.at[e], dst.at[e], weight_sems.at[2 * e + i]))
     routes = [
         pltpu.make_async_copy(pieces[b].at[pl.ds(tok, 16)], info.at[b], sems.at[len(pieces) + b]) for b in range(2)
     ]
-    for copy in routes + copies:
+    for copy in routes + copies + loads[0]:
         copy.start()
-    for copy in routes + copies:
+    for copy in routes + copies + loads[0]:
         copy.wait()
+    for later in loads[1:]:
+        for copy in later:
+            copy.start()
     dims = (((1,), (1,)), ((), ()))
     for e in range(experts):
+        for copy in loads[e] if e else []:
+            copy.wait()
         gate = lax.dot_general(gate_held[e], x[...], dims, preferred_element_type=F32)
         if e == 0:
             fill_routes(place, lang_w, info, meta)
@@ -148,11 +153,11 @@
     return pl.pallas_call(
         lambda *a: hidden_kernel(cap, first, *a),
         out_shape=outs,
-        in_specs=[SMEM, VMEM] + [ANY] * len(pieces) + [HBM if first else VMEM] * 2,
+        in_specs=[SMEM, VMEM] + [ANY] * (len(pieces) // 2) + [VMEM] * (len(pieces) // 2) + [HBM if first else VMEM] * 2,
         out_specs=(VMEM,) * len(outs),
         scratch_shapes=scratch,
         compiler_params=pltpu.CompilerParams(vmem_limit_bytes=8 * 2**20),
-    )(place, lang_row, *map(in_hbm, pieces), where(w_gate), where(w_up))
+    )(place, lang_row, *map(in_hbm, pieces[: len(pieces) // 2]), *map(held, pieces[len(pieces) // 2 :]), where(w_gate), where(w_up))
 
 
 def down_kernel(cap, place, meta, made, made_c, made_y, made_d, w_down, rows, own, other, total, sems):
@@ -329,10 +334,13 @@
             else:
                 across = [over_x(three[2], f"tok_dx{k}")]
             new[f"near{k}"] = three + across
+            if step == n:
+                new[f"far{k}"] = [over_core(p, f"tok_c{i}{k}") for i, p in enumerate(three)]
         k = at(step - 2)
         if k is not None:
             near = live.pop(f"near{k}")
-            far = [live.pop("c0") if i == 0 and k == 0 else over_core(p, f"tok_c{i}{k}") for i, p in enumerate(near)]
+            far = [live.pop("c0")] if k == 0 else live.pop(f"far{k}", [])
+            far += [over_core(p, f"tok_c{i}{k}") for i, p in enumerate(near) if i >= len(far)]
             made = hidden_rows(cap, not kept, place, live["lang"], tok, near + far, *(kept or (w_gate, w_up)))
             new[f"h{k}"], metas[k] = made[:2]
             kept = kept or made[2:]
@@ -341,22 +349,25 @@
             new[f"hy{k}"] = over_y(live[f"h{k}"], f"hid_y{k}")
         if step == n:
             live.pop("t0")
+        if step == n + 1:
+            weigh(3)
+            new["own3"], new["other3"] = sums.pop(3)
         live = lax.optimization_barrier({**live, **new})
 
     live["hy1"] = over_y(live["h1"], "hid_y1")
+    met3 = over_x(live["other3"], "sum_x3")
     weigh(2)
     met2 = over_x(sums[2][1], "sum_x2")
-    weigh(3)
-    met3 = over_x(sums[3][1], "sum_x3")
+    live["hy0"] = over_y(after(live["h0"], sums[2][1]), "hid_y0")
     weigh(1)
     met1 = over_x(sums[1][1], "sum_x1")
-    back3 = over_z((sums[3][0] + met3.astype(F32)).astype(BF16), 1, "sum_z3")
-    way2 = over_z((sums[2][0] + met2.astype(F32)).astype(BF16), 3, "sum_z2")
-    live["hy0"] = over_y(after(live["h0"], sums[2][1]), "hid_y0")
+    back3 = over_z((live["own3"] + met3.astype(F32)).astype(BF16), 1, "sum_z3")
+    way2 = (sums[2][0] + met2.astype(F32)).astype(BF16)
+    way2 = over_z(way2, 3, "sum_z2")
     weigh(0)
-    met0 = over_x(sums[0][1], "sum_x0")
     part = sums[1][0] + met1.astype(F32) + way2.astype(F32)
-    last, own_part = lax.optimization_barrier((part.astype(BF16), parts[0]))
+    last, own_part, other0 = lax.optimization_barrier((part.astype(BF16), parts[0], sums[0][1]))
+    met0 = over_x(other0, "sum_x0")
     back1 = over_z(last, 3, "sum_z1")
     out = sums[0][0] + met0.astype(F32) + back3.astype(F32) + back1.astype(F32)
     gram = gram_blocks(cap, place, [metas[k] for k in ORDER], [own_part if k == 0 else parts[k] for k in ORDER])

time: 124 us -> 122 us (0.984)
  waiting for transfers between devices: 21.2 us -> 28.4 us
  local copies, waits for them, and re-layouts: 5.95 us -> 2.11 us
  starting transfers between devices: 48.3 us -> 44.8 us
  Pallas kernels: 46.1 us -> 44.1 us
    ppermute x12, waiting for transfers between devices: 6.67 us -> 11.3 us  [over_x(): return lax.ppermute(a, 'expert', ACROSS_X)]
    unnamed x74 -> x38, local copies, waits for them, and re-layouts: 3.93 us -> 0.08 us
    ppermute x6, starting transfers between devices: 16.9 us -> 14.3 us  [over_z(): return lax.ppermute(a, 'expert', planes_up(k % 4))]
    pallas_call x4, Pallas kernels: 28.2 us -> 26.1 us  [hidden_rows(): pl.pallas_call(lambda *a: hidden_kernel(cap, first, *a), out_shape=outs,...]
    ppermute x27, waiting for transfers between devices: 2.53 us -> 4.39 us  [over_core(): return lax.ppermute(a, 'col', CORE)]
  transfers between devices with their start and end apart: 56 -> 56, of which waited for: 17 -> 18; matrix products, arithmetic and copies ran while one was open for 2% -> 2% of each run, Pallas kernels for 36% -> 35%
where the time goes in v4:
time: 122 us
  starting transfers between devices  44.8 us (37%)
  Pallas kernels  44.1 us (36%)
  waiting for transfers between devices  28.4 us (23%)
  local copies, waits for them, and re-layouts  2.11 us (2%)
    pallas_call x4, Pallas kernels, hidden_rows(): pl.pallas_call(lambda *a: hidden_kernel(cap, first, *a), out_shape=outs,...  26.1 us
    ppermute x6, starting transfers between devices, over_z(): return lax.ppermute(a, 'expert', planes_up(k % 4))  14.3 us
    ppermute x12, starting transfers between devices, over_x(): return lax.ppermute(a, 'expert', ACROSS_X)  12.7 us
    ppermute x11, starting transfers between devices, over_y(): return lax.ppermute(a, 'col', ACROSS_Y)  12 us
    ppermute x12, waiting for transfers between devices, over_x(): return lax.ppermute(a, 'expert', ACROSS_X)  11.3 us
    pallas_call x4, Pallas kernels, down_rows(): pl.pallas_call(lambda *a: down_kernel(cap, *a), out_shape=(pltpu.VMEM((ex...  10.7 us
    ppermute x11, waiting for transfers between devices, over_y(): return lax.ppermute(a, 'col', ACROSS_Y)  6.52 us
    ppermute x6, waiting for transfers between devices, over_z(): return lax.ppermute(a, 'expert', planes_up(k % 4))  6.23 us
  transfers between devices with their start and end apart: 56, of which 18 were waited for; matrix products, arithmetic and copies ran while one was open for 2% of the time, Pallas kernels for 35%

profile of v4, /device:TPU:0, one launch (start us, length us, event | category | flops | bytes accessed | tf_op | source)
XLA Modules:
  0.0 121.6 jit_solution(2234151800263167496)
XLA Ops:
  0.6 1.7 %shard_map.95.a_2_ = bf16[144,1024]{1,0:T(8,128)(2,1)S(1)} custom-call(bf16[128,1024]{1,0:T(8,128)(2,1)} %tokens.1, s32[8,128]{1,0:T(8,128)} %bitcast.9, f32[8,128]{1,0:T(8,128)} %bitcast.10, s32[1,128]{1,0:T(1,128)} %bitcast.11), custom_call_target="tpu_custom_call" | custom-call | tf_op jit(solution)/shard_map/pallas_call | solution.py:40
  2.8 2.6 %collective-permute-start.1 = (bf16[144,1024]{1,0:T(8,128)(2,1)S(1)}, bf16[144,1024]{1,0:T(8,128)(2,1)S(1)}, u32[]{:S(2)}, u32[]{:S(2)}) collective-permute-start(bf16[144,1024]{1,0:T(8,128)(2,1)S(1)} %shard_map.95.a_2_), channel_id=1, source_target_pairs={{24,0},{28,4},{0,8},{4,12},{8,16},{12,20},{16,24},{20,28},{25,1},{... | collective-permute-start | bytes 884744 | tf_op jit(solution)/shard_map/tok_z3/ppermute | solution.py:287
  8.5 2.2 %collective-permute-start.4 = (bf16[144,1024]{1,0:T(8,128)(2,1)S(1)}, bf16[144,1024]{1,0:T(8,128)(2,1)S(1)}, u32[]{:S(2)}, u32[]{:S(2)}) collective-permute-start(bf16[144,1024]{1,0:T(8,128)(2,1)S(1)} %shard_map.95.a_2_), channel_id=1, source_target_pairs={{8,0},{12,4},{16,8},{20,12},{24,16},{28,20},{0,24},{4,28},{9,1},{1... | collective-permute-start | bytes 884744 | tf_op jit(solution)/shard_map/tok_z1/ppermute | solution.py:287
  11.4 4.0 %collective-permute-done.1.a_2_ = bf16[144,1024]{1,0:T(8,128)(2,1)S(1)} collective-permute-done((bf16[144,1024]{1,0:T(8,128)(2,1)S(1)}, bf16[144,1024]{1,0:T(8,128)(2,1)S(1)}, u32[]{:S(2)}, u32[]{:S(2)}) %collective-permute-start.1) | collective-permute-done | bytes 294944 | tf_op jit(solution)/shard_map/tok_z3/ppermute | solution.py:287
  15.8 1.6 %collective-permute-start.7 = (bf16[144,1024]{1,0:T(8,128)(2,1)S(1)}, bf16[144,1024]{1,0:T(8,128)(2,1)}, u32[]{:S(2)}, u32[]{:S(2)}) collective-permute-start(bf16[144,1024]{1,0:T(8,128)(2,1)S(1)} %collective-permute-done.1.a_2_), channel_id=1, source_target_pairs={{24,0},{28,4},{0,8},{4,12},{8,16},{12,20},{16,24},{20,28},{25,1},{... | collective-permute-start | bytes 884744 | tf_op jit(solution)/shard_map/tok_z2/ppermute | solution.py:287
  19.4 2.2 %collective-permute-done.4.a_2_ = bf16[144,1024]{1,0:T(8,128)(2,1)S(1)} collective-permute-done((bf16[144,1024]{1,0:T(8,128)(2,1)S(1)}, bf16[144,1024]{1,0:T(8,128)(2,1)S(1)}, u32[]{:S(2)}, u32[]{:S(2)}) %collective-permute-start.4) | collective-permute-done | bytes 294944 | tf_op jit(solution)/shard_map/tok_z1/ppermute | solution.py:287
  21.6 1.6 %collective-permute-start.5 = (bf16[64,1024]{1,0:T(8,128)(2,1)S(1)}, bf16[64,1024]{1,0:T(8,128)(2,1)S(1)}, u32[]{:S(2)}, u32[]{:S(2)}) collective-permute-start(bf16[64,1024]{1,0:T(8,128)(2,1)S(1)} %slice.18), channel_id=1, source_target_pairs={{0,4},{4,0},{8,12},{12,8},{16,20},{20,16},{24,28},{28,24},{1,5},{5... | collective-permute-start | bytes 393224 | tf_op jit(solution)/shard_map/tok_dx0/ppermute | solution.py:282
  24.6 3.2 %collective-permute-done.5.a_5_ = bf16[64,1024]{1,0:T(8,128)(2,1)S(1)} collective-permute-done((bf16[64,1024]{1,0:T(8,128)(2,1)S(1)}, bf16[64,1024]{1,0:T(8,128)(2,1)S(1)}, u32[]{:S(2)}, u32[]{:S(2)}) %collective-permute-start.5) | collective-permute-done | bytes 131104 | tf_op jit(solution)/shard_map/tok_dx0/ppermute | solution.py:282
  34.5 8.8 %shard_map.96 = (bf16[2,192,384]{2,1,0:T(8,128)(2,1)S(1)}, f32[2,8,128]{2,1,0:T(8,128)S(1)}, bf16[2,384,4096]{2,1,0:T(8,128)(2,1)S(1)}, bf16[2,384,4096]{2,1,0:T(8,128)(2,1)S(1)}) custom-call(s32[2]{0:T(128)S(1)} %pad_add_fusion.a_0_, f32[1,128]{1,0:T(1,128)S(1)} %pad_bitcast_fusion.a_1_, bf16[144,1024]{1,0:T(8,128)(2,1)} %copy-done, ...), custom_call_target="tpu_custom_call" | custom-call | tf_op jit(solution)/shard_map/pallas_call | solution.py:153
  49.6 5.8 %shard_map.97 = (bf16[2,192,384]{2,1,0:T(8,128)(2,1)S(1)}, f32[2,8,128]{2,1,0:T(8,128)S(1)}) custom-call(s32[2]{0:T(128)S(1)} %pad_add_fusion.a_0_, f32[1,128]{1,0:T(1,128)S(1)} %pad_bitcast_fusion.a_1_, bf16[144,1024]{1,0:T(8,128)(2,1)} %copy-done.8, bf16[144,1024]{1,0:T(8,128)(2,1)} %copy-done.3, bf16[144,1024]{1,0:T(8,128)(2,1)} %copy-done.4, ...), custom_call_target="tpu_custom_call" | custom-call | tf_op jit(solution)/shard_map/pallas_call | solution.py:153
  55.4 1.9 %collective-permute-done.23.a_5_ = bf16[64,1024]{1,0:T(8,128)(2,1)S(1)} collective-permute-done((bf16[64,1024]{1,0:T(8,128)(2,1)S(1)}, bf16[64,1024]{1,0:T(8,128)(2,1)S(1)}, u32[]{:S(2)}, u32[]{:S(2)}) %collective-permute-start.23) | collective-permute-done | bytes 131104 | tf_op jit(solution)/shard_map/tok_dx2/ppermute | solution.py:282
  64.3 5.8 %shard_map.98 = (bf16[2,192,384]{2,1,0:T(8,128)(2,1)S(1)}, f32[2,8,128]{2,1,0:T(8,128)S(1)}) custom-call(s32[2]{0:T(128)S(1)} %pad_add_fusion.a_0_, f32[1,128]{1,0:T(1,128)S(1)} %pad_bitcast_fusion.a_1_, bf16[144,1024]{1,0:T(8,128)(2,1)} %collective-permute-done.7.a_2_, bf16[144,1024]{1,0:T(8,128)(2,1)} %copy-done.1, bf16[144,1024]{1,0:T(8,128)(2,1)} %copy-done.2, ...), custom_call_target="tpu_custom_call" | custom-call | tf_op jit(solution)/shard_map/pallas_call | solution.py:153
  74.2 2.8 %shard_map.100 = (bf16[2,192,1536]{2,1,0:T(8,128)(2,1)S(1)}, f32[128,1024]{1,0:T(8,128)S(1)}, bf16[128,1024]{1,0:T(8,128)(2,1)S(1)}) custom-call(s32[2]{0:T(128)S(1)} %pad_add_fusion.a_0_, f32[2,8,128]{2,1,0:T(8,128)S(1)} %get-tuple-element.149.a_1_.a_2_, bf16[2,192,384]{2,1,0:T(8,128)(2,1)S(1)} %get-tuple-element.150.a_2_, ...), custom_call_target="tpu_custom_call" | custom-call | tf_op jit(solution)/shard_map/pallas_call | solution.py:195
  77.0 5.7 %shard_map.99 = (bf16[2,192,384]{2,1,0:T(8,128)(2,1)S(1)}, f32[2,8,128]{2,1,0:T(8,128)S(1)}) custom-call(s32[2]{0:T(128)S(1)} %pad_add_fusion.a_0_, f32[1,128]{1,0:T(1,128)S(1)} %pad_bitcast_fusion.a_1_, bf16[144,1024]{1,0:T(8,128)(2,1)} %copy-done.7, bf16[144,1024]{1,0:T(8,128)(2,1)} %copy-done.10, bf16[144,1024]{1,0:T(8,128)(2,1)} %copy-done.11, ...), custom_call_target="tpu_custom_call" | custom-call | tf_op jit(solution)/shard_map/pallas_call | solution.py:153
  84.9 2.6 %shard_map.101 = (bf16[2,192,1536]{2,1,0:T(8,128)(2,1)S(1)}, f32[128,1024]{1,0:T(8,128)S(1)}, bf16[128,1024]{1,0:T(8,128)(2,1)S(1)}) custom-call(s32[2]{0:T(128)S(1)} %pad_add_fusion.a_0_, f32[2,8,128]{2,1,0:T(8,128)S(1)} %get-tuple-element.155.a_1_.a_3_, bf16[2,192,384]{2,1,0:T(8,128)(2,1)S(1)} %get-tuple-element.156.a_2_, ...), custom_call_target="tpu_custom_call" | custom-call | tf_op jit(solution)/shard_map/pallas_call | solution.py:195
  88.6 3.8 %collective-permute-done.47.a_4_ = bf16[2,192,384]{2,1,0:T(8,128)(2,1)S(1)} collective-permute-done((bf16[2,192,384]{2,1,0:T(8,128)(2,1)S(1)}, bf16[2,192,384]{2,1,0:T(8,128)(2,1)S(1)}, u32[]{:S(2)}, u32[]{:S(2)}) %collective-permute-start.47) | collective-permute-done | bytes 294944 | tf_op jit(solution)/shard_map/hid_y1/ppermute | solution.py:277
  94.1 1.8 %collective-permute-done.50 = bf16[128,1024]{1,0:T(8,128)(2,1)S(1)} collective-permute-done((bf16[128,1024]{1,0:T(8,128)(2,1)S(1)}, bf16[128,1024]{1,0:T(8,128)(2,1)S(1)}, u32[]{:S(2)}, u32[]{:S(2)}) %collective-permute-start.50) | collective-permute-done | bytes 262176 | tf_op jit(solution)/shard_map/sum_x2/ppermute | solution.py:282
  96.0 3.7 %collective-permute-start.51 = (bf16[128,1024]{1,0:T(8,128)(2,1)S(1)}, bf16[128,1024]{1,0:T(8,128)(2,1)S(1)}, u32[]{:S(2)}, u32[]{:S(2)}) collective-permute-start(bf16[128,1024]{1,0:T(8,128)(2,1)S(1)} %add_convert_fusion.3), channel_id=1, source_target_pairs={{24,0},{28,4},{0,8},{4,12},{8,16},{12,20},{16,24},{20,28},{25,1},{... | collective-permute-start | bytes 786440 | tf_op jit(solution)/shard_map/sum_z2/ppermute | solution.py:287
  99.7 2.6 %shard_map.103 = (bf16[2,192,1536]{2,1,0:T(8,128)(2,1)S(1)}, f32[128,1024]{1,0:T(8,128)S(1)}, bf16[128,1024]{1,0:T(8,128)(2,1)S(1)}) custom-call(s32[2]{0:T(128)S(1)} %pad_add_fusion.a_0_, f32[2,8,128]{2,1,0:T(8,128)S(1)} %get-tuple-element.161.a_1_.a_4_, bf16[2,192,384]{2,1,0:T(8,128)(2,1)S(1)} %get-tuple-element.162.a_2_, ...), custom_call_target="tpu_custom_call" | custom-call | tf_op jit(solution)/shard_map/pallas_call | solution.py:195
  104.0 2.5 %collective-permute-start.54 = (bf16[128,1024]{1,0:T(8,128)(2,1)S(1)}, bf16[128,1024]{1,0:T(8,128)(2,1)S(1)}, u32[]{:S(2)}, u32[]{:S(2)}) collective-permute-start(bf16[128,1024]{1,0:T(8,128)(2,1)S(1)} %add_convert_fusion.1), channel_id=1, source_target_pairs={{8,0},{12,4},{16,8},{20,12},{24,16},{28,20},{0,24},{4,28},{9,1},{1... | collective-permute-start | bytes 786440 | tf_op jit(solution)/shard_map/sum_z3/ppermute | solution.py:287
  106.5 3.1 %collective-permute-done.49 = bf16[128,1024]{1,0:T(8,128)(2,1)S(1)} collective-permute-done((bf16[128,1024]{1,0:T(8,128)(2,1)S(1)}, bf16[128,1024]{1,0:T(8,128)(2,1)S(1)}, u32[]{:S(2)}, u32[]{:S(2)}) %collective-permute-start.49) | collective-permute-done | bytes 262176 | tf_op jit(solution)/shard_map/sum_x1/ppermute | solution.py:282
  109.7 2.6 %shard_map.102 = (bf16[2,192,1536]{2,1,0:T(8,128)(2,1)S(1)}, f32[128,1024]{1,0:T(8,128)S(1)}, bf16[128,1024]{1,0:T(8,128)(2,1)S(1)}) custom-call(s32[2]{0:T(128)S(1)} %pad_add_fusion.a_0_, f32[2,8,128]{2,1,0:T(8,128)S(1)} %get-tuple-element.105.a_1_, bf16[2,192,384]{2,1,0:T(8,128)(2,1)S(1)} %get-tuple-element.159.a_2_, ...), custom_call_target="tpu_custom_call" | custom-call | tf_op jit(solution)/shard_map/pallas_call | solution.py:195
  112.4 1.6 %collective-permute-start.55 = (bf16[128,1024]{1,0:T(8,128)(2,1)S(1)}, bf16[128,1024]{1,0:T(8,128)(2,1)S(1)}, u32[]{:S(2)}, u32[]{:S(2)}) collective-permute-start(bf16[128,1024]{1,0:T(8,128)(2,1)S(1)} %add_convert_fusion.2), channel_id=1, source_target_pairs={{24,0},{28,4},{0,8},{4,12},{8,16},{12,20},{16,24},{20,28},{25,1},{... | collective-permute-start | bytes 786440 | tf_op jit(solution)/shard_map/sum_z1/ppermute | solution.py:287
  115.0 5.7 %shard_map.104 = f32[2,384,1536]{2,1,0:T(8,128)} custom-call(s32[2]{0:T(128)S(1)} %pad_add_fusion.a_0_, f32[2,8,128]{2,1,0:T(8,128)S(1)} %get-tuple-element.105.a_1_, f32[2,8,128]{2,1,0:T(8,128)S(1)} %get-tuple-element.149.a_1_.a_2_, f32[2,8,128]{2,1,0:T(8,128)S(1)} %get-tuple-element.155.a_1_.a_3_, f32[2,8,128]{2,1,0:T(8,128)S(1)} %get-tuple-element.161.a_1_.a_4_, ...), custom_call_target="tpu_custom_call" | custom-call | tf_op jit(solution)/shard_map/pallas_call | solution.py:246
  (149 shorter events, 40.4 us)
Async XLA Ops:
  2.3 9.1 %collective-permute-start = (bf16[144,1024]{1,0:T(8,128)(2,1)S(1)}, bf16[144,1024]{1,0:T(8,128)(2,1)S(1)}, u32[]{:S(2)}, u32[]{:S(2)}) collective-permute-start(bf16[144,1024]{1,0:T(8,128)(2,1)S(1)} %shard_map.95.a_2_), channel_id=1, source_target_pairs={{0,1},{1,0},{2,3},{3,2},{4,5},{5,4},{6,7},{7,6},{8,9},{9,8},{10,11... | collective-permute-start | bytes 884744 | tf_op jit(solution)/shard_map/tok_c00/ppermute | solution.py:272
  2.8 12.6 %collective-permute-start.1 = (bf16[144,1024]{1,0:T(8,128)(2,1)S(1)}, bf16[144,1024]{1,0:T(8,128)(2,1)S(1)}, u32[]{:S(2)}, u32[]{:S(2)}) collective-permute-start(bf16[144,1024]{1,0:T(8,128)(2,1)S(1)} %shard_map.95.a_2_), channel_id=1, source_target_pairs={{24,0},{28,4},{0,8},{4,12},{8,16},{12,20},{16,24},{20,28},{25,1},{... | collective-permute-start | bytes 884744 | tf_op jit(solution)/shard_map/tok_z3/ppermute | solution.py:287
  5.5 9.9 %collective-permute-start.2 = (bf16[144,1024]{1,0:T(8,128)(2,1)S(1)}, bf16[144,1024]{1,0:T(8,128)(2,1)S(1)}, u32[]{:S(2)}, u32[]{:S(2)}) collective-permute-start(bf16[144,1024]{1,0:T(8,128)(2,1)S(1)} %shard_map.95.a_2_), channel_id=1, source_target_pairs={{0,4},{4,0},{8,12},{12,8},{16,20},{20,16},{24,28},{28,24},{1,5},{5... | collective-permute-start | bytes 884744 | tf_op jit(solution)/shard_map/tok_x0/ppermute | solution.py:282
  8.5 13.2 %collective-permute-start.4 = (bf16[144,1024]{1,0:T(8,128)(2,1)S(1)}, bf16[144,1024]{1,0:T(8,128)(2,1)S(1)}, u32[]{:S(2)}, u32[]{:S(2)}) collective-permute-start(bf16[144,1024]{1,0:T(8,128)(2,1)S(1)} %shard_map.95.a_2_), channel_id=1, source_target_pairs={{8,0},{12,4},{16,8},{20,12},{24,16},{28,20},{0,24},{4,28},{9,1},{1... | collective-permute-start | bytes 884744 | tf_op jit(solution)/shard_map/tok_z1/ppermute | solution.py:287
  15.8 12.5 %collective-permute-start.7 = (bf16[144,1024]{1,0:T(8,128)(2,1)S(1)}, bf16[144,1024]{1,0:T(8,128)(2,1)}, u32[]{:S(2)}, u32[]{:S(2)}) collective-permute-start(bf16[144,1024]{1,0:T(8,128)(2,1)S(1)} %collective-permute-done.1.a_2_), channel_id=1, source_target_pairs={{24,0},{28,4},{0,8},{4,12},{8,16},{12,20},{16,24},{20,28},{25,1},{... | collective-permute-start | bytes 884744 | tf_op jit(solution)/shard_map/tok_z2/ppermute | solution.py:287
  17.3 11.0 %collective-permute-start.8 = (bf16[144,1024]{1,0:T(8,128)(2,1)S(1)}, bf16[144,1024]{1,0:T(8,128)(2,1)S(1)}, u32[]{:S(2)}, u32[]{:S(2)}) collective-permute-start(bf16[144,1024]{1,0:T(8,128)(2,1)S(1)} %collective-permute-done.1.a_2_), channel_id=1, source_target_pairs={{0,4},{4,0},{8,12},{12,8},{16,20},{20,16},{24,28},{28,24},{1,5},{5... | collective-permute-start | bytes 884744 | tf_op jit(solution)/shard_map/tok_x3/ppermute | solution.py:282
  17.9 10.5 %collective-permute-start.9 = (bf16[144,1024]{1,0:T(8,128)(2,1)S(1)}, bf16[144,1024]{1,0:T(8,128)(2,1)S(1)}, u32[]{:S(2)}, u32[]{:S(2)}) collective-permute-start(bf16[144,1024]{1,0:T(8,128)(2,1)S(1)} %collective-permute-done.1.a_2_), channel_id=1, source_target_pairs={{0,2},{1,3},{2,0},{3,1},{4,6},{5,7},{6,4},{7,5},{8,10},{9,11},{10,... | collective-permute-start | bytes 884744 | tf_op jit(solution)/shard_map/tok_y3/ppermute | solution.py:277
  29.0 14.4 %collective-permute-start.16 = (bf16[144,1024]{1,0:T(8,128)(2,1)}, bf16[144,1024]{1,0:T(8,128)(2,1)S(1)}, u32[]{:S(2)}, u32[]{:S(2)}) collective-permute-start(bf16[144,1024]{1,0:T(8,128)(2,1)} %collective-permute-done.7.a_2_), channel_id=1, source_target_pairs={{0,4},{4,0},{8,12},{12,8},{16,20},{20,16},{24,28},{28,24},{1,5},{5... | collective-permute-start | bytes 884744 | tf_op jit(solution)/shard_map/tok_x2/ppermute | solution.py:282
  30.2 13.1 %collective-permute-start.17 = (bf16[144,1024]{1,0:T(8,128)(2,1)}, bf16[144,1024]{1,0:T(8,128)(2,1)S(1)}, u32[]{:S(2)}, u32[]{:S(2)}) collective-permute-start(bf16[144,1024]{1,0:T(8,128)(2,1)} %collective-permute-done.7.a_2_), channel_id=1, source_target_pairs={{0,2},{1,3},{2,0},{3,1},{4,6},{5,7},{6,4},{7,5},{8,10},{9,11},{10,... | collective-permute-start | bytes 884744 | tf_op jit(solution)/shard_map/tok_y2/ppermute | solution.py:277
  33.1 10.2 %collective-permute-start.14 = (bf16[64,1024]{1,0:T(8,128)(2,1)}, bf16[64,1024]{1,0:T(8,128)(2,1)}, u32[]{:S(2)}, u32[]{:S(2)}) collective-permute-start(bf16[64,1024]{1,0:T(8,128)(2,1)} %slice.20), channel_id=1, source_target_pairs={{0,4},{4,0},{8,12},{12,8},{16,20},{20,16},{24,28},{28,24},{1,5},{5... | collective-permute-start | bytes 393224 | tf_op jit(solution)/shard_map/tok_dx3/ppermute | solution.py:282
  33.8 9.6 %collective-permute-start.15 = (bf16[64,1024]{1,0:T(8,128)(2,1)}, bf16[64,1024]{1,0:T(8,128)(2,1)}, u32[]{:S(2)}, u32[]{:S(2)}) collective-permute-start(bf16[64,1024]{1,0:T(8,128)(2,1)} %slice.21), channel_id=1, source_target_pairs={{0,2},{1,3},{2,0},{3,1},{4,6},{5,7},{6,4},{7,5},{8,10},{9,11},{10,... | collective-permute-start | bytes 393224 | tf_op jit(solution)/shard_map/tok_dy3/ppermute | solution.py:277
  45.5 12.8 %collective-permute-start.25 = (bf16[144,1024]{1,0:T(8,128)(2,1)S(1)}, bf16[144,1024]{1,0:T(8,128)(2,1)S(1)}, u32[]{:S(2)}, u32[]{:S(2)}) collective-permute-start(bf16[144,1024]{1,0:T(8,128)(2,1)S(1)} %collective-permute-done.4.a_2_), channel_id=1, source_target_pairs={{0,4},{4,0},{8,12},{12,8},{16,20},{20,16},{24,28},{28,24},{1,5},{5... | collective-permute-start | bytes 884744 | tf_op jit(solution)/shard_map/tok_x1/ppermute | solution.py:282
  46.7 11.6 %collective-permute-start.26 = (bf16[144,1024]{1,0:T(8,128)(2,1)S(1)}, bf16[144,1024]{1,0:T(8,128)(2,1)S(1)}, u32[]{:S(2)}, u32[]{:S(2)}) collective-permute-start(bf16[144,1024]{1,0:T(8,128)(2,1)S(1)} %collective-permute-done.4.a_2_), channel_id=1, source_target_pairs={{0,2},{1,3},{2,0},{3,1},{4,6},{5,7},{6,4},{7,5},{8,10},{9,11},{10,... | collective-permute-start | bytes 884744 | tf_op jit(solution)/shard_map/tok_y1/ppermute | solution.py:277
  48.3 9.1 %collective-permute-start.23 = (bf16[64,1024]{1,0:T(8,128)(2,1)S(1)}, bf16[64,1024]{1,0:T(8,128)(2,1)S(1)}, u32[]{:S(2)}, u32[]{:S(2)}) collective-permute-start(bf16[64,1024]{1,0:T(8,128)(2,1)S(1)} %slice.22), channel_id=1, source_target_pairs={{0,4},{4,0},{8,12},{12,8},{16,20},{20,16},{24,28},{28,24},{1,5},{5... | collective-permute-start | bytes 393224 | tf_op jit(solution)/shard_map/tok_dx2/ppermute | solution.py:282
  49.0 9.3 %collective-permute-start.24 = (bf16[64,1024]{1,0:T(8,128)(2,1)S(1)}, bf16[64,1024]{1,0:T(8,128)(2,1)S(1)}, u32[]{:S(2)}, u32[]{:S(2)}) collective-permute-start(bf16[64,1024]{1,0:T(8,128)(2,1)S(1)} %slice.23), channel_id=1, source_target_pairs={{0,2},{1,3},{2,0},{3,1},{4,6},{5,7},{6,4},{7,5},{8,10},{9,11},{10,... | collective-permute-start | bytes 393224 | tf_op jit(solution)/shard_map/tok_dy2/ppermute | solution.py:277
  61.0 9.1 %collective-permute-start.27 = (bf16[144,1024]{1,0:T(8,128)(2,1)S(1)}, bf16[144,1024]{1,0:T(8,128)(2,1)S(1)}, u32[]{:S(2)}, u32[]{:S(2)}) collective-permute-start(bf16[144,1024]{1,0:T(8,128)(2,1)S(1)} %collective-permute-done.4.a_2_), channel_id=1, source_target_pairs={{0,1},{1,0},{2,3},{3,2},{4,5},{5,4},{6,7},{7,6},{8,9},{9,8},{10,11... | collective-permute-start | bytes 884744 | tf_op jit(solution)/shard_map/tok_c01/ppermute | solution.py:272
  61.7 9.2 %collective-permute-start.35 = (bf16[2,192,384]{2,1,0:T(8,128)(2,1)S(1)}, bf16[2,192,384]{2,1,0:T(8,128)(2,1)S(1)}, u32[]{:S(2)}, u32[]{:S(2)}) collective-permute-start(bf16[2,192,384]{2,1,0:T(8,128)(2,1)S(1)} %get-tuple-element.150.a_2_), channel_id=1, source_target_pairs={{0,2},{1,3},{2,0},{3,1},{4,6},{5,7},{6,4},{7,5},{8,10},{9,11},{10,... | collective-permute-start | bytes 884744 | tf_op jit(solution)/shard_map/hid_y3/ppermute | solution.py:277
  72.7 10.1 %collective-permute-start.38 = (bf16[2,192,384]{2,1,0:T(8,128)(2,1)S(1)}, bf16[2,192,384]{2,1,0:T(8,128)(2,1)S(1)}, u32[]{:S(2)}, u32[]{:S(2)}) collective-permute-start(bf16[2,192,384]{2,1,0:T(8,128)(2,1)S(1)} %get-tuple-element.156.a_2_), channel_id=1, source_target_pairs={{0,2},{1,3},{2,0},{3,1},{4,6},{5,7},{6,4},{7,5},{8,10},{9,11},{10,... | collective-permute-start | bytes 884744 | tf_op jit(solution)/shard_map/hid_y2/ppermute | solution.py:277
  83.4 9.1 %collective-permute-start.47 = (bf16[2,192,384]{2,1,0:T(8,128)(2,1)S(1)}, bf16[2,192,384]{2,1,0:T(8,128)(2,1)S(1)}, u32[]{:S(2)}, u32[]{:S(2)}) collective-permute-start(bf16[2,192,384]{2,1,0:T(8,128)(2,1)S(1)} %get-tuple-element.162.a_2_), channel_id=1, source_target_pairs={{0,2},{1,3},{2,0},{3,1},{4,6},{5,7},{6,4},{7,5},{8,10},{9,11},{10,... | collective-permute-start | bytes 884744 | tf_op jit(solution)/shard_map/hid_y1/ppermute | solution.py:277
  88.6 11.1 %collective-permute-start.46 = (bf16[2,192,384]{2,1,0:T(8,128)(2,1)S(1)}, bf16[2,192,384]{2,1,0:T(8,128)(2,1)S(1)}, u32[]{:S(2)}, u32[]{:S(2)}) collective-permute-start(bf16[2,192,384]{2,1,0:T(8,128)(2,1)S(1)} %get-tuple-element.162.a_2_), channel_id=1, source_target_pairs={{0,1},{1,0},{2,3},{3,2},{4,5},{5,4},{6,7},{7,6},{8,9},{9,8},{10,11... | collective-permute-start | bytes 884744 | tf_op jit(solution)/shard_map/hid_c1/ppermute | solution.py:272
  92.4 10.9 %collective-permute-start.44 = (bf16[2,192,384]{2,1,0:T(8,128)(2,1)S(1)}, bf16[2,192,384]{2,1,0:T(8,128)(2,1)S(1)}, u32[]{:S(2)}, u32[]{:S(2)}) collective-permute-start(bf16[2,192,384]{2,1,0:T(8,128)(2,1)S(1)} %get-tuple-element.159.a_2_), channel_id=1, source_target_pairs={{0,2},{1,3},{2,0},{3,1},{4,6},{5,7},{6,4},{7,5},{8,10},{9,11},{10,... | collective-permute-start | bytes 884744 | tf_op jit(solution)/shard_map/hid_y0/ppermute | solution.py:277
  93.1 10.8 %collective-permute-start.53 = (bf16[128,1024]{1,0:T(8,128)(2,1)S(1)}, bf16[128,1024]{1,0:T(8,128)(2,1)S(1)}, u32[]{:S(2)}, u32[]{:S(2)}) collective-permute-start(bf16[128,1024]{1,0:T(8,128)(2,1)S(1)} %get-tuple-element.170), channel_id=1, source_target_pairs={{0,4},{4,0},{8,12},{12,8},{16,20},{20,16},{24,28},{28,24},{1,5},{5... | collective-permute-start | bytes 786440 | tf_op jit(solution)/shard_map/sum_x3/ppermute | solution.py:282
  96.0 10.5 %collective-permute-start.51 = (bf16[128,1024]{1,0:T(8,128)(2,1)S(1)}, bf16[128,1024]{1,0:T(8,128)(2,1)S(1)}, u32[]{:S(2)}, u32[]{:S(2)}) collective-permute-start(bf16[128,1024]{1,0:T(8,128)(2,1)S(1)} %add_convert_fusion.3), channel_id=1, source_target_pairs={{24,0},{28,4},{0,8},{4,12},{8,16},{12,20},{16,24},{20,28},{25,1},{... | collective-permute-start | bytes 786440 | tf_op jit(solution)/shard_map/sum_z2/ppermute | solution.py:287
  104.0 16.8 %collective-permute-start.54 = (bf16[128,1024]{1,0:T(8,128)(2,1)S(1)}, bf16[128,1024]{1,0:T(8,128)(2,1)S(1)}, u32[]{:S(2)}, u32[]{:S(2)}) collective-permute-start(bf16[128,1024]{1,0:T(8,128)(2,1)S(1)} %add_convert_fusion.1), channel_id=1, source_target_pairs={{8,0},{12,4},{16,8},{20,12},{24,16},{28,20},{0,24},{4,28},{9,1},{1... | collective-permute-start | bytes 786440 | tf_op jit(solution)/shard_map/sum_z3/ppermute | solution.py:287
  (51 other events, 435.2 us)

commit v5 on v4

--- a/solution.py
+++ b/solution.py
@@ -160,17 +160,12 @@
     )(place, lang_row, *map(in_hbm, pieces[: len(pieces) // 2]), *map(held, pieces[len(pieces) // 2 :]), where(w_gate), where(w_up))
 
 
-def down_kernel(cap, place, meta, made, made_c, made_y, made_d, w_down, rows, own, other, total, sems):
+def down_kernel(cap, place, meta, made, made_c, made_y, made_d, w_down, rows, own, other, total):
     units = made.shape[2]
     tok = meta.shape[2]
-    copies = []
     for i, src in enumerate((made, made_c, made_y, made_d)):
         at = pl.multiple_of((place[1] ^ i) * units, units)
-        copies.append(pltpu.make_async_copy(src, rows.at[:, :, pl.ds(at, units)], sems.at[i]))
-    for copy in copies:
-        copy.start()
-    for copy in copies:
-        copy.wait()
+        rows[:, :, pl.ds(at, units)] = src[...]
     for e in range(w_down.shape[0]):
         eo = jnp.dot(rows[e], w_down[e], preferred_element_type=F32)
         for b in range(2):
@@ -199,11 +194,11 @@
             pltpu.VMEM((tok, cols), F32),
             pltpu.VMEM((tok, cols), BF16),
         ),
-        in_specs=[SMEM, VMEM] + [ANY] * 4 + [VMEM],
+        in_specs=[SMEM, VMEM] + [VMEM] * 4 + [VMEM],
         out_specs=(VMEM, VMEM, VMEM),
-        scratch_shapes=[pltpu.VMEM((2 * tok, cols), F32), pltpu.SemaphoreType.DMA((4,))],
+        scratch_shapes=[pltpu.VMEM((2 * tok, cols), F32)],
         compiler_params=pltpu.CompilerParams(vmem_limit_bytes=8 * 2**20),
-    )(place, meta, *pieces, held(w_down))
+    )(place, meta, *map(held, pieces), held(w_down))
 
 
 def gram_kernel(cap, place, *refs):

time: 122 us -> 121 us (level)
  no operation moved by 1% of the time
where the time goes in v5:
time: 121 us
  starting transfers between devices  45.1 us (37%)
  Pallas kernels  43.5 us (36%)
  waiting for transfers between devices  28.2 us (23%)
  local copies, waits for them, and re-layouts  2.11 us (2%)
    pallas_call x4, Pallas kernels, hidden_rows(): pl.pallas_call(lambda *a: hidden_kernel(cap, first, *a), out_shape=outs,...  26.1 us
    ppermute x6, starting transfers between devices, over_z(): return lax.ppermute(a, 'expert', planes_up(k % 4))  14.5 us
    ppermute x12, starting transfers between devices, over_x(): return lax.ppermute(a, 'expert', ACROSS_X)  12.8 us
    ppermute x11, starting transfers between devices, over_y(): return lax.ppermute(a, 'col', ACROSS_Y)  12 us
    ppermute x12, waiting for transfers between devices, over_x(): return lax.ppermute(a, 'expert', ACROSS_X)  11 us
    pallas_call x4, Pallas kernels, down_rows(): pl.pallas_call(lambda *a: down_kernel(cap, *a), out_shape=(pltpu.VMEM((ex...  10.1 us
    ppermute x11, waiting for transfers between devices, over_y(): return lax.ppermute(a, 'col', ACROSS_Y)  6.61 us
    ppermute x6, waiting for transfers between devices, over_z(): return lax.ppermute(a, 'expert', planes_up(k % 4))  6.23 us
  transfers between devices with their start and end apart: 56, of which 18 were waited for; matrix products, arithmetic and copies ran while one was open for 2% of the time, Pallas kernels for 35%

profile of v5, /device:TPU:0, one launch (start us, length us, event | category | flops | bytes accessed | tf_op | source)
XLA Modules:
  0.0 121.1 jit_solution(10456770335739217300)
XLA Ops:
  0.6 1.7 %shard_map.95.a_2_ = bf16[144,1024]{1,0:T(8,128)(2,1)S(1)} custom-call(bf16[128,1024]{1,0:T(8,128)(2,1)} %tokens.1, s32[8,128]{1,0:T(8,128)} %bitcast.9, f32[8,128]{1,0:T(8,128)} %bitcast.10, s32[1,128]{1,0:T(1,128)} %bitcast.11), custom_call_target="tpu_custom_call" | custom-call | tf_op jit(solution)/shard_map/pallas_call | solution.py:40
  2.8 2.6 %collective-permute-start.1 = (bf16[144,1024]{1,0:T(8,128)(2,1)S(1)}, bf16[144,1024]{1,0:T(8,128)(2,1)S(1)}, u32[]{:S(2)}, u32[]{:S(2)}) collective-permute-start(bf16[144,1024]{1,0:T(8,128)(2,1)S(1)} %shard_map.95.a_2_), channel_id=1, source_target_pairs={{24,0},{28,4},{0,8},{4,12},{8,16},{12,20},{16,24},{20,28},{25,1},{... | collective-permute-start | bytes 884744 | tf_op jit(solution)/shard_map/tok_z3/ppermute | solution.py:282
  8.5 2.2 %collective-permute-start.4 = (bf16[144,1024]{1,0:T(8,128)(2,1)S(1)}, bf16[144,1024]{1,0:T(8,128)(2,1)S(1)}, u32[]{:S(2)}, u32[]{:S(2)}) collective-permute-start(bf16[144,1024]{1,0:T(8,128)(2,1)S(1)} %shard_map.95.a_2_), channel_id=1, source_target_pairs={{8,0},{12,4},{16,8},{20,12},{24,16},{28,20},{0,24},{4,28},{9,1},{1... | collective-permute-start | bytes 884744 | tf_op jit(solution)/shard_map/tok_z1/ppermute | solution.py:282
  11.4 4.0 %collective-permute-done.1.a_2_ = bf16[144,1024]{1,0:T(8,128)(2,1)S(1)} collective-permute-done((bf16[144,1024]{1,0:T(8,128)(2,1)S(1)}, bf16[144,1024]{1,0:T(8,128)(2,1)S(1)}, u32[]{:S(2)}, u32[]{:S(2)}) %collective-permute-start.1) | collective-permute-done | bytes 294944 | tf_op jit(solution)/shard_map/tok_z3/ppermute | solution.py:282
  15.8 1.6 %collective-permute-start.7 = (bf16[144,1024]{1,0:T(8,128)(2,1)S(1)}, bf16[144,1024]{1,0:T(8,128)(2,1)}, u32[]{:S(2)}, u32[]{:S(2)}) collective-permute-start(bf16[144,1024]{1,0:T(8,128)(2,1)S(1)} %collective-permute-done.1.a_2_), channel_id=1, source_target_pairs={{24,0},{28,4},{0,8},{4,12},{8,16},{12,20},{16,24},{20,28},{25,1},{... | collective-permute-start | bytes 884744 | tf_op jit(solution)/shard_map/tok_z2/ppermute | solution.py:282
  19.4 2.2 %collective-permute-done.4.a_2_ = bf16[144,1024]{1,0:T(8,128)(2,1)S(1)} collective-permute-done((bf16[144,1024]{1,0:T(8,128)(2,1)S(1)}, bf16[144,1024]{1,0:T(8,128)(2,1)S(1)}, u32[]{:S(2)}, u32[]{:S(2)}) %collective-permute-start.4) | collective-permute-done | bytes 294944 | tf_op jit(solution)/shard_map/tok_z1/ppermute | solution.py:282
  21.6 1.6 %collective-permute-start.5 = (bf16[64,1024]{1,0:T(8,128)(2,1)S(1)}, bf16[64,1024]{1,0:T(8,128)(2,1)S(1)}, u32[]{:S(2)}, u32[]{:S(2)}) collective-permute-start(bf16[64,1024]{1,0:T(8,128)(2,1)S(1)} %slice.18), channel_id=1, source_target_pairs={{0,4},{4,0},{8,12},{12,8},{16,20},{20,16},{24,28},{28,24},{1,5},{5... | collective-permute-start | bytes 393224 | tf_op jit(solution)/shard_map/tok_dx0/ppermute | solution.py:277
  24.6 3.2 %collective-permute-done.5.a_5_ = bf16[64,1024]{1,0:T(8,128)(2,1)S(1)} collective-permute-done((bf16[64,1024]{1,0:T(8,128)(2,1)S(1)}, bf16[64,1024]{1,0:T(8,128)(2,1)S(1)}, u32[]{:S(2)}, u32[]{:S(2)}) %collective-permute-start.5) | collective-permute-done | bytes 131104 | tf_op jit(solution)/shard_map/tok_dx0/ppermute | solution.py:277
  34.5 8.8 %shard_map.96 = (bf16[2,192,384]{2,1,0:T(8,128)(2,1)S(1)}, f32[2,8,128]{2,1,0:T(8,128)S(1)}, bf16[2,384,4096]{2,1,0:T(8,128)(2,1)S(1)}, bf16[2,384,4096]{2,1,0:T(8,128)(2,1)S(1)}) custom-call(s32[2]{0:T(128)S(1)} %pad_add_fusion.a_0_, f32[1,128]{1,0:T(1,128)S(1)} %pad_bitcast_fusion.a_1_, bf16[144,1024]{1,0:T(8,128)(2,1)} %copy-done, ...), custom_call_target="tpu_custom_call" | custom-call | tf_op jit(solution)/shard_map/pallas_call | solution.py:153
  49.6 5.8 %shard_map.97 = (bf16[2,192,384]{2,1,0:T(8,128)(2,1)S(1)}, f32[2,8,128]{2,1,0:T(8,128)S(1)}) custom-call(s32[2]{0:T(128)S(1)} %pad_add_fusion.a_0_, f32[1,128]{1,0:T(1,128)S(1)} %pad_bitcast_fusion.a_1_, bf16[144,1024]{1,0:T(8,128)(2,1)} %copy-done.8, bf16[144,1024]{1,0:T(8,128)(2,1)} %copy-done.3, bf16[144,1024]{1,0:T(8,128)(2,1)} %copy-done.4, ...), custom_call_target="tpu_custom_call" | custom-call | tf_op jit(solution)/shard_map/pallas_call | solution.py:153
  55.4 1.9 %collective-permute-done.23.a_5_ = bf16[64,1024]{1,0:T(8,128)(2,1)S(1)} collective-permute-done((bf16[64,1024]{1,0:T(8,128)(2,1)S(1)}, bf16[64,1024]{1,0:T(8,128)(2,1)S(1)}, u32[]{:S(2)}, u32[]{:S(2)}) %collective-permute-start.23) | collective-permute-done | bytes 131104 | tf_op jit(solution)/shard_map/tok_dx2/ppermute | solution.py:277
  64.3 5.8 %shard_map.98 = (bf16[2,192,384]{2,1,0:T(8,128)(2,1)S(1)}, f32[2,8,128]{2,1,0:T(8,128)S(1)}) custom-call(s32[2]{0:T(128)S(1)} %pad_add_fusion.a_0_, f32[1,128]{1,0:T(1,128)S(1)} %pad_bitcast_fusion.a_1_, bf16[144,1024]{1,0:T(8,128)(2,1)} %collective-permute-done.7.a_2_, bf16[144,1024]{1,0:T(8,128)(2,1)} %copy-done.1, bf16[144,1024]{1,0:T(8,128)(2,1)} %copy-done.2, ...), custom_call_target="tpu_custom_call" | custom-call | tf_op jit(solution)/shard_map/pallas_call | solution.py:153
  74.2 2.5 %shard_map.100 = (bf16[2,192,1536]{2,1,0:T(8,128)(2,1)S(1)}, f32[128,1024]{1,0:T(8,128)S(1)}, bf16[128,1024]{1,0:T(8,128)(2,1)S(1)}) custom-call(s32[2]{0:T(128)S(1)} %pad_add_fusion.a_0_, f32[2,8,128]{2,1,0:T(8,128)S(1)} %get-tuple-element.149.a_1_.a_2_, bf16[2,192,384]{2,1,0:T(8,128)(2,1)S(1)} %get-tuple-element.150.a_2_, ...), custom_call_target="tpu_custom_call" | custom-call | tf_op jit(solution)/shard_map/pallas_call | solution.py:190
  76.8 5.8 %shard_map.99 = (bf16[2,192,384]{2,1,0:T(8,128)(2,1)S(1)}, f32[2,8,128]{2,1,0:T(8,128)S(1)}) custom-call(s32[2]{0:T(128)S(1)} %pad_add_fusion.a_0_, f32[1,128]{1,0:T(1,128)S(1)} %pad_bitcast_fusion.a_1_, bf16[144,1024]{1,0:T(8,128)(2,1)} %copy-done.7, bf16[144,1024]{1,0:T(8,128)(2,1)} %copy-done.10, bf16[144,1024]{1,0:T(8,128)(2,1)} %copy-done.11, ...), custom_call_target="tpu_custom_call" | custom-call | tf_op jit(solution)/shard_map/pallas_call | solution.py:153
  84.6 2.5 %shard_map.101 = (bf16[2,192,1536]{2,1,0:T(8,128)(2,1)S(1)}, f32[128,1024]{1,0:T(8,128)S(1)}, bf16[128,1024]{1,0:T(8,128)(2,1)S(1)}) custom-call(s32[2]{0:T(128)S(1)} %pad_add_fusion.a_0_, f32[2,8,128]{2,1,0:T(8,128)S(1)} %get-tuple-element.155.a_1_.a_3_, bf16[2,192,384]{2,1,0:T(8,128)(2,1)S(1)} %get-tuple-element.156.a_2_, ...), custom_call_target="tpu_custom_call" | custom-call | tf_op jit(solution)/shard_map/pallas_call | solution.py:190
  88.2 3.9 %collective-permute-done.47.a_4_ = bf16[2,192,384]{2,1,0:T(8,128)(2,1)S(1)} collective-permute-done((bf16[2,192,384]{2,1,0:T(8,128)(2,1)S(1)}, bf16[2,192,384]{2,1,0:T(8,128)(2,1)S(1)}, u32[]{:S(2)}, u32[]{:S(2)}) %collective-permute-start.47) | collective-permute-done | bytes 294944 | tf_op jit(solution)/shard_map/hid_y1/ppermute | solution.py:272
  93.9 1.7 %collective-permute-done.50 = bf16[128,1024]{1,0:T(8,128)(2,1)S(1)} collective-permute-done((bf16[128,1024]{1,0:T(8,128)(2,1)S(1)}, bf16[128,1024]{1,0:T(8,128)(2,1)S(1)}, u32[]{:S(2)}, u32[]{:S(2)}) %collective-permute-start.50) | collective-permute-done | bytes 262176 | tf_op jit(solution)/shard_map/sum_x2/ppermute | solution.py:277
  95.6 3.7 %collective-permute-start.51 = (bf16[128,1024]{1,0:T(8,128)(2,1)S(1)}, bf16[128,1024]{1,0:T(8,128)(2,1)S(1)}, u32[]{:S(2)}, u32[]{:S(2)}) collective-permute-start(bf16[128,1024]{1,0:T(8,128)(2,1)S(1)} %add_convert_fusion.3), channel_id=1, source_target_pairs={{24,0},{28,4},{0,8},{4,12},{8,16},{12,20},{16,24},{20,28},{25,1},{... | collective-permute-start | bytes 786440 | tf_op jit(solution)/shard_map/sum_z2/ppermute | solution.py:282
  99.3 2.5 %shard_map.103 = (bf16[2,192,1536]{2,1,0:T(8,128)(2,1)S(1)}, f32[128,1024]{1,0:T(8,128)S(1)}, bf16[128,1024]{1,0:T(8,128)(2,1)S(1)}) custom-call(s32[2]{0:T(128)S(1)} %pad_add_fusion.a_0_, f32[2,8,128]{2,1,0:T(8,128)S(1)} %get-tuple-element.161.a_1_.a_4_, bf16[2,192,384]{2,1,0:T(8,128)(2,1)S(1)} %get-tuple-element.162.a_2_, ...), custom_call_target="tpu_custom_call" | custom-call | tf_op jit(solution)/shard_map/pallas_call | solution.py:190
  103.5 2.7 %collective-permute-start.54 = (bf16[128,1024]{1,0:T(8,128)(2,1)S(1)}, bf16[128,1024]{1,0:T(8,128)(2,1)S(1)}, u32[]{:S(2)}, u32[]{:S(2)}) collective-permute-start(bf16[128,1024]{1,0:T(8,128)(2,1)S(1)} %add_convert_fusion.1), channel_id=1, source_target_pairs={{8,0},{12,4},{16,8},{20,12},{24,16},{28,20},{0,24},{4,28},{9,1},{1... | collective-permute-start | bytes 786440 | tf_op jit(solution)/shard_map/sum_z3/ppermute | solution.py:282
  106.2 2.9 %collective-permute-done.49 = bf16[128,1024]{1,0:T(8,128)(2,1)S(1)} collective-permute-done((bf16[128,1024]{1,0:T(8,128)(2,1)S(1)}, bf16[128,1024]{1,0:T(8,128)(2,1)S(1)}, u32[]{:S(2)}, u32[]{:S(2)}) %collective-permute-start.49) | collective-permute-done | bytes 262176 | tf_op jit(solution)/shard_map/sum_x1/ppermute | solution.py:277
  109.2 2.5 %shard_map.102 = (bf16[2,192,1536]{2,1,0:T(8,128)(2,1)S(1)}, f32[128,1024]{1,0:T(8,128)S(1)}, bf16[128,1024]{1,0:T(8,128)(2,1)S(1)}) custom-call(s32[2]{0:T(128)S(1)} %pad_add_fusion.a_0_, f32[2,8,128]{2,1,0:T(8,128)S(1)} %get-tuple-element.105.a_1_, bf16[2,192,384]{2,1,0:T(8,128)(2,1)S(1)} %get-tuple-element.159.a_2_, ...), custom_call_target="tpu_custom_call" | custom-call | tf_op jit(solution)/shard_map/pallas_call | solution.py:190
  111.8 1.7 %collective-permute-start.55 = (bf16[128,1024]{1,0:T(8,128)(2,1)S(1)}, bf16[128,1024]{1,0:T(8,128)(2,1)S(1)}, u32[]{:S(2)}, u32[]{:S(2)}) collective-permute-start(bf16[128,1024]{1,0:T(8,128)(2,1)S(1)} %add_convert_fusion.2), channel_id=1, source_target_pairs={{24,0},{28,4},{0,8},{4,12},{8,16},{12,20},{16,24},{20,28},{25,1},{... | collective-permute-start | bytes 786440 | tf_op jit(solution)/shard_map/sum_z1/ppermute | solution.py:282
  114.5 5.7 %shard_map.104 = f32[2,384,1536]{2,1,0:T(8,128)} custom-call(s32[2]{0:T(128)S(1)} %pad_add_fusion.a_0_, f32[2,8,128]{2,1,0:T(8,128)S(1)} %get-tuple-element.105.a_1_, f32[2,8,128]{2,1,0:T(8,128)S(1)} %get-tuple-element.149.a_1_.a_2_, f32[2,8,128]{2,1,0:T(8,128)S(1)} %get-tuple-element.155.a_1_.a_3_, f32[2,8,128]{2,1,0:T(8,128)S(1)} %get-tuple-element.161.a_1_.a_4_, ...), custom_call_target="tpu_custom_call" | custom-call | tf_op jit(solution)/shard_map/pallas_call | solution.py:241
  (149 shorter events, 40.5 us)
Async XLA Ops:
  2.3 9.1 %collective-permute-start = (bf16[144,1024]{1,0:T(8,128)(2,1)S(1)}, bf16[144,1024]{1,0:T(8,128)(2,1)S(1)}, u32[]{:S(2)}, u32[]{:S(2)}) collective-permute-start(bf16[144,1024]{1,0:T(8,128)(2,1)S(1)} %shard_map.95.a_2_), channel_id=1, source_target_pairs={{0,1},{1,0},{2,3},{3,2},{4,5},{5,4},{6,7},{7,6},{8,9},{9,8},{10,11... | collective-permute-start | bytes 884744 | tf_op jit(solution)/shard_map/tok_c00/ppermute | solution.py:267
  2.8 12.6 %collective-permute-start.1 = (bf16[144,1024]{1,0:T(8,128)(2,1)S(1)}, bf16[144,1024]{1,0:T(8,128)(2,1)S(1)}, u32[]{:S(2)}, u32[]{:S(2)}) collective-permute-start(bf16[144,1024]{1,0:T(8,128)(2,1)S(1)} %shard_map.95.a_2_), channel_id=1, source_target_pairs={{24,0},{28,4},{0,8},{4,12},{8,16},{12,20},{16,24},{20,28},{25,1},{... | collective-permute-start | bytes 884744 | tf_op jit(solution)/shard_map/tok_z3/ppermute | solution.py:282
  5.5 9.9 %collective-permute-start.2 = (bf16[144,1024]{1,0:T(8,128)(2,1)S(1)}, bf16[144,1024]{1,0:T(8,128)(2,1)S(1)}, u32[]{:S(2)}, u32[]{:S(2)}) collective-permute-start(bf16[144,1024]{1,0:T(8,128)(2,1)S(1)} %shard_map.95.a_2_), channel_id=1, source_target_pairs={{0,4},{4,0},{8,12},{12,8},{16,20},{20,16},{24,28},{28,24},{1,5},{5... | collective-permute-start | bytes 884744 | tf_op jit(solution)/shard_map/tok_x0/ppermute | solution.py:277
  8.5 13.2 %collective-permute-start.4 = (bf16[144,1024]{1,0:T(8,128)(2,1)S(1)}, bf16[144,1024]{1,0:T(8,128)(2,1)S(1)}, u32[]{:S(2)}, u32[]{:S(2)}) collective-permute-start(bf16[144,1024]{1,0:T(8,128)(2,1)S(1)} %shard_map.95.a_2_), channel_id=1, source_target_pairs={{8,0},{12,4},{16,8},{20,12},{24,16},{28,20},{0,24},{4,28},{9,1},{1... | collective-permute-start | bytes 884744 | tf_op jit(solution)/shard_map/tok_z1/ppermute | solution.py:282
  15.8 12.5 %collective-permute-start.7 = (bf16[144,1024]{1,0:T(8,128)(2,1)S(1)}, bf16[144,1024]{1,0:T(8,128)(2,1)}, u32[]{:S(2)}, u32[]{:S(2)}) collective-permute-start(bf16[144,1024]{1,0:T(8,128)(2,1)S(1)} %collective-permute-done.1.a_2_), channel_id=1, source_target_pairs={{24,0},{28,4},{0,8},{4,12},{8,16},{12,20},{16,24},{20,28},{25,1},{... | collective-permute-start | bytes 884744 | tf_op jit(solution)/shard_map/tok_z2/ppermute | solution.py:282
  17.3 11.0 %collective-permute-start.8 = (bf16[144,1024]{1,0:T(8,128)(2,1)S(1)}, bf16[144,1024]{1,0:T(8,128)(2,1)S(1)}, u32[]{:S(2)}, u32[]{:S(2)}) collective-permute-start(bf16[144,1024]{1,0:T(8,128)(2,1)S(1)} %collective-permute-done.1.a_2_), channel_id=1, source_target_pairs={{0,4},{4,0},{8,12},{12,8},{16,20},{20,16},{24,28},{28,24},{1,5},{5... | collective-permute-start | bytes 884744 | tf_op jit(solution)/shard_map/tok_x3/ppermute | solution.py:277
  17.9 10.5 %collective-permute-start.9 = (bf16[144,1024]{1,0:T(8,128)(2,1)S(1)}, bf16[144,1024]{1,0:T(8,128)(2,1)S(1)}, u32[]{:S(2)}, u32[]{:S(2)}) collective-permute-start(bf16[144,1024]{1,0:T(8,128)(2,1)S(1)} %collective-permute-done.1.a_2_), channel_id=1, source_target_pairs={{0,2},{1,3},{2,0},{3,1},{4,6},{5,7},{6,4},{7,5},{8,10},{9,11},{10,... | collective-permute-start | bytes 884744 | tf_op jit(solution)/shard_map/tok_y3/ppermute | solution.py:272
  29.0 14.4 %collective-permute-start.16 = (bf16[144,1024]{1,0:T(8,128)(2,1)}, bf16[144,1024]{1,0:T(8,128)(2,1)S(1)}, u32[]{:S(2)}, u32[]{:S(2)}) collective-permute-start(bf16[144,1024]{1,0:T(8,128)(2,1)} %collective-permute-done.7.a_2_), channel_id=1, source_target_pairs={{0,4},{4,0},{8,12},{12,8},{16,20},{20,16},{24,28},{28,24},{1,5},{5... | collective-permute-start | bytes 884744 | tf_op jit(solution)/shard_map/tok_x2/ppermute | solution.py:277
  30.2 13.1 %collective-permute-start.17 = (bf16[144,1024]{1,0:T(8,128)(2,1)}, bf16[144,1024]{1,0:T(8,128)(2,1)S(1)}, u32[]{:S(2)}, u32[]{:S(2)}) collective-permute-start(bf16[144,1024]{1,0:T(8,128)(2,1)} %collective-permute-done.7.a_2_), channel_id=1, source_target_pairs={{0,2},{1,3},{2,0},{3,1},{4,6},{5,7},{6,4},{7,5},{8,10},{9,11},{10,... | collective-permute-start | bytes 884744 | tf_op jit(solution)/shard_map/tok_y2/ppermute | solution.py:272
  33.1 10.2 %collective-permute-start.14 = (bf16[64,1024]{1,0:T(8,128)(2,1)}, bf16[64,1024]{1,0:T(8,128)(2,1)}, u32[]{:S(2)}, u32[]{:S(2)}) collective-permute-start(bf16[64,1024]{1,0:T(8,128)(2,1)} %slice.20), channel_id=1, source_target_pairs={{0,4},{4,0},{8,12},{12,8},{16,20},{20,16},{24,28},{28,24},{1,5},{5... | collective-permute-start | bytes 393224 | tf_op jit(solution)/shard_map/tok_dx3/ppermute | solution.py:277
  33.8 9.6 %collective-permute-start.15 = (bf16[64,1024]{1,0:T(8,128)(2,1)}, bf16[64,1024]{1,0:T(8,128)(2,1)}, u32[]{:S(2)}, u32[]{:S(2)}) collective-permute-start(bf16[64,1024]{1,0:T(8,128)(2,1)} %slice.21), channel_id=1, source_target_pairs={{0,2},{1,3},{2,0},{3,1},{4,6},{5,7},{6,4},{7,5},{8,10},{9,11},{10,... | collective-permute-start | bytes 393224 | tf_op jit(solution)/shard_map/tok_dy3/ppermute | solution.py:272
  45.5 12.8 %collective-permute-start.25 = (bf16[144,1024]{1,0:T(8,128)(2,1)S(1)}, bf16[144,1024]{1,0:T(8,128)(2,1)S(1)}, u32[]{:S(2)}, u32[]{:S(2)}) collective-permute-start(bf16[144,1024]{1,0:T(8,128)(2,1)S(1)} %collective-permute-done.4.a_2_), channel_id=1, source_target_pairs={{0,4},{4,0},{8,12},{12,8},{16,20},{20,16},{24,28},{28,24},{1,5},{5... | collective-permute-start | bytes 884744 | tf_op jit(solution)/shard_map/tok_x1/ppermute | solution.py:277
  46.7 11.6 %collective-permute-start.26 = (bf16[144,1024]{1,0:T(8,128)(2,1)S(1)}, bf16[144,1024]{1,0:T(8,128)(2,1)S(1)}, u32[]{:S(2)}, u32[]{:S(2)}) collective-permute-start(bf16[144,1024]{1,0:T(8,128)(2,1)S(1)} %collective-permute-done.4.a_2_), channel_id=1, source_target_pairs={{0,2},{1,3},{2,0},{3,1},{4,6},{5,7},{6,4},{7,5},{8,10},{9,11},{10,... | collective-permute-start | bytes 884744 | tf_op jit(solution)/shard_map/tok_y1/ppermute | solution.py:272
  48.3 9.1 %collective-permute-start.23 = (bf16[64,1024]{1,0:T(8,128)(2,1)S(1)}, bf16[64,1024]{1,0:T(8,128)(2,1)S(1)}, u32[]{:S(2)}, u32[]{:S(2)}) collective-permute-start(bf16[64,1024]{1,0:T(8,128)(2,1)S(1)} %slice.22), channel_id=1, source_target_pairs={{0,4},{4,0},{8,12},{12,8},{16,20},{20,16},{24,28},{28,24},{1,5},{5... | collective-permute-start | bytes 393224 | tf_op jit(solution)/shard_map/tok_dx2/ppermute | solution.py:277
  49.0 9.3 %collective-permute-start.24 = (bf16[64,1024]{1,0:T(8,128)(2,1)S(1)}, bf16[64,1024]{1,0:T(8,128)(2,1)S(1)}, u32[]{:S(2)}, u32[]{:S(2)}) collective-permute-start(bf16[64,1024]{1,0:T(8,128)(2,1)S(1)} %slice.23), channel_id=1, source_target_pairs={{0,2},{1,3},{2,0},{3,1},{4,6},{5,7},{6,4},{7,5},{8,10},{9,11},{10,... | collective-permute-start | bytes 393224 | tf_op jit(solution)/shard_map/tok_dy2/ppermute | solution.py:272
  61.0 9.1 %collective-permute-start.27 = (bf16[144,1024]{1,0:T(8,128)(2,1)S(1)}, bf16[144,1024]{1,0:T(8,128)(2,1)S(1)}, u32[]{:S(2)}, u32[]{:S(2)}) collective-permute-start(bf16[144,1024]{1,0:T(8,128)(2,1)S(1)} %collective-permute-done.4.a_2_), channel_id=1, source_target_pairs={{0,1},{1,0},{2,3},{3,2},{4,5},{5,4},{6,7},{7,6},{8,9},{9,8},{10,11... | collective-permute-start | bytes 884744 | tf_op jit(solution)/shard_map/tok_c01/ppermute | solution.py:267
  61.7 9.2 %collective-permute-start.35 = (bf16[2,192,384]{2,1,0:T(8,128)(2,1)S(1)}, bf16[2,192,384]{2,1,0:T(8,128)(2,1)S(1)}, u32[]{:S(2)}, u32[]{:S(2)}) collective-permute-start(bf16[2,192,384]{2,1,0:T(8,128)(2,1)S(1)} %get-tuple-element.150.a_2_), channel_id=1, source_target_pairs={{0,2},{1,3},{2,0},{3,1},{4,6},{5,7},{6,4},{7,5},{8,10},{9,11},{10,... | collective-permute-start | bytes 884744 | tf_op jit(solution)/shard_map/hid_y3/ppermute | solution.py:272
  72.7 9.8 %collective-permute-start.38 = (bf16[2,192,384]{2,1,0:T(8,128)(2,1)S(1)}, bf16[2,192,384]{2,1,0:T(8,128)(2,1)S(1)}, u32[]{:S(2)}, u32[]{:S(2)}) collective-permute-start(bf16[2,192,384]{2,1,0:T(8,128)(2,1)S(1)} %get-tuple-element.156.a_2_), channel_id=1, source_target_pairs={{0,2},{1,3},{2,0},{3,1},{4,6},{5,7},{6,4},{7,5},{8,10},{9,11},{10,... | collective-permute-start | bytes 884744 | tf_op jit(solution)/shard_map/hid_y2/ppermute | solution.py:272
  83.1 9.1 %collective-permute-start.47 = (bf16[2,192,384]{2,1,0:T(8,128)(2,1)S(1)}, bf16[2,192,384]{2,1,0:T(8,128)(2,1)S(1)}, u32[]{:S(2)}, u32[]{:S(2)}) collective-permute-start(bf16[2,192,384]{2,1,0:T(8,128)(2,1)S(1)} %get-tuple-element.162.a_2_), channel_id=1, source_target_pairs={{0,2},{1,3},{2,0},{3,1},{4,6},{5,7},{6,4},{7,5},{8,10},{9,11},{10,... | collective-permute-start | bytes 884744 | tf_op jit(solution)/shard_map/hid_y1/ppermute | solution.py:272
  88.2 11.1 %collective-permute-start.46 = (bf16[2,192,384]{2,1,0:T(8,128)(2,1)S(1)}, bf16[2,192,384]{2,1,0:T(8,128)(2,1)S(1)}, u32[]{:S(2)}, u32[]{:S(2)}) collective-permute-start(bf16[2,192,384]{2,1,0:T(8,128)(2,1)S(1)} %get-tuple-element.162.a_2_), channel_id=1, source_target_pairs={{0,1},{1,0},{2,3},{3,2},{4,5},{5,4},{6,7},{7,6},{8,9},{9,8},{10,11... | collective-permute-start | bytes 884744 | tf_op jit(solution)/shard_map/hid_c1/ppermute | solution.py:267
  92.2 10.8 %collective-permute-start.44 = (bf16[2,192,384]{2,1,0:T(8,128)(2,1)S(1)}, bf16[2,192,384]{2,1,0:T(8,128)(2,1)S(1)}, u32[]{:S(2)}, u32[]{:S(2)}) collective-permute-start(bf16[2,192,384]{2,1,0:T(8,128)(2,1)S(1)} %get-tuple-element.159.a_2_), channel_id=1, source_target_pairs={{0,2},{1,3},{2,0},{3,1},{4,6},{5,7},{6,4},{7,5},{8,10},{9,11},{10,... | collective-permute-start | bytes 884744 | tf_op jit(solution)/shard_map/hid_y0/ppermute | solution.py:272
  92.8 10.6 %collective-permute-start.53 = (bf16[128,1024]{1,0:T(8,128)(2,1)S(1)}, bf16[128,1024]{1,0:T(8,128)(2,1)S(1)}, u32[]{:S(2)}, u32[]{:S(2)}) collective-permute-start(bf16[128,1024]{1,0:T(8,128)(2,1)S(1)} %get-tuple-element.170), channel_id=1, source_target_pairs={{0,4},{4,0},{8,12},{12,8},{16,20},{20,16},{24,28},{28,24},{1,5},{5... | collective-permute-start | bytes 786440 | tf_op jit(solution)/shard_map/sum_x3/ppermute | solution.py:277
  95.6 10.6 %collective-permute-start.51 = (bf16[128,1024]{1,0:T(8,128)(2,1)S(1)}, bf16[128,1024]{1,0:T(8,128)(2,1)S(1)}, u32[]{:S(2)}, u32[]{:S(2)}) collective-permute-start(bf16[128,1024]{1,0:T(8,128)(2,1)S(1)} %add_convert_fusion.3), channel_id=1, source_target_pairs={{24,0},{28,4},{0,8},{4,12},{8,16},{12,20},{16,24},{20,28},{25,1},{... | collective-permute-start | bytes 786440 | tf_op jit(solution)/shard_map/sum_z2/ppermute | solution.py:282
  103.5 16.7 %collective-permute-start.54 = (bf16[128,1024]{1,0:T(8,128)(2,1)S(1)}, bf16[128,1024]{1,0:T(8,128)(2,1)S(1)}, u32[]{:S(2)}, u32[]{:S(2)}) collective-permute-start(bf16[128,1024]{1,0:T(8,128)(2,1)S(1)} %add_convert_fusion.1), channel_id=1, source_target_pairs={{8,0},{12,4},{16,8},{20,12},{24,16},{28,20},{0,24},{4,28},{9,1},{1... | collective-permute-start | bytes 786440 | tf_op jit(solution)/shard_map/sum_z3/ppermute | solution.py:282
  (51 other events, 434.5 us)

commit v6 on v5

--- a/solution.py
+++ b/solution.py
@@ -94,7 +94,7 @@
     feat = x.shape[1] // 4
     half = len(pieces) // 2
     experts = gate_held.shape[0]
-    copies = []
+    copies, moves = [], []
     for core in range(2):
         row = 0
         for i in range(half):
@@ -106,7 +106,10 @@
             dst = x.at[pl.ds(b * tok + row, src.shape[0]), pl.ds(at, feat)]
             if i >= 3:
                 row += src.shape[0]
-            copies.append(pltpu.make_async_copy(src, dst, sems.at[core * half + i]))
+            if core == 0:
+                copies.append(pltpu.make_async_copy(src, dst, sems.at[i]))
+            else:
+                moves.append((src, dst))
     loads = [[] for _ in range(experts)]
     if first:
         for e in range(experts):
@@ -117,6 +120,8 @@
     ]
     for copy in routes + copies + loads[0]:
         copy.start()
+    for src, dst in moves:
+        dst[...] = src[...]
     for copy in routes + copies + loads[0]:
         copy.wait()
     for later in loads[1:]:
@@ -202,21 +207,10 @@
 
 
 def gram_kernel(cap, place, *refs):
-    planes = len(refs) // 2 - 2
-    metas, parts, (out, rows, scaled, sems) = refs[:planes], refs[planes : 2 * planes], refs[2 * planes :]
+    planes = len(refs) // 2 - 1
+    metas, parts, (out, scaled) = refs[:planes], refs[planes : 2 * planes], refs[2 * planes :]
     units = scaled.shape[1]
     e, n = pl.program_id(0), pl.program_id(1)
-
-    @pl.when((e == 0) & (n == 0))
-    def _():
-        copies = [
-            pltpu.make_async_copy(parts[k], rows.at[:, pl.ds(k * 2 * cap, 2 * cap), :], sems.at[k])
-            for k in range(planes)
-        ]
-        for copy in copies:
-            copy.start()
-        for copy in copies:
-            copy.wait()
 
     @pl.when(n == 0)
     def _():
@@ -226,10 +220,11 @@
                 pick = picks(metas[k][b, pl.ds(e, 1), :], cap)
                 cal = jnp.sum(jnp.where(pick, metas[k][b, 4:5, :], 0.0), axis=1, keepdims=True)
                 at = pl.ds((2 * k + b) * cap, cap)
-                scaled[at, :] = (rows[e, at, mine].astype(F32) * cal).astype(BF16)
+                scaled[at, :] = (parts[k][e, pl.ds(b * cap, cap), mine].astype(F32) * cal).astype(BF16)
 
     width = out.shape[2]
-    right = rows[e, :, pl.ds(pl.multiple_of(n * width, width), width)]
+    columns = pl.ds(pl.multiple_of(n * width, width), width)
+    right = jnp.concatenate([part[e, :, columns] for part in parts], axis=0)
     out[0] = lax.dot_general(scaled[...], right, (((0,), (0,)), ((), ())), preferred_element_type=F32)
 
 
@@ -237,20 +232,15 @@
     planes = len(parts)
     experts, _, depth = parts[0].shape
     units = depth // 4
-    total = planes * 2 * cap
     return pl.pallas_call(
         lambda *a: gram_kernel(cap, *a),
         out_shape=jax.ShapeDtypeStruct((experts, units, depth), F32),
         grid=(experts, depth // width),
-        in_specs=[SMEM] + [whole(m.shape) for m in metas] + [ANY] * planes,
+        in_specs=[SMEM] + [VMEM] * (2 * planes),
         out_specs=pl.BlockSpec((1, units, width), lambda e, n: (e, 0, n)),
-        scratch_shapes=[
-            pltpu.VMEM((experts, total, depth), BF16),
-            pltpu.VMEM((total, units), BF16),
-            pltpu.SemaphoreType.DMA((planes,)),
-        ],
-        compiler_params=pltpu.CompilerParams(vmem_limit_bytes=11 * 2**20),
-    )(place, *metas, *parts)
+        scratch_shapes=[pltpu.VMEM((planes * 2 * cap, units), BF16)],
+        compiler_params=pltpu.CompilerParams(vmem_limit_bytes=14 * 2**20),
+    )(place, *metas, *map(held, parts))
 
 
 CORE = [(c, c ^ 1) for c in range(4)]

time: 121 us -> 121 us (level)
  transfers between devices with their start and end apart: 56 -> 56, of which waited for: 18 -> 19; matrix products, arithmetic and copies ran while one was open for 2% -> 2% of each run, Pallas kernels for 35% -> 34%
where the time goes in v6:
time: 121 us
  starting transfers between devices  44.9 us (37%)
  Pallas kernels  42.9 us (35%)
  waiting for transfers between devices  28.9 us (24%)
  local copies, waits for them, and re-layouts  2.11 us (2%)
    pallas_call x4, Pallas kernels, hidden_rows(): pl.pallas_call(lambda *a: hidden_kernel(cap, first, *a), out_shape=outs,...  25.9 us
    ppermute x6, starting transfers between devices, over_z(): return lax.ppermute(a, 'expert', planes_up(k % 4))  14.5 us
    ppermute x12, starting transfers between devices, over_x(): return lax.ppermute(a, 'expert', ACROSS_X)  12.7 us
    ppermute x11, starting transfers between devices, over_y(): return lax.ppermute(a, 'col', ACROSS_Y)  12 us
    ppermute x12, waiting for transfers between devices, over_x(): return lax.ppermute(a, 'expert', ACROSS_X)  11 us
    pallas_call x4, Pallas kernels, down_rows(): pl.pallas_call(lambda *a: down_kernel(cap, *a), out_shape=(pltpu.VMEM((ex...  10.3 us
    ppermute x6, waiting for transfers between devices, over_z(): return lax.ppermute(a, 'expert', planes_up(k % 4))  6.89 us
    ppermute x11, waiting for transfers between devices, over_y(): return lax.ppermute(a, 'col', ACROSS_Y)  6.61 us
  transfers between devices with their start and end apart: 56, of which 19 were waited for; matrix products, arithmetic and copies ran while one was open for 2% of the time, Pallas kernels for 34%

profile of v6, /device:TPU:0, one launch (start us, length us, event | category | flops | bytes accessed | tf_op | source)
XLA Modules:
  0.0 121.0 jit_solution(13265281559911135781)
XLA Ops:
  0.6 1.7 %shard_map.95.a_2_ = bf16[144,1024]{1,0:T(8,128)(2,1)S(1)} custom-call(bf16[128,1024]{1,0:T(8,128)(2,1)} %tokens.1, s32[8,128]{1,0:T(8,128)} %bitcast.9, f32[8,128]{1,0:T(8,128)} %bitcast.10, s32[1,128]{1,0:T(1,128)} %bitcast.11), custom_call_target="tpu_custom_call" | custom-call | tf_op jit(solution)/shard_map/pallas_call | solution.py:40
  2.8 2.6 %collective-permute-start.1 = (bf16[144,1024]{1,0:T(8,128)(2,1)S(1)}, bf16[144,1024]{1,0:T(8,128)(2,1)S(1)}, u32[]{:S(2)}, u32[]{:S(2)}) collective-permute-start(bf16[144,1024]{1,0:T(8,128)(2,1)S(1)} %shard_map.95.a_2_), channel_id=1, source_target_pairs={{24,0},{28,4},{0,8},{4,12},{8,16},{12,20},{16,24},{20,28},{25,1},{... | collective-permute-start | bytes 884744 | tf_op jit(solution)/shard_map/tok_z3/ppermute | solution.py:272
  8.5 2.2 %collective-permute-start.4 = (bf16[144,1024]{1,0:T(8,128)(2,1)S(1)}, bf16[144,1024]{1,0:T(8,128)(2,1)S(1)}, u32[]{:S(2)}, u32[]{:S(2)}) collective-permute-start(bf16[144,1024]{1,0:T(8,128)(2,1)S(1)} %shard_map.95.a_2_), channel_id=1, source_target_pairs={{8,0},{12,4},{16,8},{20,12},{24,16},{28,20},{0,24},{4,28},{9,1},{1... | collective-permute-start | bytes 884744 | tf_op jit(solution)/shard_map/tok_z1/ppermute | solution.py:272
  11.4 4.0 %collective-permute-done.1.a_2_ = bf16[144,1024]{1,0:T(8,128)(2,1)S(1)} collective-permute-done((bf16[144,1024]{1,0:T(8,128)(2,1)S(1)}, bf16[144,1024]{1,0:T(8,128)(2,1)S(1)}, u32[]{:S(2)}, u32[]{:S(2)}) %collective-permute-start.1) | collective-permute-done | bytes 294944 | tf_op jit(solution)/shard_map/tok_z3/ppermute | solution.py:272
  15.8 1.6 %collective-permute-start.7 = (bf16[144,1024]{1,0:T(8,128)(2,1)S(1)}, bf16[144,1024]{1,0:T(8,128)(2,1)}, u32[]{:S(2)}, u32[]{:S(2)}) collective-permute-start(bf16[144,1024]{1,0:T(8,128)(2,1)S(1)} %collective-permute-done.1.a_2_), channel_id=1, source_target_pairs={{24,0},{28,4},{0,8},{4,12},{8,16},{12,20},{16,24},{20,28},{25,1},{... | collective-permute-start | bytes 884744 | tf_op jit(solution)/shard_map/tok_z2/ppermute | solution.py:272
  19.4 2.2 %collective-permute-done.4.a_2_ = bf16[144,1024]{1,0:T(8,128)(2,1)S(1)} collective-permute-done((bf16[144,1024]{1,0:T(8,128)(2,1)S(1)}, bf16[144,1024]{1,0:T(8,128)(2,1)S(1)}, u32[]{:S(2)}, u32[]{:S(2)}) %collective-permute-start.4) | collective-permute-done | bytes 294944 | tf_op jit(solution)/shard_map/tok_z1/ppermute | solution.py:272
  21.6 1.6 %collective-permute-start.5 = (bf16[64,1024]{1,0:T(8,128)(2,1)S(1)}, bf16[64,1024]{1,0:T(8,128)(2,1)S(1)}, u32[]{:S(2)}, u32[]{:S(2)}) collective-permute-start(bf16[64,1024]{1,0:T(8,128)(2,1)S(1)} %slice.18), channel_id=1, source_target_pairs={{0,4},{4,0},{8,12},{12,8},{16,20},{20,16},{24,28},{28,24},{1,5},{5... | collective-permute-start | bytes 393224 | tf_op jit(solution)/shard_map/tok_dx0/ppermute | solution.py:267
  24.6 3.2 %collective-permute-done.5.a_5_ = bf16[64,1024]{1,0:T(8,128)(2,1)S(1)} collective-permute-done((bf16[64,1024]{1,0:T(8,128)(2,1)S(1)}, bf16[64,1024]{1,0:T(8,128)(2,1)S(1)}, u32[]{:S(2)}, u32[]{:S(2)}) %collective-permute-start.5) | collective-permute-done | bytes 131104 | tf_op jit(solution)/shard_map/tok_dx0/ppermute | solution.py:267
  34.5 8.7 %shard_map.96 = (bf16[2,192,384]{2,1,0:T(8,128)(2,1)S(1)}, f32[2,8,128]{2,1,0:T(8,128)S(1)}, bf16[2,384,4096]{2,1,0:T(8,128)(2,1)S(1)}, bf16[2,384,4096]{2,1,0:T(8,128)(2,1)S(1)}) custom-call(s32[2]{0:T(128)S(1)} %pad_add_fusion.a_0_, f32[1,128]{1,0:T(1,128)S(1)} %pad_bitcast_fusion.a_1_, bf16[144,1024]{1,0:T(8,128)(2,1)} %copy-done, ...), custom_call_target="tpu_custom_call" | custom-call | tf_op jit(solution)/shard_map/pallas_call | solution.py:158
  49.5 5.8 %shard_map.97 = (bf16[2,192,384]{2,1,0:T(8,128)(2,1)S(1)}, f32[2,8,128]{2,1,0:T(8,128)S(1)}) custom-call(s32[2]{0:T(128)S(1)} %pad_add_fusion.a_0_, f32[1,128]{1,0:T(1,128)S(1)} %pad_bitcast_fusion.a_1_, bf16[144,1024]{1,0:T(8,128)(2,1)} %copy-done.8, bf16[144,1024]{1,0:T(8,128)(2,1)} %copy-done.3, bf16[144,1024]{1,0:T(8,128)(2,1)} %copy-done.4, ...), custom_call_target="tpu_custom_call" | custom-call | tf_op jit(solution)/shard_map/pallas_call | solution.py:158
  55.3 1.9 %collective-permute-done.23.a_5_ = bf16[64,1024]{1,0:T(8,128)(2,1)S(1)} collective-permute-done((bf16[64,1024]{1,0:T(8,128)(2,1)S(1)}, bf16[64,1024]{1,0:T(8,128)(2,1)S(1)}, u32[]{:S(2)}, u32[]{:S(2)}) %collective-permute-start.23) | collective-permute-done | bytes 131104 | tf_op jit(solution)/shard_map/tok_dx2/ppermute | solution.py:267
  64.1 5.8 %shard_map.98 = (bf16[2,192,384]{2,1,0:T(8,128)(2,1)S(1)}, f32[2,8,128]{2,1,0:T(8,128)S(1)}) custom-call(s32[2]{0:T(128)S(1)} %pad_add_fusion.a_0_, f32[1,128]{1,0:T(1,128)S(1)} %pad_bitcast_fusion.a_1_, bf16[144,1024]{1,0:T(8,128)(2,1)} %collective-permute-done.7.a_2_, bf16[144,1024]{1,0:T(8,128)(2,1)} %copy-done.1, bf16[144,1024]{1,0:T(8,128)(2,1)} %copy-done.2, ...), custom_call_target="tpu_custom_call" | custom-call | tf_op jit(solution)/shard_map/pallas_call | solution.py:158
  74.1 2.7 %shard_map.100 = (bf16[2,192,1536]{2,1,0:T(8,128)(2,1)S(1)}, f32[128,1024]{1,0:T(8,128)S(1)}, bf16[128,1024]{1,0:T(8,128)(2,1)S(1)}) custom-call(s32[2]{0:T(128)S(1)} %pad_add_fusion.a_0_, f32[2,8,128]{2,1,0:T(8,128)S(1)} %get-tuple-element.149.a_1_.a_2_, bf16[2,192,384]{2,1,0:T(8,128)(2,1)S(1)} %get-tuple-element.150.a_2_, ...), custom_call_target="tpu_custom_call" | custom-call | tf_op jit(solution)/shard_map/pallas_call | solution.py:195
  76.9 5.8 %shard_map.99 = (bf16[2,192,384]{2,1,0:T(8,128)(2,1)S(1)}, f32[2,8,128]{2,1,0:T(8,128)S(1)}) custom-call(s32[2]{0:T(128)S(1)} %pad_add_fusion.a_0_, f32[1,128]{1,0:T(1,128)S(1)} %pad_bitcast_fusion.a_1_, bf16[144,1024]{1,0:T(8,128)(2,1)} %copy-done.7, bf16[144,1024]{1,0:T(8,128)(2,1)} %copy-done.10, bf16[144,1024]{1,0:T(8,128)(2,1)} %copy-done.11, ...), custom_call_target="tpu_custom_call" | custom-call | tf_op jit(solution)/shard_map/pallas_call | solution.py:158
  84.7 2.5 %shard_map.101 = (bf16[2,192,1536]{2,1,0:T(8,128)(2,1)S(1)}, f32[128,1024]{1,0:T(8,128)S(1)}, bf16[128,1024]{1,0:T(8,128)(2,1)S(1)}) custom-call(s32[2]{0:T(128)S(1)} %pad_add_fusion.a_0_, f32[2,8,128]{2,1,0:T(8,128)S(1)} %get-tuple-element.155.a_1_.a_3_, bf16[2,192,384]{2,1,0:T(8,128)(2,1)S(1)} %get-tuple-element.156.a_2_, ...), custom_call_target="tpu_custom_call" | custom-call | tf_op jit(solution)/shard_map/pallas_call | solution.py:195
  88.3 3.9 %collective-permute-done.47.a_4_ = bf16[2,192,384]{2,1,0:T(8,128)(2,1)S(1)} collective-permute-done((bf16[2,192,384]{2,1,0:T(8,128)(2,1)S(1)}, bf16[2,192,384]{2,1,0:T(8,128)(2,1)S(1)}, u32[]{:S(2)}, u32[]{:S(2)}) %collective-permute-start.47) | collective-permute-done | bytes 294944 | tf_op jit(solution)/shard_map/hid_y1/ppermute | solution.py:262
  93.9 1.7 %collective-permute-done.50 = bf16[128,1024]{1,0:T(8,128)(2,1)S(1)} collective-permute-done((bf16[128,1024]{1,0:T(8,128)(2,1)S(1)}, bf16[128,1024]{1,0:T(8,128)(2,1)S(1)}, u32[]{:S(2)}, u32[]{:S(2)}) %collective-permute-start.50) | collective-permute-done | bytes 262176 | tf_op jit(solution)/shard_map/sum_x2/ppermute | solution.py:267
  95.7 3.7 %collective-permute-start.51 = (bf16[128,1024]{1,0:T(8,128)(2,1)S(1)}, bf16[128,1024]{1,0:T(8,128)(2,1)S(1)}, u32[]{:S(2)}, u32[]{:S(2)}) collective-permute-start(bf16[128,1024]{1,0:T(8,128)(2,1)S(1)} %add_convert_fusion.3), channel_id=1, source_target_pairs={{24,0},{28,4},{0,8},{4,12},{8,16},{12,20},{16,24},{20,28},{25,1},{... | collective-permute-start | bytes 786440 | tf_op jit(solution)/shard_map/sum_z2/ppermute | solution.py:272
  99.4 2.4 %shard_map.103 = (bf16[2,192,1536]{2,1,0:T(8,128)(2,1)S(1)}, f32[128,1024]{1,0:T(8,128)S(1)}, bf16[128,1024]{1,0:T(8,128)(2,1)S(1)}) custom-call(s32[2]{0:T(128)S(1)} %pad_add_fusion.a_0_, f32[2,8,128]{2,1,0:T(8,128)S(1)} %get-tuple-element.161.a_1_.a_4_, bf16[2,192,384]{2,1,0:T(8,128)(2,1)S(1)} %get-tuple-element.162.a_2_, ...), custom_call_target="tpu_custom_call" | custom-call | tf_op jit(solution)/shard_map/pallas_call | solution.py:195
  103.5 2.8 %collective-permute-start.54 = (bf16[128,1024]{1,0:T(8,128)(2,1)S(1)}, bf16[128,1024]{1,0:T(8,128)(2,1)S(1)}, u32[]{:S(2)}, u32[]{:S(2)}) collective-permute-start(bf16[128,1024]{1,0:T(8,128)(2,1)S(1)} %add_convert_fusion.1), channel_id=1, source_target_pairs={{8,0},{12,4},{16,8},{20,12},{24,16},{28,20},{0,24},{4,28},{9,1},{1... | collective-permute-start | bytes 786440 | tf_op jit(solution)/shard_map/sum_z3/ppermute | solution.py:272
  106.3 2.9 %collective-permute-done.49 = bf16[128,1024]{1,0:T(8,128)(2,1)S(1)} collective-permute-done((bf16[128,1024]{1,0:T(8,128)(2,1)S(1)}, bf16[128,1024]{1,0:T(8,128)(2,1)S(1)}, u32[]{:S(2)}, u32[]{:S(2)}) %collective-permute-start.49) | collective-permute-done | bytes 262176 | tf_op jit(solution)/shard_map/sum_x1/ppermute | solution.py:267
  109.3 2.5 %shard_map.102 = (bf16[2,192,1536]{2,1,0:T(8,128)(2,1)S(1)}, f32[128,1024]{1,0:T(8,128)S(1)}, bf16[128,1024]{1,0:T(8,128)(2,1)S(1)}) custom-call(s32[2]{0:T(128)S(1)} %pad_add_fusion.a_0_, f32[2,8,128]{2,1,0:T(8,128)S(1)} %get-tuple-element.105.a_1_, bf16[2,192,384]{2,1,0:T(8,128)(2,1)S(1)} %get-tuple-element.159.a_2_, ...), custom_call_target="tpu_custom_call" | custom-call | tf_op jit(solution)/shard_map/pallas_call | solution.py:195
  111.9 1.6 %collective-permute-start.55 = (bf16[128,1024]{1,0:T(8,128)(2,1)S(1)}, bf16[128,1024]{1,0:T(8,128)(2,1)S(1)}, u32[]{:S(2)}, u32[]{:S(2)}) collective-permute-start(bf16[128,1024]{1,0:T(8,128)(2,1)S(1)} %add_convert_fusion.2), channel_id=1, source_target_pairs={{24,0},{28,4},{0,8},{4,12},{8,16},{12,20},{16,24},{20,28},{25,1},{... | collective-permute-start | bytes 786440 | tf_op jit(solution)/shard_map/sum_z1/ppermute | solution.py:272
  114.5 5.0 %shard_map.104 = f32[2,384,1536]{2,1,0:T(8,128)} custom-call(s32[2]{0:T(128)S(1)} %pad_add_fusion.a_0_, f32[2,8,128]{2,1,0:T(8,128)S(1)} %get-tuple-element.105.a_1_, f32[2,8,128]{2,1,0:T(8,128)S(1)} %get-tuple-element.149.a_1_.a_2_, f32[2,8,128]{2,1,0:T(8,128)S(1)} %get-tuple-element.155.a_1_.a_3_, f32[2,8,128]{2,1,0:T(8,128)S(1)} %get-tuple-element.161.a_1_.a_4_, ...), custom_call_target="tpu_custom_call" | custom-call | tf_op jit(solution)/shard_map/pallas_call | solution.py:235
  (149 shorter events, 41.1 us)
Async XLA Ops:
  2.3 9.1 %collective-permute-start = (bf16[144,1024]{1,0:T(8,128)(2,1)S(1)}, bf16[144,1024]{1,0:T(8,128)(2,1)S(1)}, u32[]{:S(2)}, u32[]{:S(2)}) collective-permute-start(bf16[144,1024]{1,0:T(8,128)(2,1)S(1)} %shard_map.95.a_2_), channel_id=1, source_target_pairs={{0,1},{1,0},{2,3},{3,2},{4,5},{5,4},{6,7},{7,6},{8,9},{9,8},{10,11... | collective-permute-start | bytes 884744 | tf_op jit(solution)/shard_map/tok_c00/ppermute | solution.py:257
  2.8 12.6 %collective-permute-start.1 = (bf16[144,1024]{1,0:T(8,128)(2,1)S(1)}, bf16[144,1024]{1,0:T(8,128)(2,1)S(1)}, u32[]{:S(2)}, u32[]{:S(2)}) collective-permute-start(bf16[144,1024]{1,0:T(8,128)(2,1)S(1)} %shard_map.95.a_2_), channel_id=1, source_target_pairs={{24,0},{28,4},{0,8},{4,12},{8,16},{12,20},{16,24},{20,28},{25,1},{... | collective-permute-start | bytes 884744 | tf_op jit(solution)/shard_map/tok_z3/ppermute | solution.py:272
  5.5 9.9 %collective-permute-start.2 = (bf16[144,1024]{1,0:T(8,128)(2,1)S(1)}, bf16[144,1024]{1,0:T(8,128)(2,1)S(1)}, u32[]{:S(2)}, u32[]{:S(2)}) collective-permute-start(bf16[144,1024]{1,0:T(8,128)(2,1)S(1)} %shard_map.95.a_2_), channel_id=1, source_target_pairs={{0,4},{4,0},{8,12},{12,8},{16,20},{20,16},{24,28},{28,24},{1,5},{5... | collective-permute-start | bytes 884744 | tf_op jit(solution)/shard_map/tok_x0/ppermute | solution.py:267
  8.5 13.2 %collective-permute-start.4 = (bf16[144,1024]{1,0:T(8,128)(2,1)S(1)}, bf16[144,1024]{1,0:T(8,128)(2,1)S(1)}, u32[]{:S(2)}, u32[]{:S(2)}) collective-permute-start(bf16[144,1024]{1,0:T(8,128)(2,1)S(1)} %shard_map.95.a_2_), channel_id=1, source_target_pairs={{8,0},{12,4},{16,8},{20,12},{24,16},{28,20},{0,24},{4,28},{9,1},{1... | collective-permute-start | bytes 884744 | tf_op jit(solution)/shard_map/tok_z1/ppermute | solution.py:272
  15.8 12.5 %collective-permute-start.7 = (bf16[144,1024]{1,0:T(8,128)(2,1)S(1)}, bf16[144,1024]{1,0:T(8,128)(2,1)}, u32[]{:S(2)}, u32[]{:S(2)}) collective-permute-start(bf16[144,1024]{1,0:T(8,128)(2,1)S(1)} %collective-permute-done.1.a_2_), channel_id=1, source_target_pairs={{24,0},{28,4},{0,8},{4,12},{8,16},{12,20},{16,24},{20,28},{25,1},{... | collective-permute-start | bytes 884744 | tf_op jit(solution)/shard_map/tok_z2/ppermute | solution.py:272
  17.3 11.0 %collective-permute-start.8 = (bf16[144,1024]{1,0:T(8,128)(2,1)S(1)}, bf16[144,1024]{1,0:T(8,128)(2,1)S(1)}, u32[]{:S(2)}, u32[]{:S(2)}) collective-permute-start(bf16[144,1024]{1,0:T(8,128)(2,1)S(1)} %collective-permute-done.1.a_2_), channel_id=1, source_target_pairs={{0,4},{4,0},{8,12},{12,8},{16,20},{20,16},{24,28},{28,24},{1,5},{5... | collective-permute-start | bytes 884744 | tf_op jit(solution)/shard_map/tok_x3/ppermute | solution.py:267
  17.9 10.5 %collective-permute-start.9 = (bf16[144,1024]{1,0:T(8,128)(2,1)S(1)}, bf16[144,1024]{1,0:T(8,128)(2,1)S(1)}, u32[]{:S(2)}, u32[]{:S(2)}) collective-permute-start(bf16[144,1024]{1,0:T(8,128)(2,1)S(1)} %collective-permute-done.1.a_2_), channel_id=1, source_target_pairs={{0,2},{1,3},{2,0},{3,1},{4,6},{5,7},{6,4},{7,5},{8,10},{9,11},{10,... | collective-permute-start | bytes 884744 | tf_op jit(solution)/shard_map/tok_y3/ppermute | solution.py:262
  29.0 14.2 %collective-permute-start.16 = (bf16[144,1024]{1,0:T(8,128)(2,1)}, bf16[144,1024]{1,0:T(8,128)(2,1)S(1)}, u32[]{:S(2)}, u32[]{:S(2)}) collective-permute-start(bf16[144,1024]{1,0:T(8,128)(2,1)} %collective-permute-done.7.a_2_), channel_id=1, source_target_pairs={{0,4},{4,0},{8,12},{12,8},{16,20},{20,16},{24,28},{28,24},{1,5},{5... | collective-permute-start | bytes 884744 | tf_op jit(solution)/shard_map/tok_x2/ppermute | solution.py:267
  30.2 13.0 %collective-permute-start.17 = (bf16[144,1024]{1,0:T(8,128)(2,1)}, bf16[144,1024]{1,0:T(8,128)(2,1)S(1)}, u32[]{:S(2)}, u32[]{:S(2)}) collective-permute-start(bf16[144,1024]{1,0:T(8,128)(2,1)} %collective-permute-done.7.a_2_), channel_id=1, source_target_pairs={{0,2},{1,3},{2,0},{3,1},{4,6},{5,7},{6,4},{7,5},{8,10},{9,11},{10,... | collective-permute-start | bytes 884744 | tf_op jit(solution)/shard_map/tok_y2/ppermute | solution.py:262
  33.1 10.1 %collective-permute-start.14 = (bf16[64,1024]{1,0:T(8,128)(2,1)}, bf16[64,1024]{1,0:T(8,128)(2,1)}, u32[]{:S(2)}, u32[]{:S(2)}) collective-permute-start(bf16[64,1024]{1,0:T(8,128)(2,1)} %slice.20), channel_id=1, source_target_pairs={{0,4},{4,0},{8,12},{12,8},{16,20},{20,16},{24,28},{28,24},{1,5},{5... | collective-permute-start | bytes 393224 | tf_op jit(solution)/shard_map/tok_dx3/ppermute | solution.py:267
  33.8 9.4 %collective-permute-start.15 = (bf16[64,1024]{1,0:T(8,128)(2,1)}, bf16[64,1024]{1,0:T(8,128)(2,1)}, u32[]{:S(2)}, u32[]{:S(2)}) collective-permute-start(bf16[64,1024]{1,0:T(8,128)(2,1)} %slice.21), channel_id=1, source_target_pairs={{0,2},{1,3},{2,0},{3,1},{4,6},{5,7},{6,4},{7,5},{8,10},{9,11},{10,... | collective-permute-start | bytes 393224 | tf_op jit(solution)/shard_map/tok_dy3/ppermute | solution.py:262
  45.3 12.8 %collective-permute-start.25 = (bf16[144,1024]{1,0:T(8,128)(2,1)S(1)}, bf16[144,1024]{1,0:T(8,128)(2,1)S(1)}, u32[]{:S(2)}, u32[]{:S(2)}) collective-permute-start(bf16[144,1024]{1,0:T(8,128)(2,1)S(1)} %collective-permute-done.4.a_2_), channel_id=1, source_target_pairs={{0,4},{4,0},{8,12},{12,8},{16,20},{20,16},{24,28},{28,24},{1,5},{5... | collective-permute-start | bytes 884744 | tf_op jit(solution)/shard_map/tok_x1/ppermute | solution.py:267
  46.6 11.6 %collective-permute-start.26 = (bf16[144,1024]{1,0:T(8,128)(2,1)S(1)}, bf16[144,1024]{1,0:T(8,128)(2,1)S(1)}, u32[]{:S(2)}, u32[]{:S(2)}) collective-permute-start(bf16[144,1024]{1,0:T(8,128)(2,1)S(1)} %collective-permute-done.4.a_2_), channel_id=1, source_target_pairs={{0,2},{1,3},{2,0},{3,1},{4,6},{5,7},{6,4},{7,5},{8,10},{9,11},{10,... | collective-permute-start | bytes 884744 | tf_op jit(solution)/shard_map/tok_y1/ppermute | solution.py:262
  48.1 9.0 %collective-permute-start.23 = (bf16[64,1024]{1,0:T(8,128)(2,1)S(1)}, bf16[64,1024]{1,0:T(8,128)(2,1)S(1)}, u32[]{:S(2)}, u32[]{:S(2)}) collective-permute-start(bf16[64,1024]{1,0:T(8,128)(2,1)S(1)} %slice.22), channel_id=1, source_target_pairs={{0,4},{4,0},{8,12},{12,8},{16,20},{20,16},{24,28},{28,24},{1,5},{5... | collective-permute-start | bytes 393224 | tf_op jit(solution)/shard_map/tok_dx2/ppermute | solution.py:267
  48.9 9.3 %collective-permute-start.24 = (bf16[64,1024]{1,0:T(8,128)(2,1)S(1)}, bf16[64,1024]{1,0:T(8,128)(2,1)S(1)}, u32[]{:S(2)}, u32[]{:S(2)}) collective-permute-start(bf16[64,1024]{1,0:T(8,128)(2,1)S(1)} %slice.23), channel_id=1, source_target_pairs={{0,2},{1,3},{2,0},{3,1},{4,6},{5,7},{6,4},{7,5},{8,10},{9,11},{10,... | collective-permute-start | bytes 393224 | tf_op jit(solution)/shard_map/tok_dy2/ppermute | solution.py:262
  60.9 9.0 %collective-permute-start.27 = (bf16[144,1024]{1,0:T(8,128)(2,1)S(1)}, bf16[144,1024]{1,0:T(8,128)(2,1)S(1)}, u32[]{:S(2)}, u32[]{:S(2)}) collective-permute-start(bf16[144,1024]{1,0:T(8,128)(2,1)S(1)} %collective-permute-done.4.a_2_), channel_id=1, source_target_pairs={{0,1},{1,0},{2,3},{3,2},{4,5},{5,4},{6,7},{7,6},{8,9},{9,8},{10,11... | collective-permute-start | bytes 884744 | tf_op jit(solution)/shard_map/tok_c01/ppermute | solution.py:257
  61.6 9.2 %collective-permute-start.35 = (bf16[2,192,384]{2,1,0:T(8,128)(2,1)S(1)}, bf16[2,192,384]{2,1,0:T(8,128)(2,1)S(1)}, u32[]{:S(2)}, u32[]{:S(2)}) collective-permute-start(bf16[2,192,384]{2,1,0:T(8,128)(2,1)S(1)} %get-tuple-element.150.a_2_), channel_id=1, source_target_pairs={{0,2},{1,3},{2,0},{3,1},{4,6},{5,7},{6,4},{7,5},{8,10},{9,11},{10,... | collective-permute-start | bytes 884744 | tf_op jit(solution)/shard_map/hid_y3/ppermute | solution.py:262
  72.6 10.0 %collective-permute-start.38 = (bf16[2,192,384]{2,1,0:T(8,128)(2,1)S(1)}, bf16[2,192,384]{2,1,0:T(8,128)(2,1)S(1)}, u32[]{:S(2)}, u32[]{:S(2)}) collective-permute-start(bf16[2,192,384]{2,1,0:T(8,128)(2,1)S(1)} %get-tuple-element.156.a_2_), channel_id=1, source_target_pairs={{0,2},{1,3},{2,0},{3,1},{4,6},{5,7},{6,4},{7,5},{8,10},{9,11},{10,... | collective-permute-start | bytes 884744 | tf_op jit(solution)/shard_map/hid_y2/ppermute | solution.py:262
  83.2 9.0 %collective-permute-start.47 = (bf16[2,192,384]{2,1,0:T(8,128)(2,1)S(1)}, bf16[2,192,384]{2,1,0:T(8,128)(2,1)S(1)}, u32[]{:S(2)}, u32[]{:S(2)}) collective-permute-start(bf16[2,192,384]{2,1,0:T(8,128)(2,1)S(1)} %get-tuple-element.162.a_2_), channel_id=1, source_target_pairs={{0,2},{1,3},{2,0},{3,1},{4,6},{5,7},{6,4},{7,5},{8,10},{9,11},{10,... | collective-permute-start | bytes 884744 | tf_op jit(solution)/shard_map/hid_y1/ppermute | solution.py:262
  88.3 11.1 %collective-permute-start.46 = (bf16[2,192,384]{2,1,0:T(8,128)(2,1)S(1)}, bf16[2,192,384]{2,1,0:T(8,128)(2,1)S(1)}, u32[]{:S(2)}, u32[]{:S(2)}) collective-permute-start(bf16[2,192,384]{2,1,0:T(8,128)(2,1)S(1)} %get-tuple-element.162.a_2_), channel_id=1, source_target_pairs={{0,1},{1,0},{2,3},{3,2},{4,5},{5,4},{6,7},{7,6},{8,9},{9,8},{10,11... | collective-permute-start | bytes 884744 | tf_op jit(solution)/shard_map/hid_c1/ppermute | solution.py:257
  92.2 10.7 %collective-permute-start.44 = (bf16[2,192,384]{2,1,0:T(8,128)(2,1)S(1)}, bf16[2,192,384]{2,1,0:T(8,128)(2,1)S(1)}, u32[]{:S(2)}, u32[]{:S(2)}) collective-permute-start(bf16[2,192,384]{2,1,0:T(8,128)(2,1)S(1)} %get-tuple-element.159.a_2_), channel_id=1, source_target_pairs={{0,2},{1,3},{2,0},{3,1},{4,6},{5,7},{6,4},{7,5},{8,10},{9,11},{10,... | collective-permute-start | bytes 884744 | tf_op jit(solution)/shard_map/hid_y0/ppermute | solution.py:262
  92.9 10.6 %collective-permute-start.53 = (bf16[128,1024]{1,0:T(8,128)(2,1)S(1)}, bf16[128,1024]{1,0:T(8,128)(2,1)S(1)}, u32[]{:S(2)}, u32[]{:S(2)}) collective-permute-start(bf16[128,1024]{1,0:T(8,128)(2,1)S(1)} %get-tuple-element.170), channel_id=1, source_target_pairs={{0,4},{4,0},{8,12},{12,8},{16,20},{20,16},{24,28},{28,24},{1,5},{5... | collective-permute-start | bytes 786440 | tf_op jit(solution)/shard_map/sum_x3/ppermute | solution.py:267
  95.7 10.6 %collective-permute-start.51 = (bf16[128,1024]{1,0:T(8,128)(2,1)S(1)}, bf16[128,1024]{1,0:T(8,128)(2,1)S(1)}, u32[]{:S(2)}, u32[]{:S(2)}) collective-permute-start(bf16[128,1024]{1,0:T(8,128)(2,1)S(1)} %add_convert_fusion.3), channel_id=1, source_target_pairs={{24,0},{28,4},{0,8},{4,12},{8,16},{12,20},{16,24},{20,28},{25,1},{... | collective-permute-start | bytes 786440 | tf_op jit(solution)/shard_map/sum_z2/ppermute | solution.py:272
  103.5 16.0 %collective-permute-start.54 = (bf16[128,1024]{1,0:T(8,128)(2,1)S(1)}, bf16[128,1024]{1,0:T(8,128)(2,1)S(1)}, u32[]{:S(2)}, u32[]{:S(2)}) collective-permute-start(bf16[128,1024]{1,0:T(8,128)(2,1)S(1)} %add_convert_fusion.1), channel_id=1, source_target_pairs={{8,0},{12,4},{16,8},{20,12},{24,16},{28,20},{0,24},{4,28},{9,1},{1... | collective-permute-start | bytes 786440 | tf_op jit(solution)/shard_map/sum_z3/ppermute | solution.py:272
  (51 other events, 434.6 us)
